TPU v7x, 32 devices: a whole 2x2x4 slice. The times are simulated.
32 devices in a mesh: groups: 2 (over y), row: 8 (over z, x), col: 2 (over core).
Axes of the slice: x: 2, y: 2, z: 4, core: 2. Of those that a mesh axis runs over, the one named last changes fastest.
Arguments:
- sigma_anc: bfloat16 [16384, 8192], P(('groups', 'row'), 'col'), parts along dimension 0, as said below
- panel: bfloat16 [16384, 3072], P(('groups', 'row'), 'col'), parts along dimension 0
- holder: int32 [128], P('groups'), parts along dimension 0, may hold values from 0 to 63, each once
- dinv_diag: float32 [6144], P(('groups', 'col')), parts along dimension 0, may hold values from 0.5 to 2
Outputs:
- sigma_aj: bfloat16 [16384, 3072], P(('groups', 'row'), 'col'), parts along dimension 0
- variances: float32 [6144], P(('groups', 'col')), parts along dimension 0
There are 2 independent parts, one for each index of `groups`. A program takes and returns all parts, laid end to end along the dimension named above; each array names one. Nothing has to cross between parts.
Inputs may be any that keep to these rules, and one draw needn't show every extreme that they name: holder is a permutation of the 64 tiles. sigma_anc is symmetric and positive definite.
All inputs are finite; a program needn't handle non-finite values.
Results may differ from a plain program's by a relative error of at most 0.001.
Values may be sent and summed in bfloat16 or wider, within the bound.
No kernel may reach another device: no remote copies, remote signals or barrier semaphores. Data moves between devices by JAX's collectives and lax.ppermute only.
A program may use at most 128 MiB of HBM per device.

v0:
```python
import jax
import jax.numpy as jnp
from jax import lax
from jax.sharding import PartitionSpec as P

TILE = 128


def body(sigma_anc, panel, holder, dinv_diag):
    whole_rows = lax.all_gather(sigma_anc, "col", axis=1, tiled=True)
    local_rows = whole_rows.shape[0]
    width = whole_rows.shape[1]
    n_tiles = width // TILE
    per_dev = local_rows // TILE
    cols = panel.shape[1]
    position = lax.axis_index("row")
    my_tiles = lax.dynamic_slice_in_dim(holder, position * per_dev, per_dev)
    piece = lax.all_gather(panel, "row", axis=0, tiled=True)
    count = piece.shape[0]
    count_tiles = count // TILE
    ids = jnp.arange(count_tiles, dtype=jnp.int32)
    select = (holder[:, None] == ids[None, :]).astype(jnp.bfloat16)
    blocks = whole_rows.reshape(local_rows, n_tiles, TILE)
    picked = jnp.einsum("rtk,ts->rsk", blocks, select, preferred_element_type=jnp.float32)
    total = jnp.dot(
        picked.astype(jnp.bfloat16).reshape(local_rows, count),
        piece,
        preferred_element_type=jnp.float32,
    )
    count_tiles = count // TILE
    ids = jnp.arange(count_tiles, dtype=jnp.int32)
    select = (my_tiles[:, None] == ids[None, :]).astype(jnp.bfloat16)
    mine = jnp.einsum(
        "ji,irc->jrc",
        select,
        piece.reshape(count_tiles, TILE, cols),
        preferred_element_type=jnp.float32,
    )
    prod, mine = (total, mine)
    sigma_aj = (-prod).astype(jnp.bfloat16)
    partial_sums = jnp.sum(mine.reshape(local_rows, cols) * prod, axis=0)
    variances = dinv_diag + lax.psum(partial_sums, "row")
    return (sigma_aj, variances)


def solution(mesh):
    placed = (
        P(("groups", "row"), "col"),
        P(("groups", "row"), "col"),
        P("groups"),
        P(("groups", "col")),
    )
    return jax.shard_map(
        body,
        mesh=mesh,
        in_specs=placed,
        out_specs=(P(("groups", "row"), "col"), P(("groups", "col"))),
        check_vma=False,
    )
```

profile of v0, /device:TPU:0, one launch (start us, length us, event | category | flops | bytes accessed | tf_op | source)
XLA Modules:
  0.0 658.9 jit_solution(1104403360409697012)
XLA Ops:
  7.2 0.0 all-gather.3.cloned.1.call-start
  7.2 0.7 all-gather.3.cloned.1.call-update
  7.9 0.0 all-gather.5.cloned.1.call-start
  7.9 0.7 all-gather.5.cloned.1.call-update
  8.7 0.7 dynamic_slice.3
  9.4 33.0 %all-gather.3.cloned.1.call-done = bf16[1024,8192]{1,0:T(8,128)(2,1)} async-done(((bf16[1024,4096]{1,0:T(8,128)(2,1)}), bf16[1024,8192]{1,0:T(8,128)(2,1)}) %all-gather.3.cloned.1.call-update) | async-done | bytes 16777232 | tf_op jit(solution)/shard_map/all_gather | solution.py:10
  42.4 0.0 copy-start.1
  42.4 15.3 %copy.9 = bf16[128,8,64,128]{3,2,1,0:T(8,128)(2,1)} copy(bf16[128,8,64,128]{3,1,2,0:T(8,128)(2,1)} %bitcast.25) | data formatting | bytes 33554432
  57.6 0.0 copy-done.1
  57.6 11.5 %convolution_convert_fusion = bf16[64,1024,128]{2,0,1:T(8,128)(2,1)} fusion(bf16[1024,64,128]{2,1,0:T(8,128)(2,1)} %bitcast.22, s32[64]{0:T(128)S(1)} %copy-done.1), kind=kOutput, calls=%fused_computation.5 | convolution fusion | flops 1082134528 | bytes 33554688 | tf_op jit(solution)/shard_map/rtk,ts->rsk/dot_general | solution.py:24
  69.1 456.4 %all-gather.5.cloned.1.call-done = bf16[8192,1536]{1,0:T(8,128)(2,1)} async-done(((bf16[1024,1536]{1,0:T(8,128)(2,1)}), bf16[8192,1536]{1,0:T(8,128)(2,1)}) %all-gather.5.cloned.1.call-update) | async-done | bytes 25165840 | tf_op jit(solution)/shard_map/all_gather | solution.py:18
  525.5 38.6 %fusion = f32[8,128,1536]{2,0,1:T(8,128)S(1)} fusion(bf16[64,128,1536]{2,1,0:T(8,128)(2,1)} %bitcast.24, s32[8]{0:T(128)S(1)} %dynamic_slice.3), kind=kOutput, calls=%fused_computation | convolution fusion | flops 201327104 | bytes 31457312 | tf_op jit(solution)/shard_map/ji,irc->jrc/dot_general | solution.py:33
  564.1 3.6 copy.8
  567.8 0.0 copy-start
  567.8 63.2 %fusion.5 = (f32[1536]{0:T(1024)S(1)}, bf16[1024,1536]{1,0:T(8,128)(2,1)}) fusion(f32[8,128,1536]{2,1,0:T(8,128)S(1)} %copy.8, bf16[8192,1536]{1,0:T(8,128)(2,1)} %all-gather.5.cloned.1.call-done, bf16[128,8,64,128]{3,2,1,0:T(8,128)(2,1)} %bitcast.23), kind=kOutput, calls=%fused_computation.7 | convolution fusion | flops 25776093184 | bytes 51386368 | tf_op jit(solution)/shard_map/dot_general | solution.py:25
  631.0 20.4 %psum.7 = f32[1536]{0:T(1024)S(1)} all-reduce(f32[1536]{0:T(1024)S(1)} %get-tuple-element.2), channel_id=1, replica_groups=mesh['groups'=2,'row'=8,'col'=2] {'row'}, use_global_device_ids=true, to_apply=%region_1.0 | all-reduce | flops 1536 | bytes 12288 | tf_op jit(solution)/shard_map/psum | solution.py:42
  651.4 0.0 copy-done
  651.4 0.6 add.9
Async XLA Ops:
  7.2 35.2 %all-gather.3.cloned.1.call-start = ((), (), s32[]{:S(2)}) async-start(), calls=%async_computation | async-start | bytes 25165824 | tf_op jit(solution)/shard_map/all_gather | solution.py:10
  7.9 517.6 %all-gather.5.cloned.1.call-start = ((), (), s32[]{:S(2)}) async-start(), calls=%async_computation.1 | async-start | bytes 28311552 | tf_op jit(solution)/shard_map/all_gather | solution.py:18
  42.4 15.3 %copy-start.1 = (s32[64]{0:T(128)S(1)}, s32[64]{0:T(128)}, u32[]{:S(2)}) copy-start(s32[64]{0:T(128)} %param.6) | copy-start | bytes 772
  567.8 83.6 %copy-start = (f32[1536]{0:T(1024)S(1)}, f32[1536]{0:T(1024)}, u32[]{:S(2)}) copy-start(f32[1536]{0:T(1024)} %param.7) | copy-start | bytes 18436
Sparse Core Ops, SparseCore 0:
  9.6 32.7 all-gather.2
  43.9 481.5 all-gather.4
where the time goes:
time: 659 us
  waiting for transfers between devices  491 us (75%)
  matrix products  113 us (17%)
  blocking collectives  20.4 us (3%)
  local copies, waits for them, and re-layouts  19.6 us (3%)
  between operations  14.1 us (2%)
    all_gather x1, waiting for transfers between devices, body(): piece = lax.all_gather(panel, 'row', axis=0, tiled=True)  456 us
    dot_general x1, matrix products, body(): jnp.dot(picked.astype(jnp.bfloat16).reshape(local_rows, count), piece, pr...  63.2 us
    dot_general x1, matrix products, body(): jnp.einsum('ji,irc->jrc', select, piece.reshape(count_tiles, TILE, cols),...  38.6 us
    all_gather x1, waiting for transfers between devices, body(): whole_rows = lax.all_gather(sigma_anc, 'col', axis=1, tiled=True)  33 us
    psum x1, blocking collectives, body(): variances = dinv_diag + lax.psum(partial_sums, 'row')  20.4 us
    unnamed x5, local copies, waits for them, and re-layouts  15.3 us
  transfers between devices with their start and end apart: 2, of which 2 were waited for; matrix products, arithmetic and copies ran while one was open for 4% of the time, Pallas kernels for 0%

commit v1 on v0

v1 whole, which is shorter than its diff:
```python
import functools

import jax
import jax.numpy as jnp
from jax import lax
from jax.experimental import pallas as pl
from jax.experimental.pallas import tpu as pltpu
from jax.sharding import PartitionSpec as P

TILE = 128
F32 = jnp.float32
VMEM_LIMIT = 56 * 1024 * 1024


def reorder_kernel(slots, a, o):
    o[...] = a[...]


def reorder(whole, logical):
    rows, width = whole.shape
    return pl.pallas_call(
        reorder_kernel,
        grid_spec=pltpu.PrefetchScalarGridSpec(
            num_scalar_prefetch=1,
            grid=(width // TILE,),
            in_specs=[pl.BlockSpec((rows, TILE), lambda k, t: (0, t[k]))],
            out_specs=pl.BlockSpec((rows, TILE), lambda k, t: (0, k)),
        ),
        out_shape=jax.ShapeDtypeStruct((rows, width), whole.dtype),
        cost_estimate=pl.CostEstimate(flops=0, bytes_accessed=4 * rows * width, transcendentals=0),
    )(logical, whole)


def pick_kernel(count, here, at, *refs):
    j = pl.program_id(0)
    pieces, base, out = refs[:count], refs[count], refs[count + 1]
    value = base[...]
    for p in range(count):
        value = jnp.where(here[p, j] != 0, pieces[p][...], value)
    out[...] = value


def pick(pieces, sources, wanted, base):
    rows, cols = base.shape
    per = rows // TILE
    rel = jnp.stack([wanted - s * per for s in sources])
    here = ((rel >= 0) & (rel < per)).astype(jnp.int32)
    at = jnp.clip(rel, 0, per - 1)
    count = len(pieces)
    specs = [
        pl.BlockSpec((TILE, cols), functools.partial(lambda p, j, h, a: (a[p, j], 0), p))
        for p in range(count)
    ]
    tile = pl.BlockSpec((TILE, cols), lambda j, h, a: (j, 0))
    return pl.pallas_call(
        functools.partial(pick_kernel, count),
        grid_spec=pltpu.PrefetchScalarGridSpec(
            num_scalar_prefetch=2,
            grid=(per,),
            in_specs=specs + [tile],
            out_specs=tile,
        ),
        out_shape=jax.ShapeDtypeStruct((rows, cols), base.dtype),
        cost_estimate=pl.CostEstimate(
            flops=0, bytes_accessed=2 * (count + 2) * rows * cols, transcendentals=0
        ),
    )(here, at, *pieces, base)


def finish_kernel(tiles, here, at, acc, coeff, left, right, mine, out, part):
    i = pl.program_id(0)

    @pl.when(i == 0)
    def _():
        part[...] = jnp.zeros_like(part)

    half = left.shape[1]
    for late, lo in ((left, 0), (right, half)):
        span = pl.ds(lo, half)
        prod = acc[:, span] + jnp.dot(coeff[...], late[...], preferred_element_type=F32)
        out[:, span] = (-prod).astype(out.dtype)
        for t in range(tiles):
            j = i * tiles + t
            row = pl.multiple_of(at[j] * TILE, TILE)
            tile = jnp.where(
                here[j] != 0,
                late[pl.ds(row, TILE), :],
                mine[t * TILE : (t + 1) * TILE, span],
            )
            piece = tile.astype(F32) * prod[t * TILE : (t + 1) * TILE]
            part[:, span] += jnp.sum(piece, axis=0, keepdims=True)


def finish(acc, coeff, left, right, mine, source, wanted):
    rows, cols = acc.shape
    per = rows // TILE
    tiles = 2 if per % 2 == 0 else 1
    block = tiles * TILE
    rel = wanted - source * per
    here = ((rel >= 0) & (rel < per)).astype(jnp.int32)
    at = jnp.clip(rel, 0, per - 1)
    whole = lambda a: pl.BlockSpec(a.shape, lambda i, h, a: (0, 0))
    stripe = lambda a: pl.BlockSpec((block, a.shape[1]), lambda i, h, a: (i, 0))
    return pl.pallas_call(
        functools.partial(finish_kernel, tiles),
        grid_spec=pltpu.PrefetchScalarGridSpec(
            num_scalar_prefetch=2,
            grid=(per // tiles,),
            in_specs=[stripe(acc), stripe(coeff), whole(left), whole(right), stripe(mine)],
            out_specs=[stripe(acc), pl.BlockSpec((1, cols), lambda i, h, a: (0, 0))],
        ),
        out_shape=[
            jax.ShapeDtypeStruct((rows, cols), jnp.bfloat16),
            jax.ShapeDtypeStruct((1, cols), F32),
        ],
        compiler_params=pltpu.CompilerParams(vmem_limit_bytes=VMEM_LIMIT),
        cost_estimate=pl.CostEstimate(
            flops=2 * rows * cols * coeff.shape[1],
            bytes_accessed=8 * rows * cols + 4 * rows * coeff.shape[1],
            transcendentals=0,
        ),
    )(here, at, acc, coeff, left, right, mine)


def row_sum(value, n):
    step = 1
    if n & (n - 1):
        return lax.psum(value, "row")
    while step < n:
        value = value + lax.ppermute(value, "row", [(i, i ^ step) for i in range(n)])
        step *= 2
    return value


def body(sigma_anc, panel, holder, dinv_diag):
    n = lax.axis_size("row")
    me = lax.axis_index("row")
    rows, cols = panel.shape
    per = rows // TILE
    half = cols // 2
    order = list(range(0, n, 2)) + list(range(1, n, 2))[::-1]
    table = jnp.array(order, jnp.int32)
    place = jnp.array([order.index(i) for i in range(n)], jnp.int32)[me]
    fwd = [(order[i], order[(i + 1) % n]) for i in range(n)]
    bwd = [(b, a) for a, b in fwd]
    logical = jnp.argsort(holder).astype(jnp.int32)
    wanted = lax.dynamic_slice_in_dim(holder, me * per, per)

    whole = lax.all_gather(sigma_anc, "col", axis=1, tiled=True)
    sigma = reorder(whole, logical)

    def coeff(source):
        return lax.dynamic_slice_in_dim(sigma, source * rows, rows, axis=1)

    def term(source, piece):
        return jnp.dot(coeff(source), piece, preferred_element_type=F32)

    acc = term(me, panel)
    mine = pick([panel], [me], wanted, panel)
    a = b = panel
    for hop in range(1, n // 2):
        a, b = lax.ppermute(a, "row", fwd), lax.ppermute(b, "row", bwd)
        sources = [table[(place - hop) % n], table[(place + hop) % n]]
        acc = acc + term(sources[0], a)
        acc = acc + term(sources[1], b)
        mine = pick([a, b], sources, wanted, mine)
    left = lax.ppermute(a[:, :half], "row", fwd)
    right = lax.ppermute(b[:, half:], "row", bwd)
    source = table[(place + n // 2) % n]
    sigma_aj, part = finish(acc, coeff(source), left, right, mine, source, wanted)
    variances = dinv_diag + row_sum(part, n).reshape(cols)
    return sigma_aj, variances


def solution(mesh):
    placed = (
        P(("groups", "row"), "col"),
        P(("groups", "row"), "col"),
        P("groups"),
        P(("groups", "col")),
    )
    return jax.shard_map(
        body,
        mesh=mesh,
        in_specs=placed,
        out_specs=(P(("groups", "row"), "col"), P(("groups", "col"))),
        check_vma=False,
    )
```

time: 659 us -> 365 us (0.55)
  waiting for transfers between devices: 491 us -> 164 us
  Pallas kernels: 0 us -> 78.6 us
  matrix products: 113 us -> 56.7 us
  blocking collectives: 20.4 us -> 0 us
  starting transfers between devices: 0.08 us -> 14.9 us
  between operations: 14.1 us -> 27.6 us
  other arithmetic: 0.6 us -> 8.57 us
  local copies, waits for them, and re-layouts: 19.6 us -> 12.1 us
    all_gather x2 -> x1, waiting for transfers between devices: 489 us -> 0.01 us  [body(): whole = lax.all_gather(sigma_anc, 'col', axis=1, tiled=True)]
    ppermute x0 -> x11, waiting for transfers between devices: none -> 164 us  [the longest x6 157 us: body(): a, b = (lax.ppermute(a, 'row', fwd), lax.ppermute(b, 'row', bwd))]
    pallas_call x0 -> x6, Pallas kernels: none -> 78.6 us  [the longest x1 38.5 us: reorder(): pl.pallas_call(reorder_kernel, grid_spec=pltpu.PrefetchScalarGridSpec(num...]
    dot_general x3 -> x7, matrix products: 113 us -> 56.7 us  [term(): return jnp.dot(coeff(source), piece, preferred_element_type=F32)]
    psum x1 -> x0, blocking collectives: 20.4 us -> none  [body(): variances = dinv_diag + lax.psum(partial_sums, 'row')]
    ppermute x0 -> x11, starting transfers between devices: none -> 14.9 us  [the longest x6 7.13 us: body(): a, b = (lax.ppermute(a, 'row', fwd), lax.ppermute(b, 'row', bwd))]
    unnamed x5 -> x26, local copies, waits for them, and re-layouts: 15.3 us -> 3.58 us
  transfers between devices with their start and end apart: 2 -> 12, of which waited for: 2 -> 6; matrix products, arithmetic and copies ran while one was open for 4% -> 20% of each run, Pallas kernels for 0% -> 19%
where the time goes in v1:
time: 365 us; the launch traced here: 363 us
  waiting for transfers between devices  164 us (45%)
  Pallas kernels  78.6 us (22%)
  matrix products  56.7 us (16%)
  between operations  27.6 us (8%)
  starting transfers between devices  14.9 us (4%)
  local copies, waits for them, and re-layouts  12.1 us (3%)
  other arithmetic  8.57 us (2%)
    ppermute x6, waiting for transfers between devices, body(): a, b = (lax.ppermute(a, 'row', fwd), lax.ppermute(b, 'row', bwd))  157 us
    dot_general x7, matrix products, term(): return jnp.dot(coeff(source), piece, preferred_element_type=F32)  56.7 us
    pallas_call x1, Pallas kernels, reorder(): pl.pallas_call(reorder_kernel, grid_spec=pltpu.PrefetchScalarGridSpec(num...  38.5 us
    pallas_call x4, Pallas kernels, pick(): pl.pallas_call(functools.partial(pick_kernel, count), grid_spec=pltpu.Pre...  30 us
    pallas_call x1, Pallas kernels, finish(): pl.pallas_call(functools.partial(finish_kernel, tiles), grid_spec=pltpu.P...  10.1 us
  transfers between devices with their start and end apart: 12, of which 6 were waited for; matrix products, arithmetic and copies ran while one was open for 20% of the time, Pallas kernels for 19%

profile of v1, /device:TPU:0, one launch (start us, length us, event | category | flops | bytes accessed | tf_op | source)
XLA Modules:
  0.0 362.9 jit_solution(16434404819237152172)
XLA Ops:
  9.1 3.0 collective-permute-start
  12.1 68.0 %collective-permute-done.refs_0_ = bf16[1024,1536]{1,0:T(8,128)(2,1)S(1)} collective-permute-done((bf16[1024,1536]{1,0:T(8,128)(2,1)S(1)}, bf16[1024,1536]{1,0:T(8,128)(2,1)S(1)}, u32[]{:S(2)}, u32[]{:S(2)}) %collective-permute-start) | collective-permute-done | bytes 3145760 | tf_op jit(solution)/shard_map/ppermute | solution.py:162
  80.1 1.8 collective-permute-start.2
  82.2 67.4 %collective-permute-done.2.refs_0_ = bf16[1024,1536]{1,0:T(8,128)(2,1)} collective-permute-done((bf16[1024,1536]{1,0:T(8,128)(2,1)S(1)}, bf16[1024,1536]{1,0:T(8,128)(2,1)}, u32[]{:S(2)}, u32[]{:S(2)}) %collective-permute-start.2) | collective-permute-done | bytes 3145760 | tf_op jit(solution)/shard_map/ppermute | solution.py:162
  166.4 2.0 sort.17
  169.7 7.2 %shard_map.78.refs_2_ = bf16[1024,1536]{1,0:T(8,128)(2,1)} custom-call(s32[1,8]{1,0:T(1,128)} %get-tuple-element.10.here, s32[1,8]{1,0:T(1,128)} %get-tuple-element.8.at, bf16[1024,1536]{1,0:T(8,128)(2,1)} %refs_1_.1, bf16[1024,1536]{1,0:T(8,128)(2,1)} %refs_1_.1), custom_call_target="tpu_custom_call" | custom-call | bytes 9437184 | tf_op jit(solution)/shard_map/pallas_call | solution.py:55
  180.8 7.7 %shard_map.79.refs_2_ = bf16[1024,1536]{1,0:T(8,128)(2,1)} custom-call(s32[2,8]{1,0:T(2,128)} %and_convert_fusion.1.here, s32[2,8]{1,0:T(2,128)} %broadcast_clamp_fusion.at, bf16[1024,1536]{1,0:T(8,128)(2,1)} %copy-done.7, bf16[1024,1536]{1,0:T(8,128)(2,1)} %copy-done.5, bf16[1024,1536]{1,0:T(8,128)(2,1)} %shard_map.78.refs_2_), custom_call_target="tpu_custom_call" | custom-call | bytes 12582912 | tf_op jit(solution)/shard_map/pallas_call | solution.py:55
  188.5 7.6 %shard_map.80.refs_2_ = bf16[1024,1536]{1,0:T(8,128)(2,1)} custom-call(s32[2,8]{1,0:T(2,128)} %and_convert_fusion.2.here, s32[2,8]{1,0:T(2,128)} %broadcast_clamp_fusion.1.at, bf16[1024,1536]{1,0:T(8,128)(2,1)} %collective-permute-done.2.refs_0_, bf16[1024,1536]{1,0:T(8,128)(2,1)} %collective-permute-done.3.refs_1_, bf16[1024,1536]{1,0:T(8,128)(2,1)} %shard_map.79.refs_2_), custom_call_target="tpu_custom_call" | custom-call | bytes 12582912 | tf_op jit(solution)/shard_map/pallas_call | solution.py:55
  196.2 22.0 %collective-permute-done.4.refs_0_ = bf16[1024,1536]{1,0:T(8,128)(2,1)} collective-permute-done((bf16[1024,1536]{1,0:T(8,128)(2,1)}, bf16[1024,1536]{1,0:T(8,128)(2,1)}, u32[]{:S(2)}, u32[]{:S(2)}) %collective-permute-start.4) | collective-permute-done | bytes 3145760 | tf_op jit(solution)/shard_map/ppermute | solution.py:162
  218.2 2.7 slice.8
  224.2 7.5 %shard_map.81.mine = bf16[1024,1536]{1,0:T(8,128)(2,1)} custom-call(s32[2,8]{1,0:T(2,128)} %and_convert_fusion.3.here, s32[2,8]{1,0:T(2,128)} %broadcast_clamp_fusion.2.at, bf16[1024,1536]{1,0:T(8,128)(2,1)} %collective-permute-done.4.refs_0_, bf16[1024,1536]{1,0:T(8,128)(2,1)} %copy-done.1, bf16[1024,1536]{1,0:T(8,128)(2,1)} %shard_map.80.refs_2_), custom_call_target="tpu_custom_call" | custom-call | bytes 12582912 | tf_op jit(solution)/shard_map/pallas_call | solution.py:55
  231.7 38.5 %shard_map.77 = bf16[1024,8192]{1,0:T(8,128)(2,1)} custom-call(s32[64]{0:T(128)} %get-tuple-element.5.slots, bf16[1024,8192]{1,0:T(8,128)(2,1)} %all-gather.2.cloned.1.call-done.a), custom_call_target="tpu_custom_call" | custom-call | bytes 33554432 | tf_op jit(solution)/shard_map/pallas_call | solution.py:21
  270.2 3.3 constant_dynamic-slice_fusion.coeff
  273.5 7.2 %fusion.14 = f32[1024,1536]{1,0:T(8,128)} fusion(bf16[1024,1536]{1,0:T(8,128)(2,1)S(1)} %copy-done.4, bf16[1024,8192]{1,0:T(8,128)(2,1)} %shard_map.77, s32[]{:T(128)S(6)} %select_n.86), kind=kOutput, calls=%fused_computation.13 | convolution fusion | flops 3221225472 | bytes 11534340 | tf_op jit(solution)/shard_map/dot_general | solution.py:156
  283.0 5.3 %fusion.12 = f32[1024,1536]{1,0:T(8,128)} fusion(bf16[1024,1536]{1,0:T(8,128)(2,1)S(1)} %copy-done.8, bf16[1024,8192]{1,0:T(8,128)(2,1)S(1)} %copy-done, s32[]{:T(128)S(6)} %select_n.89), kind=kOutput, calls=%fused_computation.11 | convolution fusion | flops 3221225472 | bytes 11534340 | tf_op jit(solution)/shard_map/dot_general | solution.py:156
  288.3 7.2 %fusion.8 = f32[1024,1536]{1,0:T(8,128)} fusion(bf16[1024,1536]{1,0:T(8,128)(2,1)} %collective-permute-done.2.refs_0_, bf16[1024,8192]{1,0:T(8,128)(2,1)S(1)} %copy-done, s32[]{:T(128)S(6)} %select_n.95), kind=kOutput, calls=%fused_computation.7 | convolution fusion | flops 3221225472 | bytes 11534340 | tf_op jit(solution)/shard_map/dot_general | solution.py:156
  295.5 7.2 %fusion.4 = f32[1024,1536]{1,0:T(8,128)} fusion(bf16[1024,1536]{1,0:T(8,128)(2,1)} %collective-permute-done.4.refs_0_, bf16[1024,8192]{1,0:T(8,128)(2,1)S(1)} %copy-done, s32[]{:T(128)S(6)} %select_n.101), kind=kOutput, calls=%fused_computation.3 | convolution fusion | flops 3221225472 | bytes 11534340 | tf_op jit(solution)/shard_map/dot_general | solution.py:156
  302.7 7.3 %fusion.6 = f32[1024,1536]{1,0:T(8,128)} fusion(bf16[1024,1536]{1,0:T(8,128)(2,1)} %collective-permute-done.3.refs_1_, bf16[1024,8192]{1,0:T(8,128)(2,1)S(1)} %copy-done, s32[]{:T(128)S(6)} %select_n.98), kind=kOutput, calls=%fused_computation.5 | convolution fusion | flops 3221225472 | bytes 11534340 | tf_op jit(solution)/shard_map/dot_general | solution.py:156
  309.9 5.2 %fusion.10 = f32[1024,1536]{1,0:T(8,128)} fusion(bf16[1024,1536]{1,0:T(8,128)(2,1)S(1)} %copy-done.6, bf16[1024,8192]{1,0:T(8,128)(2,1)S(1)} %copy-done, s32[]{:T(128)S(6)} %select_n.92), kind=kOutput, calls=%fused_computation.9 | convolution fusion | flops 3221225472 | bytes 11534340 | tf_op jit(solution)/shard_map/dot_general | solution.py:156
  315.1 17.4 %add_add_fusion.acc = f32[1024,1536]{1,0:T(8,128)} fusion(f32[1024,1536]{1,0:T(8,128)} %fusion.4, f32[1024,1536]{1,0:T(8,128)} %fusion.6, f32[1024,1536]{1,0:T(8,128)} %fusion.8, f32[1024,1536]{1,0:T(8,128)} %fusion.10, f32[1024,1536]{1,0:T(8,128)} %fusion.14, f32[1024,1536]{1,0:T(8,128)} %fusion.12, bf16[1024,1536]{1,0:T(8,128)(2,1)S(1)} %copy-done.2, ...), kind=kOutput, calls=%fused_computation | convolution fusion | flops 3230662656 | bytes 49283076 | tf_op jit(solution)/shard_map/dot_general | solution.py:156
  332.5 10.1 %shard_map.82 = (bf16[1024,1536]{1,0:T(8,128)(2,1)}, f32[1,1536]{1,0:T(1,128)}) custom-call(s32[8]{0:T(128)} %get-tuple-element.11.here, s32[8]{0:T(128)} %get-tuple-element.18.at, f32[1024,1536]{1,0:T(8,128)} %add_add_fusion.acc, bf16[1024,1024]{1,0:T(8,128)(2,1)} %constant_dynamic-slice_fusion.coeff, bf16[1024,768]{1,0:T(8,128)(2,1)} %collective-permute-done.6.left, ...), custom_call_target="tpu_custom_call" | custom-call | flops 3221225472 | bytes 16777216 | tf_op jit(solution)/shard_map/pallas_call | solution.py:104
  343.8 2.7 collective-permute-done.8
  349.0 1.9 collective-permute-done.9
  350.9 2.9 collective-permute-start.10
  (60 shorter events, 22.4 us)
Async XLA Ops:
  7.2 144.4 %copy-start.12 = (s32[8]{0:T(128)S(1)}, s32[8]{0:T(128)}, u32[]{:S(2)}) copy-start(s32[8]{0:T(128)} %constant.99.clone) | copy-start | bytes 100
  7.2 149.7 %copy-start.9 = (s32[8]{0:T(128)S(1)}, s32[8]{0:T(128)}, u32[]{:S(2)}) copy-start(s32[8]{0:T(128)} %constant.98.clone) | copy-start | bytes 100
  7.2 159.2 %copy-start.11 = (s32[64]{0:T(128)S(1)}, s32[64]{0:T(128)}, u32[]{:S(2)}) copy-start(s32[64]{0:T(128)} %param.8) | copy-start | bytes 772
  7.2 224.5 %all-gather.2.cloned.1.call-start = ((), (), s32[]{:S(2)}) async-start(), calls=%async_computation | async-start | bytes 25165824 | tf_op jit(solution)/shard_map/all_gather | solution.py:149
  9.1 71.0 %collective-permute-start = (bf16[1024,1536]{1,0:T(8,128)(2,1)S(1)}, bf16[1024,1536]{1,0:T(8,128)(2,1)S(1)}, u32[]{:S(2)}, u32[]{:S(2)}) collective-permute-start(bf16[1024,1536]{1,0:T(8,128)(2,1)S(1)} %copy-done.3), channel_id=1, source_target_pairs={{0,4},{4,8},{8,12},{12,14},{14,10},{10,6},{6,2},{2,0},{1,5},{5,9},... | collective-permute-start | bytes 9437192 | tf_op jit(solution)/shard_map/ppermute | solution.py:162
  12.1 69.8 %collective-permute-start.1 = (bf16[1024,1536]{1,0:T(8,128)(2,1)S(1)}, bf16[1024,1536]{1,0:T(8,128)(2,1)S(1)}, u32[]{:S(2)}, u32[]{:S(2)}) collective-permute-start(bf16[1024,1536]{1,0:T(8,128)(2,1)S(1)} %copy-done.3), channel_id=1, source_target_pairs={{4,0},{8,4},{12,8},{14,12},{10,14},{6,10},{2,6},{0,2},{5,1},{9,5},... | collective-permute-start | bytes 9437192 | tf_op jit(solution)/shard_map/ppermute | solution.py:162
  80.1 70.9 %copy-start.7 = (bf16[1024,1536]{1,0:T(8,128)(2,1)}, bf16[1024,1536]{1,0:T(8,128)(2,1)S(1)}, u32[]{:S(2)}) copy-start(bf16[1024,1536]{1,0:T(8,128)(2,1)S(1)} %collective-permute-done.refs_0_) | copy-start | bytes 9437188
  80.1 69.4 %collective-permute-start.2 = (bf16[1024,1536]{1,0:T(8,128)(2,1)S(1)}, bf16[1024,1536]{1,0:T(8,128)(2,1)}, u32[]{:S(2)}, u32[]{:S(2)}) collective-permute-start(bf16[1024,1536]{1,0:T(8,128)(2,1)S(1)} %collective-permute-done.refs_0_), channel_id=1, source_target_pairs={{0,4},{4,8},{8,12},{12,14},{14,10},{10,6},{6,2},{2,0},{1,5},{5,9},... | collective-permute-start | bytes 9437192 | tf_op jit(solution)/shard_map/ppermute | solution.py:162
  82.0 69.1 %copy-start.5 = (bf16[1024,1536]{1,0:T(8,128)(2,1)}, bf16[1024,1536]{1,0:T(8,128)(2,1)S(1)}, u32[]{:S(2)}) copy-start(bf16[1024,1536]{1,0:T(8,128)(2,1)S(1)} %collective-permute-done.1.refs_1_) | copy-start | bytes 9437188
  82.0 69.1 %collective-permute-start.3 = (bf16[1024,1536]{1,0:T(8,128)(2,1)S(1)}, bf16[1024,1536]{1,0:T(8,128)(2,1)}, u32[]{:S(2)}, u32[]{:S(2)}) collective-permute-start(bf16[1024,1536]{1,0:T(8,128)(2,1)S(1)} %collective-permute-done.1.refs_1_), channel_id=1, source_target_pairs={{4,0},{8,4},{12,8},{14,12},{10,14},{6,10},{2,6},{0,2},{5,1},{9,5},... | collective-permute-start | bytes 9437192 | tf_op jit(solution)/shard_map/ppermute | solution.py:162
  149.5 68.7 %collective-permute-start.4 = (bf16[1024,1536]{1,0:T(8,128)(2,1)}, bf16[1024,1536]{1,0:T(8,128)(2,1)}, u32[]{:S(2)}, u32[]{:S(2)}) collective-permute-start(bf16[1024,1536]{1,0:T(8,128)(2,1)} %collective-permute-done.2.refs_0_), channel_id=1, source_target_pairs={{0,4},{4,8},{8,12},{12,14},{14,10},{10,6},{6,2},{2,0},{1,5},{5,9},... | collective-permute-start | bytes 9437192 | tf_op jit(solution)/shard_map/ppermute | solution.py:162
  151.0 71.0 %collective-permute-start.5 = (bf16[1024,1536]{1,0:T(8,128)(2,1)}, bf16[1024,1536]{1,0:T(8,128)(2,1)S(1)}, u32[]{:S(2)}, u32[]{:S(2)}) collective-permute-start(bf16[1024,1536]{1,0:T(8,128)(2,1)} %collective-permute-done.3.refs_1_), channel_id=1, source_target_pairs={{4,0},{8,4},{12,8},{14,12},{10,14},{6,10},{2,6},{0,2},{5,1},{9,5},... | collective-permute-start | bytes 9437192 | tf_op jit(solution)/shard_map/ppermute | solution.py:162
  220.9 111.7 %collective-permute-start.6 = (bf16[1024,768]{1,0:T(8,128)(2,1)}, bf16[1024,768]{1,0:T(8,128)(2,1)}, u32[]{:S(2)}, u32[]{:S(2)}) collective-permute-start(bf16[1024,768]{1,0:T(8,128)(2,1)} %slice.8), channel_id=1, source_target_pairs={{0,4},{4,8},{8,12},{12,14},{14,10},{10,6},{6,2},{2,0},{1,5},{5,9},... | collective-permute-start | bytes 4718600 | tf_op jit(solution)/shard_map/ppermute | solution.py:167
  222.1 2.2 copy-start.1
  223.4 109.1 %collective-permute-start.7 = (bf16[1024,768]{1,0:T(8,128)(2,1)}, bf16[1024,768]{1,0:T(8,128)(2,1)}, u32[]{:S(2)}, u32[]{:S(2)}) collective-permute-start(bf16[1024,768]{1,0:T(8,128)(2,1)} %slice.9), channel_id=1, source_target_pairs={{4,0},{8,4},{12,8},{14,12},{10,14},{6,10},{2,6},{0,2},{5,1},{9,5},... | collective-permute-start | bytes 4718600 | tf_op jit(solution)/shard_map/ppermute | solution.py:168
  270.2 3.3 copy-start.4
  273.5 8.7 %copy-start = (bf16[1024,8192]{1,0:T(8,128)(2,1)S(1)}, bf16[1024,8192]{1,0:T(8,128)(2,1)}, u32[]{:S(2)}) copy-start(bf16[1024,8192]{1,0:T(8,128)(2,1)} %shard_map.77) | copy-start | bytes 50331652
  273.5 9.6 %copy-start.8 = (bf16[1024,1536]{1,0:T(8,128)(2,1)S(1)}, bf16[1024,1536]{1,0:T(8,128)(2,1)}, u32[]{:S(2)}) copy-start(bf16[1024,1536]{1,0:T(8,128)(2,1)} %copy-done.7) | copy-start | bytes 9437188
  302.6 7.3 %copy-start.6 = (bf16[1024,1536]{1,0:T(8,128)(2,1)S(1)}, bf16[1024,1536]{1,0:T(8,128)(2,1)}, u32[]{:S(2)}) copy-start(bf16[1024,1536]{1,0:T(8,128)(2,1)} %copy-done.5) | copy-start | bytes 9437188
  309.9 5.2 %copy-start.2 = (bf16[1024,1536]{1,0:T(8,128)(2,1)S(1)}, bf16[1024,1536]{1,0:T(8,128)(2,1)}, u32[]{:S(2)}) copy-start(bf16[1024,1536]{1,0:T(8,128)(2,1)} %copy-done.1) | copy-start | bytes 9437188
  332.5 22.9 %copy-start.10 = (f32[1536]{0:T(1024)S(1)}, f32[1536]{0:T(1024)}, u32[]{:S(2)}) copy-start(f32[1536]{0:T(1024)} %param.9) | copy-start | bytes 18436
  342.7 3.8 %collective-permute-start.8 = (f32[1,1536]{1,0:T(1,128)}, f32[1,1536]{1,0:T(1,128)S(1)}, u32[]{:S(2)}, u32[]{:S(2)}) collective-permute-start(f32[1,1536]{1,0:T(1,128)} %get-tuple-element.7), channel_id=1, source_target_pairs={{0,2},{2,0},{4,6},{6,4},{8,10},{10,8},{12,14},{14,12},{1,3},{3,1},... | collective-permute-start | bytes 18440 | tf_op jit(solution)/shard_map/ppermute | solution.py:130
  347.2 3.6 %collective-permute-start.9 = (f32[1,1536]{1,0:T(1,128)S(1)}, f32[1,1536]{1,0:T(1,128)S(1)}, u32[]{:S(2)}, u32[]{:S(2)}) collective-permute-start(f32[1,1536]{1,0:T(1,128)S(1)} %add.171), channel_id=1, source_target_pairs={{0,4},{2,6},{4,0},{6,2},{8,12},{10,14},{12,8},{14,10},{1,5},{3,7},... | collective-permute-start | bytes 18440 | tf_op jit(solution)/shard_map/ppermute | solution.py:130
  350.9 4.6 %collective-permute-start.10 = (f32[1,1536]{1,0:T(1,128)S(1)}, f32[1,1536]{1,0:T(1,128)S(1)}, u32[]{:S(2)}, u32[]{:S(2)}) collective-permute-start(f32[1,1536]{1,0:T(1,128)S(1)} %add.172), channel_id=1, source_target_pairs={{0,8},{2,10},{4,12},{6,14},{8,0},{10,2},{12,4},{14,6},{1,9},{3,11}... | collective-permute-start | bytes 18440 | tf_op jit(solution)/shard_map/ppermute | solution.py:130
  (1 other events, 1.9 us)
Sparse Core Ops, SparseCore 0:
  9.6 32.7 all-gather.1

commit v2 on v1

--- a/solution.py
+++ b/solution.py
@@ -155,17 +155,32 @@
     def term(source, piece):
         return jnp.dot(coeff(source), piece, preferred_element_type=F32)
 
-    acc = term(me, panel)
     mine = pick([panel], [me], wanted, panel)
     a = b = panel
-    for hop in range(1, n // 2):
+    acc = None
+    ready, fresh = [(me, panel)], []
+    for hop in range(1, n // 2 + 1):
+        if hop == 2:
+            a, b, mine, sigma = lax.optimization_barrier((a, b, mine, sigma))
+        if hop > 2:
+            for source, piece in ready:
+                update = term(source, piece)
+                acc = update if acc is None else acc + update
+            mine = pick([p for _, p in ready], [s for s, _ in ready], wanted, mine)
+            a, b, acc, mine = lax.optimization_barrier((a, b, acc, mine))
+            ready = []
+        ready, fresh = ready + fresh, []
+        if hop == n // 2:
+            break
         a, b = lax.ppermute(a, "row", fwd), lax.ppermute(b, "row", bwd)
-        sources = [table[(place - hop) % n], table[(place + hop) % n]]
-        acc = acc + term(sources[0], a)
-        acc = acc + term(sources[1], b)
-        mine = pick([a, b], sources, wanted, mine)
+        fresh = [(table[(place - hop) % n], a), (table[(place + hop) % n], b)]
     left = lax.ppermute(a[:, :half], "row", fwd)
     right = lax.ppermute(b[:, half:], "row", bwd)
+    for source, piece in ready:
+        update = term(source, piece)
+        acc = update if acc is None else acc + update
+    mine = pick([p for _, p in ready], [s for s, _ in ready], wanted, mine)
+    left, right, acc, mine = lax.optimization_barrier((left, right, acc, mine))
     source = table[(place + n // 2) % n]
     sigma_aj, part = finish(acc, coeff(source), left, right, mine, source, wanted)
     variances = dinv_diag + row_sum(part, n).reshape(cols)

time: 365 us -> 296 us (0.81)
  waiting for transfers between devices: 164 us -> 104 us
  matrix products: 56.7 us -> 51.7 us
    ppermute x6, waiting for transfers between devices: 157 us -> 74.8 us  [body(): a, b = (lax.ppermute(a, 'row', fwd), lax.ppermute(b, 'row', bwd))]
    all_gather x1, waiting for transfers between devices: 0.01 us -> 9 us  [body(): whole = lax.all_gather(sigma_anc, 'col', axis=1, tiled=True)]
    ppermute x1, waiting for transfers between devices: 0.01 us -> 6.04 us  [body(): left = lax.ppermute(a[:, :half], 'row', fwd)]
    dot_general x7, matrix products: 56.7 us -> 51.7 us  [term(): return jnp.dot(coeff(source), piece, preferred_element_type=F32)]
    ppermute x1, waiting for transfers between devices: 0.01 us -> 4.91 us  [body(): right = lax.ppermute(b[:, half:], 'row', bwd)]
  transfers between devices with their start and end apart: 12 -> 12, of which waited for: 6 -> 11; matrix products, arithmetic and copies ran while one was open for 20% -> 22% of each run, Pallas kernels for 19% -> 24%
where the time goes in v2:
time: 296 us; the launch traced here: 294 us
  waiting for transfers between devices  104 us (35%)
  Pallas kernels  80.1 us (27%)
  matrix products  51.7 us (17%)
  between operations  27.8 us (9%)
  starting transfers between devices  13 us (4%)
  local copies, waits for them, and re-layouts  9.51 us (3%)
  other arithmetic  8 us (3%)
    ppermute x6, waiting for transfers between devices, body(): a, b = (lax.ppermute(a, 'row', fwd), lax.ppermute(b, 'row', bwd))  74.8 us
    dot_general x7, matrix products, term(): return jnp.dot(coeff(source), piece, preferred_element_type=F32)  51.7 us
    pallas_call x1, Pallas kernels, reorder(): pl.pallas_call(reorder_kernel, grid_spec=pltpu.PrefetchScalarGridSpec(num...  38.6 us
    pallas_call x4, Pallas kernels, pick(): pl.pallas_call(functools.partial(pick_kernel, count), grid_spec=pltpu.Pre...  31.4 us
    pallas_call x1, Pallas kernels, finish(): pl.pallas_call(functools.partial(finish_kernel, tiles), grid_spec=pltpu.P...  10.2 us
    all_gather x1, waiting for transfers between devices, body(): whole = lax.all_gather(sigma_anc, 'col', axis=1, tiled=True)  9 us
    ppermute x3, waiting for transfers between devices, row_sum(): lax.ppermute(value, 'row', [(i, i ^ step) for i in range(n)])  8.23 us
    ppermute x6, starting transfers between devices, body(): a, b = (lax.ppermute(a, 'row', fwd), lax.ppermute(b, 'row', bwd))  7.08 us
  transfers between devices with their start and end apart: 12, of which 11 were waited for; matrix products, arithmetic and copies ran while one was open for 22% of the time, Pallas kernels for 24%

profile of v2, /device:TPU:0, one launch (start us, length us, event | category | flops | bytes accessed | tf_op | source)
XLA Modules:
  0.0 293.7 jit_solution(17774250930104918117)
XLA Ops:
  9.1 3.0 %collective-permute-start = (bf16[1024,1536]{1,0:T(8,128)(2,1)S(1)}, bf16[1024,1536]{1,0:T(8,128)(2,1)}, u32[]{:S(2)}, u32[]{:S(2)}) collective-permute-start(bf16[1024,1536]{1,0:T(8,128)(2,1)S(1)} %copy-done), channel_id=1, source_target_pairs={{0,4},{4,8},{8,12},{12,14},{14,10},{10,6},{6,2},{2,0},{1,5},{5,9},... | collective-permute-start | bytes 9437192 | tf_op jit(solution)/shard_map/ppermute | solution.py:175
  25.8 7.6 %shard_map.77.refs_3_ = bf16[1024,1536]{1,0:T(8,128)(2,1)} custom-call(s32[1,8]{1,0:T(1,128)} %get-tuple-element.57.here, s32[1,8]{1,0:T(1,128)} %get-tuple-element.43.at, bf16[1024,1536]{1,0:T(8,128)(2,1)} %refs_0_.3, bf16[1024,1536]{1,0:T(8,128)(2,1)} %refs_0_.3), custom_call_target="tpu_custom_call" | custom-call | bytes 9437184 | tf_op jit(solution)/shard_map/pallas_call | solution.py:55
  33.4 9.0 %all-gather.2.cloned.1.call-done.a = bf16[1024,8192]{1,0:T(8,128)(2,1)} async-done(((bf16[1024,4096]{1,0:T(8,128)(2,1)}), bf16[1024,8192]{1,0:T(8,128)(2,1)}) %all-gather.2.cloned.1.call-update) | async-done | bytes 16777232 | tf_op jit(solution)/shard_map/all_gather | solution.py:149
  42.4 38.6 %shard_map.78 = bf16[1024,8192]{1,0:T(8,128)(2,1)} custom-call(s32[64]{0:T(128)} %get-tuple-element.21.slots, bf16[1024,8192]{1,0:T(8,128)(2,1)} %all-gather.2.cloned.1.call-done.a), custom_call_target="tpu_custom_call" | custom-call | bytes 33554432 | tf_op jit(solution)/shard_map/pallas_call | solution.py:21
  86.3 8.3 %shard_map.79.refs_2_ = bf16[1024,1536]{1,0:T(8,128)(2,1)} custom-call(s32[3,8]{1,0:T(4,128)} %and_convert_fusion.2.here, s32[3,8]{1,0:T(4,128)} %fusion.24.at, bf16[1024,1536]{1,0:T(8,128)(2,1)} %refs_0_.3, bf16[1024,1536]{1,0:T(8,128)(2,1)} %collective-permute-done.refs_1_, bf16[1024,1536]{1,0:T(8,128)(2,1)} %collective-permute-done.1.refs_2_, ...), custom_call_target="tpu_custom_call" | custom-call | bytes 15728640 | tf_op jit(solution)/shard_map/pallas_call | solution.py:55
  94.7 5.0 %fusion.15 = f32[1024,1536]{1,0:T(8,128)S(1)} fusion(bf16[1024,1536]{1,0:T(8,128)(2,1)S(1)} %copy-done.1, bf16[1024,8192]{1,0:T(8,128)(2,1)} %shard_map.78, s32[]{:T(128)S(6)} %select_n.86), kind=kOutput, calls=%fused_computation.14 | convolution fusion | flops 3221225472 | bytes 11534340 | tf_op jit(solution)/shard_map/dot_general | solution.py:156
  99.7 5.9 %fusion.13 = f32[1024,1536]{1,0:T(8,128)S(1)} fusion(bf16[1024,1536]{1,0:T(8,128)(2,1)} %collective-permute-done.refs_1_, bf16[1024,8192]{1,0:T(8,128)(2,1)} %shard_map.78, s32[]{:T(128)S(6)} %select_n.89), kind=kOutput, calls=%fused_computation.12 | convolution fusion | flops 3221225472 | bytes 11534340 | tf_op jit(solution)/shard_map/dot_general | solution.py:156
  105.6 8.6 %add_add_fusion.2 = f32[1024,1536]{1,0:T(8,128)} fusion(f32[1024,1536]{1,0:T(8,128)S(1)} %fusion.15, f32[1024,1536]{1,0:T(8,128)S(1)} %fusion.13, bf16[1024,1536]{1,0:T(8,128)(2,1)} %collective-permute-done.1.refs_2_, bf16[1024,8192]{1,0:T(8,128)(2,1)} %shard_map.78, s32[]{:T(128)S(6)} %select_n.92), kind=kOutput, calls=%fused_computation.2 | convolution fusion | flops 3224371200 | bytes 24117252 | tf_op jit(solution)/shard_map/dot_general | solution.py:156
  114.3 37.4 %collective-permute-done.2.refs_0_ = bf16[1024,1536]{1,0:T(8,128)(2,1)} collective-permute-done((bf16[1024,1536]{1,0:T(8,128)(2,1)}, bf16[1024,1536]{1,0:T(8,128)(2,1)}, u32[]{:S(2)}, u32[]{:S(2)}) %collective-permute-start.2) | collective-permute-done | bytes 3145760 | tf_op jit(solution)/shard_map/ppermute | solution.py:175
  160.5 3.1 %constant_dynamic-slice_fusion.coeff = bf16[1024,1024]{1,0:T(8,128)(2,1)} fusion(bf16[1024,8192]{1,0:T(8,128)(2,1)} %shard_map.78, s32[]{:T(128)S(6)} %select_n.105), kind=kLoop, calls=%fused_computation.18 | loop fusion | bytes 4194308 | tf_op jit(solution)/shard_map/dynamic_slice | solution.py:153
  163.6 7.7 %shard_map.80.refs_2_ = bf16[1024,1536]{1,0:T(8,128)(2,1)} custom-call(s32[2,8]{1,0:T(2,128)} %and_convert_fusion.1.here, s32[2,8]{1,0:T(2,128)} %broadcast_clamp_fusion.1.at, bf16[1024,1536]{1,0:T(8,128)(2,1)} %collective-permute-done.2.refs_0_, bf16[1024,1536]{1,0:T(8,128)(2,1)} %collective-permute-done.3.refs_1_, bf16[1024,1536]{1,0:T(8,128)(2,1)} %shard_map.79.refs_2_), custom_call_target="tpu_custom_call" | custom-call | bytes 12582912 | tf_op jit(solution)/shard_map/pallas_call | solution.py:55
  171.4 5.9 %fusion.10 = f32[1024,1536]{1,0:T(8,128)S(1)} fusion(bf16[1024,1536]{1,0:T(8,128)(2,1)} %collective-permute-done.2.refs_0_, bf16[1024,8192]{1,0:T(8,128)(2,1)} %shard_map.78, s32[]{:T(128)S(6)} %select_n.95), kind=kOutput, calls=%fused_computation.9 | convolution fusion | flops 3221225472 | bytes 11534340 | tf_op jit(solution)/shard_map/dot_general | solution.py:156
  177.3 10.6 %add_add_fusion.1 = f32[1024,1536]{1,0:T(8,128)} fusion(f32[1024,1536]{1,0:T(8,128)} %add_add_fusion.2, f32[1024,1536]{1,0:T(8,128)S(1)} %fusion.10, bf16[1024,1536]{1,0:T(8,128)(2,1)} %collective-permute-done.3.refs_1_, bf16[1024,8192]{1,0:T(8,128)(2,1)} %shard_map.78, s32[]{:T(128)S(6)} %select_n.98), kind=kOutput, calls=%fused_computation.1 | convolution fusion | flops 3224371200 | bytes 24117252 | tf_op jit(solution)/shard_map/dot_general | solution.py:156
  187.9 33.9 %collective-permute-done.4.refs_0_ = bf16[1024,1536]{1,0:T(8,128)(2,1)S(1)} collective-permute-done((bf16[1024,1536]{1,0:T(8,128)(2,1)}, bf16[1024,1536]{1,0:T(8,128)(2,1)S(1)}, u32[]{:S(2)}, u32[]{:S(2)}) %collective-permute-start.4) | collective-permute-done | bytes 3145760 | tf_op jit(solution)/shard_map/ppermute | solution.py:175
  226.3 2.7 slice.7
  229.0 7.7 %shard_map.81.mine = bf16[1024,1536]{1,0:T(8,128)(2,1)} custom-call(s32[2,8]{1,0:T(2,128)} %and_convert_fusion.here, s32[2,8]{1,0:T(2,128)} %broadcast_clamp_fusion.at, bf16[1024,1536]{1,0:T(8,128)(2,1)} %copy-done.2, bf16[1024,1536]{1,0:T(8,128)(2,1)} %collective-permute-done.5.refs_1_, bf16[1024,1536]{1,0:T(8,128)(2,1)} %shard_map.80.refs_2_), custom_call_target="tpu_custom_call" | custom-call | bytes 12582912 | tf_op jit(solution)/shard_map/pallas_call | solution.py:55
  236.7 5.0 %fusion.4 = f32[1024,1536]{1,0:T(8,128)S(1)} fusion(bf16[1024,1536]{1,0:T(8,128)(2,1)S(1)} %copy-done.3, bf16[1024,8192]{1,0:T(8,128)(2,1)} %shard_map.78, s32[]{:T(128)S(6)} %select_n.101), kind=kOutput, calls=%fused_computation.5 | convolution fusion | flops 3221225472 | bytes 11534340 | tf_op jit(solution)/shard_map/dot_general | solution.py:156
  241.7 10.6 %add_add_fusion.acc = f32[1024,1536]{1,0:T(8,128)} fusion(f32[1024,1536]{1,0:T(8,128)} %add_add_fusion.1, f32[1024,1536]{1,0:T(8,128)S(1)} %fusion.4, bf16[1024,1536]{1,0:T(8,128)(2,1)} %collective-permute-done.5.refs_1_, bf16[1024,8192]{1,0:T(8,128)(2,1)} %shard_map.78, s32[]{:T(128)S(6)} %select_n.104), kind=kOutput, calls=%fused_computation | convolution fusion | flops 3224371200 | bytes 24117252 | tf_op jit(solution)/shard_map/dot_general | solution.py:156
  252.3 6.0 %collective-permute-done.6.left = bf16[1024,768]{1,0:T(8,128)(2,1)} collective-permute-done((bf16[1024,768]{1,0:T(8,128)(2,1)}, bf16[1024,768]{1,0:T(8,128)(2,1)}, u32[]{:S(2)}, u32[]{:S(2)}) %collective-permute-start.6) | collective-permute-done | bytes 1572896 | tf_op jit(solution)/shard_map/ppermute | solution.py:177
  258.3 4.9 %collective-permute-done.7.right = bf16[1024,768]{1,0:T(8,128)(2,1)} collective-permute-done((bf16[1024,768]{1,0:T(8,128)(2,1)}, bf16[1024,768]{1,0:T(8,128)(2,1)}, u32[]{:S(2)}, u32[]{:S(2)}) %collective-permute-start.7) | collective-permute-done | bytes 1572896 | tf_op jit(solution)/shard_map/ppermute | solution.py:178
  263.2 10.2 %shard_map.82 = (bf16[1024,1536]{1,0:T(8,128)(2,1)}, f32[1,1536]{1,0:T(1,128)}) custom-call(s32[8]{0:T(128)} %get-tuple-element.58.here, s32[8]{0:T(128)} %get-tuple-element.49.at, f32[1024,1536]{1,0:T(8,128)} %add_add_fusion.acc, bf16[1024,1024]{1,0:T(8,128)(2,1)} %constant_dynamic-slice_fusion.coeff, bf16[1024,768]{1,0:T(8,128)(2,1)} %collective-permute-done.6.left, ...), custom_call_target="tpu_custom_call" | custom-call | flops 3221225472 | bytes 16777216 | tf_op jit(solution)/shard_map/pallas_call | solution.py:104
  273.5 3.8 %collective-permute-done.8 = f32[1,1536]{1,0:T(1,128)S(1)} collective-permute-done((f32[1,1536]{1,0:T(1,128)}, f32[1,1536]{1,0:T(1,128)S(1)}, u32[]{:S(2)}, u32[]{:S(2)}) %collective-permute-start.8) | collective-permute-done | bytes 6176 | tf_op jit(solution)/shard_map/ppermute | solution.py:130
  281.6 2.1 collective-permute-start.10
  283.7 2.5 collective-permute-done.10
  (50 shorter events, 25.6 us)
Async XLA Ops:
  7.2 5.0 %copy-start.7 = (s32[8]{0:T(128)S(1)}, s32[8]{0:T(128)}, u32[]{:S(2)}) copy-start(s32[8]{0:T(128)} %constant.101.clone) | copy-start | bytes 100
  7.2 10.2 %copy-start.4 = (s32[8]{0:T(128)S(1)}, s32[8]{0:T(128)}, u32[]{:S(2)}) copy-start(s32[8]{0:T(128)} %constant.100.clone) | copy-start | bytes 100
  7.2 1.9 copy-start
  7.2 15.4 %copy-start.6 = (s32[64]{0:T(128)S(1)}, s32[64]{0:T(128)}, u32[]{:S(2)}) copy-start(s32[64]{0:T(128)} %param.8) | copy-start | bytes 772
  7.2 35.2 %all-gather.2.cloned.1.call-start = ((), (), s32[]{:S(2)}) async-start(), calls=%async_computation | async-start | bytes 25165824 | tf_op jit(solution)/shard_map/all_gather | solution.py:149
  9.1 71.9 %collective-permute-start = (bf16[1024,1536]{1,0:T(8,128)(2,1)S(1)}, bf16[1024,1536]{1,0:T(8,128)(2,1)}, u32[]{:S(2)}, u32[]{:S(2)}) collective-permute-start(bf16[1024,1536]{1,0:T(8,128)(2,1)S(1)} %copy-done), channel_id=1, source_target_pairs={{0,4},{4,8},{8,12},{12,14},{14,10},{10,6},{6,2},{2,0},{1,5},{5,9},... | collective-permute-start | bytes 9437192 | tf_op jit(solution)/shard_map/ppermute | solution.py:175
  12.1 69.7 %collective-permute-start.1 = (bf16[1024,1536]{1,0:T(8,128)(2,1)S(1)}, bf16[1024,1536]{1,0:T(8,128)(2,1)}, u32[]{:S(2)}, u32[]{:S(2)}) collective-permute-start(bf16[1024,1536]{1,0:T(8,128)(2,1)S(1)} %copy-done), channel_id=1, source_target_pairs={{4,0},{8,4},{12,8},{14,12},{10,14},{6,10},{2,6},{0,2},{5,1},{9,5},... | collective-permute-start | bytes 9437192 | tf_op jit(solution)/shard_map/ppermute | solution.py:175
  81.8 69.9 %collective-permute-start.2 = (bf16[1024,1536]{1,0:T(8,128)(2,1)}, bf16[1024,1536]{1,0:T(8,128)(2,1)}, u32[]{:S(2)}, u32[]{:S(2)}) collective-permute-start(bf16[1024,1536]{1,0:T(8,128)(2,1)} %collective-permute-done.refs_1_), channel_id=1, source_target_pairs={{0,4},{4,8},{8,12},{12,14},{14,10},{10,6},{6,2},{2,0},{1,5},{5,9},... | collective-permute-start | bytes 9437192 | tf_op jit(solution)/shard_map/ppermute | solution.py:175
  83.4 69.8 %collective-permute-start.3 = (bf16[1024,1536]{1,0:T(8,128)(2,1)}, bf16[1024,1536]{1,0:T(8,128)(2,1)}, u32[]{:S(2)}, u32[]{:S(2)}) collective-permute-start(bf16[1024,1536]{1,0:T(8,128)(2,1)} %collective-permute-done.1.refs_2_), channel_id=1, source_target_pairs={{4,0},{8,4},{12,8},{14,12},{10,14},{6,10},{2,6},{0,2},{5,1},{9,5},... | collective-permute-start | bytes 9437192 | tf_op jit(solution)/shard_map/ppermute | solution.py:175
  86.3 8.3 %copy-start.1 = (bf16[1024,1536]{1,0:T(8,128)(2,1)S(1)}, bf16[1024,1536]{1,0:T(8,128)(2,1)}, u32[]{:S(2)}) copy-start(bf16[1024,1536]{1,0:T(8,128)(2,1)} %refs_0_.3) | copy-start | bytes 9437188
  153.1 68.7 %collective-permute-start.4 = (bf16[1024,1536]{1,0:T(8,128)(2,1)}, bf16[1024,1536]{1,0:T(8,128)(2,1)S(1)}, u32[]{:S(2)}, u32[]{:S(2)}) collective-permute-start(bf16[1024,1536]{1,0:T(8,128)(2,1)} %collective-permute-done.2.refs_0_), channel_id=1, source_target_pairs={{0,4},{4,8},{8,12},{12,14},{14,10},{10,6},{6,2},{2,0},{1,5},{5,9},... | collective-permute-start | bytes 9437192 | tf_op jit(solution)/shard_map/ppermute | solution.py:175
  154.6 68.5 %collective-permute-start.5 = (bf16[1024,1536]{1,0:T(8,128)(2,1)}, bf16[1024,1536]{1,0:T(8,128)(2,1)}, u32[]{:S(2)}, u32[]{:S(2)}) collective-permute-start(bf16[1024,1536]{1,0:T(8,128)(2,1)} %collective-permute-done.3.refs_1_), channel_id=1, source_target_pairs={{4,0},{8,4},{12,8},{14,12},{10,14},{6,10},{2,6},{0,2},{5,1},{9,5},... | collective-permute-start | bytes 9437192 | tf_op jit(solution)/shard_map/ppermute | solution.py:175
  221.8 7.1 %copy-start.2 = (bf16[1024,1536]{1,0:T(8,128)(2,1)}, bf16[1024,1536]{1,0:T(8,128)(2,1)S(1)}, u32[]{:S(2)}) copy-start(bf16[1024,1536]{1,0:T(8,128)(2,1)S(1)} %collective-permute-done.4.refs_0_) | copy-start | bytes 9437188
  224.3 34.0 %collective-permute-start.6 = (bf16[1024,768]{1,0:T(8,128)(2,1)}, bf16[1024,768]{1,0:T(8,128)(2,1)}, u32[]{:S(2)}, u32[]{:S(2)}) collective-permute-start(bf16[1024,768]{1,0:T(8,128)(2,1)} %slice.6), channel_id=1, source_target_pairs={{0,4},{4,8},{8,12},{12,14},{14,10},{10,6},{6,2},{2,0},{1,5},{5,9},... | collective-permute-start | bytes 4718600 | tf_op jit(solution)/shard_map/ppermute | solution.py:177
  228.9 34.3 %collective-permute-start.7 = (bf16[1024,768]{1,0:T(8,128)(2,1)}, bf16[1024,768]{1,0:T(8,128)(2,1)}, u32[]{:S(2)}, u32[]{:S(2)}) collective-permute-start(bf16[1024,768]{1,0:T(8,128)(2,1)} %slice.7), channel_id=1, source_target_pairs={{4,0},{8,4},{12,8},{14,12},{10,14},{6,10},{2,6},{0,2},{5,1},{9,5},... | collective-permute-start | bytes 4718600 | tf_op jit(solution)/shard_map/ppermute | solution.py:178
  229.0 7.7 %copy-start.3 = (bf16[1024,1536]{1,0:T(8,128)(2,1)S(1)}, bf16[1024,1536]{1,0:T(8,128)(2,1)}, u32[]{:S(2)}) copy-start(bf16[1024,1536]{1,0:T(8,128)(2,1)} %copy-done.2) | copy-start | bytes 9437188
  263.2 23.0 %copy-start.5 = (f32[1536]{0:T(1024)S(1)}, f32[1536]{0:T(1024)}, u32[]{:S(2)}) copy-start(f32[1536]{0:T(1024)} %param.9) | copy-start | bytes 18436
  273.4 3.8 %collective-permute-start.8 = (f32[1,1536]{1,0:T(1,128)}, f32[1,1536]{1,0:T(1,128)S(1)}, u32[]{:S(2)}, u32[]{:S(2)}) collective-permute-start(f32[1,1536]{1,0:T(1,128)} %get-tuple-element.39), channel_id=1, source_target_pairs={{0,2},{2,0},{4,6},{6,4},{8,10},{10,8},{12,14},{14,12},{1,3},{3,1},... | collective-permute-start | bytes 18440 | tf_op jit(solution)/shard_map/ppermute | solution.py:130
  278.0 3.6 %collective-permute-start.9 = (f32[1,1536]{1,0:T(1,128)S(1)}, f32[1,1536]{1,0:T(1,128)S(1)}, u32[]{:S(2)}, u32[]{:S(2)}) collective-permute-start(f32[1,1536]{1,0:T(1,128)S(1)} %add.171), channel_id=1, source_target_pairs={{0,4},{2,6},{4,0},{6,2},{8,12},{10,14},{12,8},{14,10},{1,5},{3,7},... | collective-permute-start | bytes 18440 | tf_op jit(solution)/shard_map/ppermute | solution.py:130
  281.6 4.6 %collective-permute-start.10 = (f32[1,1536]{1,0:T(1,128)S(1)}, f32[1,1536]{1,0:T(1,128)S(1)}, u32[]{:S(2)}, u32[]{:S(2)}) collective-permute-start(f32[1,1536]{1,0:T(1,128)S(1)} %add.172), channel_id=1, source_target_pairs={{0,8},{2,10},{4,12},{6,14},{8,0},{10,2},{12,4},{14,6},{1,9},{3,11}... | collective-permute-start | bytes 18440 | tf_op jit(solution)/shard_map/ppermute | solution.py:130
Sparse Core Ops, SparseCore 0:
  9.6 32.7 all-gather.1

commit v3 on v0

v3 whole, which is shorter than its diff:
```python
import functools

import jax
import jax.numpy as jnp
from jax import lax
from jax.experimental import pallas as pl
from jax.experimental.pallas import tpu as pltpu
from jax.sharding import PartitionSpec as P

TILE = 128
F32 = jnp.float32
VMEM_LIMIT = 56 * 1024 * 1024


def reorder_kernel(side, at, own, other, out):
    k = pl.program_id(0)
    out[...] = jnp.where(side[k] == 0, own[...], other[...])


def reorder(own, other, logical):
    rows, half = own.shape
    per_half = half // TILE
    side = (logical // per_half != lax.axis_index("col")).astype(jnp.int32)
    step = jnp.arange(2 * per_half, dtype=jnp.int32)
    upto = step[None, :] <= step[:, None]
    last = lambda flag: jnp.max(jnp.where(upto & flag[None, :], step[None, :], 0), axis=1)
    at = (logical % per_half)[jnp.stack([last(side == 0), last(side == 1)])]
    tile = lambda p: pl.BlockSpec((rows, TILE), functools.partial(lambda p, k, s, a: (0, a[p, k]), p))
    return pl.pallas_call(
        reorder_kernel,
        grid_spec=pltpu.PrefetchScalarGridSpec(
            num_scalar_prefetch=2,
            grid=(2 * per_half,),
            in_specs=[tile(0), tile(1)],
            out_specs=pl.BlockSpec((rows, TILE), lambda k, s, a: (0, k)),
        ),
        out_shape=jax.ShapeDtypeStruct((rows, 2 * half), own.dtype),
        cost_estimate=pl.CostEstimate(flops=0, bytes_accessed=rows * half, transcendentals=0),
    )(side, at, own, other)


def found(wanted, source, per):
    rel = wanted - source * per
    here = ((rel >= 0) & (rel < per)).astype(jnp.int32)
    return here, jnp.clip(rel, 0, per - 1)


def tile_rows(at):
    return pl.ds(pl.multiple_of(at * TILE, TILE), TILE)


def accumulate_kernel(count, first, blocks, source, here, at, *refs):
    sigmas, pieces = refs[:count], refs[count : 3 * count]
    acc_in, mine_in = (None, None) if first else refs[3 * count : 3 * count + 2]
    acc, mine = refs[-2:]
    j = pl.program_id(0)
    for side in range(2):

        @pl.when(j // blocks == side)
        def _():
            for p in range(count):
                term = jnp.dot(sigmas[p][...], pieces[2 * p + side][...], preferred_element_type=F32)
                if p > 0:
                    acc[...] += term
                elif first:
                    acc[...] = term
                else:
                    acc[...] = acc_in[...] + term
            for t in range(acc.shape[0] // TILE):
                rows = slice(t * TILE, (t + 1) * TILE)
                value = None if first else mine_in[rows, :]
                for p in range(count):
                    got = pieces[2 * p + side][tile_rows(at[p, t]), :]
                    value = got if value is None else jnp.where(here[p, t] != 0, got, value)
                mine[rows, :] = value


def sides(rows, unit, blocks):
    left = pl.BlockSpec((rows, unit), lambda j, *_: (0, jnp.minimum(j, blocks - 1)))
    right = pl.BlockSpec((rows, unit), lambda j, *_: (0, jnp.maximum(j - blocks, 0)))
    return [left, right]


def accumulate(sigma, sources, pieces, wanted, state, unit):
    count = len(sources)
    first = state is None
    rows, half = pieces[0][0].shape
    blocks = half // unit
    per = rows // TILE
    marks = [found(wanted, s, per) for s in sources]
    here = jnp.stack([m[0] for m in marks])
    at = jnp.stack([m[1] for m in marks])
    cut = pl.BlockSpec((rows, unit), lambda j, *_: (0, j))
    sigma_specs = [
        pl.BlockSpec((rows, rows), functools.partial(lambda p, j, s, *_: (0, s[p]), p))
        for p in range(count)
    ]
    flat = [x for pair in pieces for x in pair]
    extra = [] if first else list(state)
    start = 3 + 3 * count
    return pl.pallas_call(
        functools.partial(accumulate_kernel, count, first, blocks),
        grid_spec=pltpu.PrefetchScalarGridSpec(
            num_scalar_prefetch=3,
            grid=(2 * blocks,),
            in_specs=sigma_specs + sides(rows, unit, blocks) * count + [cut] * len(extra),
            out_specs=[cut, cut],
        ),
        out_shape=[
            jax.ShapeDtypeStruct((rows, 2 * half), F32),
            jax.ShapeDtypeStruct((rows, 2 * half), flat[0].dtype),
        ],
        input_output_aliases={} if first else {start: 0, start + 1: 1},
        compiler_params=pltpu.CompilerParams(vmem_limit_bytes=VMEM_LIMIT),
        cost_estimate=pl.CostEstimate(flops=count * rows * half, bytes_accessed=rows * half, transcendentals=0),
    )(jnp.stack(sources), here, at, *([sigma] * count), *flat, *extra)


def finish_kernel(blocks, source, here, at, sigma, left, right, acc, mine, out, part):
    j = pl.program_id(0)
    for side, late in enumerate((left, right)):

        @pl.when(j // blocks == side)
        def _():
            prod = acc[...] + jnp.dot(sigma[...], late[...], preferred_element_type=F32)
            out[...] = (-prod).astype(out.dtype)
            total = None
            for t in range(acc.shape[0] // TILE):
                rows = slice(t * TILE, (t + 1) * TILE)
                tile = jnp.where(here[t] != 0, late[tile_rows(at[t]), :], mine[rows, :])
                add = tile.astype(F32) * prod[rows]
                total = add if total is None else total + add
            part[...] = jnp.sum(total, axis=0, keepdims=True)


def finish(sigma, source, left, right, state, wanted, unit):
    acc, mine = state
    rows, cols = acc.shape
    blocks = left.shape[1] // unit
    here, at = found(wanted, source, rows // TILE)
    cut = pl.BlockSpec((rows, unit), lambda j, *_: (0, j))
    return pl.pallas_call(
        functools.partial(finish_kernel, blocks),
        grid_spec=pltpu.PrefetchScalarGridSpec(
            num_scalar_prefetch=3,
            grid=(2 * blocks,),
            in_specs=[pl.BlockSpec((rows, rows), lambda j, s, *_: (0, s[0]))]
            + sides(rows, unit, blocks)
            + [cut, cut],
            out_specs=[cut, pl.BlockSpec((1, unit), lambda j, *_: (0, j))],
        ),
        out_shape=[
            jax.ShapeDtypeStruct((rows, cols), jnp.bfloat16),
            jax.ShapeDtypeStruct((1, cols), F32),
        ],
        compiler_params=pltpu.CompilerParams(vmem_limit_bytes=VMEM_LIMIT),
        cost_estimate=pl.CostEstimate(flops=rows * cols, bytes_accessed=rows * cols, transcendentals=0),
    )(source[None], here, at, sigma, left, right, acc, mine)


def row_sum(value, n):
    step = 1
    if n & (n - 1):
        return lax.psum(value, "row")
    while step < n:
        value = value + lax.ppermute(value, "row", [(i, i ^ step) for i in range(n)])
        step *= 2
    return value


def body(sigma_anc, panel, holder, dinv_diag):
    n = lax.axis_size("row")
    me = lax.axis_index("row")
    rows, cols = panel.shape
    per = rows // TILE
    half = cols // 2
    unit = half // 3 if half % (3 * TILE) == 0 else half
    order = list(range(0, n, 2)) + list(range(1, n, 2))[::-1]
    table = jnp.array(order, jnp.int32)
    place = jnp.array([order.index(i) for i in range(n)], jnp.int32)[me]
    fwd = [(order[i], order[(i + 1) % n]) for i in range(n)]
    bwd = [(b, a) for a, b in fwd]
    ahead = lambda x: lax.ppermute(x, "row", fwd)
    back = lambda x: lax.ppermute(x, "row", bwd)
    wanted = lax.dynamic_slice_in_dim(holder, me * per, per)
    tile_ids = jnp.arange(holder.shape[0], dtype=jnp.int32)
    logical = jnp.sum(
        jnp.where(holder[:, None] == tile_ids[None, :], tile_ids[:, None], 0), axis=0
    )

    own = (panel[:, :half], panel[:, half:])
    (al, ar), (bl, br) = own, own
    state = None
    ready = [(me, own)]
    sigma = None
    for hop in range(1, n // 2):
        if hop > 2:
            state = accumulate(sigma, [s for s, _ in ready], [p for _, p in ready], wanted, state, unit)
            ready = []
            al, br, state = lax.optimization_barrier((al, br, state))
        al, br = ahead(al), back(br)
        if hop == 1:
            other = lax.ppermute(sigma_anc, "col", [(0, 1), (1, 0)])
            sigma = reorder(sigma_anc, other, logical)
        if hop == 2:
            ar, bl, sigma = lax.optimization_barrier((ar, bl, sigma))
        ar, bl = ahead(ar), back(bl)
        sources = [table[(place - hop) % n], table[(place + hop) % n]]
        if hop > 1:
            ready += fresh
        fresh = [(sources[0], (al, ar)), (sources[1], (bl, br))]
    state = accumulate(sigma, [s for s, _ in ready], [p for _, p in ready], wanted, state, unit)
    al, br, state = lax.optimization_barrier((al, br, state))
    al, br = ahead(al), back(br)
    state = accumulate(sigma, [s for s, _ in fresh], [p for _, p in fresh], wanted, state, unit)
    al, br, state = lax.optimization_barrier((al, br, state))
    source = table[(place + n // 2) % n]
    out, part = finish(sigma, source, al, br, state, wanted, unit)
    return out, dinv_diag + row_sum(part, n).reshape(cols)


def solution(mesh):
    placed = (
        P(("groups", "row"), "col"),
        P(("groups", "row"), "col"),
        P("groups"),
        P(("groups", "col")),
    )
    return jax.shard_map(
        body,
        mesh=mesh,
        in_specs=placed,
        out_specs=(P(("groups", "row"), "col"), P(("groups", "col"))),
        check_vma=False,
    )
```

time: 659 us -> 271 us (0.41)
  waiting for transfers between devices: 491 us -> 122 us
  matrix products: 113 us -> 0 us
  Pallas kernels: 0 us -> 99.1 us
  blocking collectives: 20.4 us -> 0 us
  starting transfers between devices: 0.08 us -> 20 us
  local copies, waits for them, and re-layouts: 19.6 us -> 6.64 us
  other arithmetic: 0.6 us -> 11.8 us
    all_gather x2 -> x0, waiting for transfers between devices: 489 us -> none  [the longest x1 456 us: body(): piece = lax.all_gather(panel, 'row', axis=0, tiled=True)]
    ppermute x0 -> x18, waiting for transfers between devices: none -> 122 us  [the longest x7 108 us: body(): ahead = lambda x: lax.ppermute(x, 'row', fwd)]
    dot_general x3 -> x0, matrix products: 113 us -> none  [the longest x1 63.2 us: body(): jnp.dot(picked.astype(jnp.bfloat16).reshape(local_rows, count), piece, pr...]
    pallas_call x0 -> x5, Pallas kernels: none -> 99.1 us  [the longest x3 47.9 us: accumulate(): pl.pallas_call(functools.partial(accumulate_kernel, count, first, blocks)...]
    psum x1 -> x0, blocking collectives: 20.4 us -> none  [body(): variances = dinv_diag + lax.psum(partial_sums, 'row')]
    ppermute x0 -> x18, starting transfers between devices: none -> 20 us  [the longest x7 12.5 us: body(): ahead = lambda x: lax.ppermute(x, 'row', fwd)]
    unnamed x5 -> x24, local copies, waits for them, and re-layouts: 15.3 us -> 1.21 us
    another operation x0 -> x12, other arithmetic: none -> 10.1 us  [the longest x3 5.52 us: accumulate(): jnp.stack(sources)]
  transfers between devices with their start and end apart: 2 -> 18, of which waited for: 2 -> 11; matrix products, arithmetic and copies ran while one was open for 4% -> 6% of each run, Pallas kernels for 0% -> 33%
where the time goes in v3:
time: 271 us; the launch traced here: 270 us
  waiting for transfers between devices  122 us (45%)
  Pallas kernels  99.1 us (37%)
  starting transfers between devices  20 us (7%)
  other arithmetic  11.8 us (4%)
  between operations  10.1 us (4%)
  local copies, waits for them, and re-layouts  6.64 us (2%)
    ppermute x7, waiting for transfers between devices, body(): ahead = lambda x: lax.ppermute(x, 'row', fwd)  108 us
    pallas_call x3, Pallas kernels, accumulate(): pl.pallas_call(functools.partial(accumulate_kernel, count, first, blocks)...  47.9 us
    pallas_call x1, Pallas kernels, reorder(): pl.pallas_call(reorder_kernel, grid_spec=pltpu.PrefetchScalarGridSpec(num...  39.8 us
    ppermute x7, starting transfers between devices, body(): ahead = lambda x: lax.ppermute(x, 'row', fwd)  12.5 us
    pallas_call x1, Pallas kernels, finish(): pl.pallas_call(functools.partial(finish_kernel, blocks), grid_spec=pltpu....  11.4 us
    ppermute x3, waiting for transfers between devices, row_sum(): lax.ppermute(value, 'row', [(i, i ^ step) for i in range(n)])  7.54 us
    ppermute x7, waiting for transfers between devices, body(): back = lambda x: lax.ppermute(x, 'row', bwd)  5.85 us
    another operation x3, other arithmetic, accumulate(): jnp.stack(sources)  5.52 us
  transfers between devices with their start and end apart: 18, of which 11 were waited for; matrix products, arithmetic and copies ran while one was open for 6% of the time, Pallas kernels for 33%

profile of v3, /device:TPU:0, one launch (start us, length us, event | category | flops | bytes accessed | tf_op | source)
XLA Modules:
  0.0 269.6 jit_solution(11028420667622182345)
XLA Ops:
  1.2 2.1 fusion.3
  3.3 2.6 collective-permute-start.3
  5.9 2.0 collective-permute-start
  8.1 33.1 %collective-permute-done.3.refs_5_ = bf16[1024,768]{1,0:T(8,128)(2,1)} collective-permute-done((bf16[1024,768]{1,0:T(8,128)(2,1)S(1)}, bf16[1024,768]{1,0:T(8,128)(2,1)}, u32[]{:S(2)}, u32[]{:S(2)}) %collective-permute-start.3) | collective-permute-done | bytes 1572896 | tf_op jit(solution)/shard_map/ppermute | solution.py:183
  41.2 2.0 collective-permute-start.4
  56.3 1.9 pad_add_fusion.3.source
  60.5 39.8 %shard_map.77.refs_0_.refs_1_.refs_2_.sigma = bf16[1024,8192]{1,0:T(8,128)(2,1)} custom-call(s32[64]{0:T(128)} %copy-done.9, s32[2,64]{1,0:T(2,128)} %reshape.146.at, bf16[1024,4096]{1,0:T(8,128)(2,1)} %own.1, bf16[1024,4096]{1,0:T(8,128)(2,1)} %collective-permute-done.2.other), custom_call_target="tpu_custom_call" | custom-call | bytes 4194304 | tf_op jit(solution)/shard_map/pallas_call | solution.py:29
  100.3 2.0 collective-permute-start.10
  102.4 17.1 %shard_map.78 = (f32[1024,1536]{1,0:T(8,128)}, bf16[1024,1536]{1,0:T(8,128)(2,1)}) custom-call(s32[3]{0:T(128)} %pad_add_fusion.3.source, s32[3,8]{1,0:T(4,128)} %add_convert_fusion.here, s32[3,8]{1,0:T(4,128)} %pad_add_fusion.at, bf16[1024,8192]{1,0:T(8,128)(2,1)} %shard_map.77.refs_0_.refs_1_.refs_2_.sigma, ...), custom_call_target="tpu_custom_call" | custom-call | flops 2359296 | bytes 786432 | tf_op jit(solution)/shard_map/pallas_call | solution.py:101
  119.6 2.0 collective-permute-start.7
  124.6 17.6 %collective-permute-done.9.refs_3_ = bf16[1024,768]{1,0:T(8,128)(2,1)S(1)} collective-permute-done((bf16[1024,768]{1,0:T(8,128)(2,1)}, bf16[1024,768]{1,0:T(8,128)(2,1)S(1)}, u32[]{:S(2)}, u32[]{:S(2)}) %collective-permute-start.9) | collective-permute-done | bytes 1572896 | tf_op jit(solution)/shard_map/ppermute | solution.py:183
  142.2 2.0 collective-permute-start.13
  145.5 15.4 %shard_map.79 = (f32[1024,1536]{1,0:T(8,128)}, bf16[1024,1536]{1,0:T(8,128)(2,1)}) custom-call(s32[2]{0:T(128)} %pad_add_fusion.4.source, s32[2,8]{1,0:T(2,128)} %add_convert_fusion.1.here, s32[2,8]{1,0:T(2,128)} %pad_add_fusion.1.at, bf16[1024,8192]{1,0:T(8,128)(2,1)} %shard_map.77.refs_0_.refs_1_.refs_2_.sigma, ...), custom_call_target="tpu_custom_call", output_to_operand_aliasing={{0}: (9, {}), {1}: (10, {})} | custom-call | flops 1572864 | bytes 786432 | tf_op jit(solution)/shard_map/pallas_call | solution.py:101
  160.8 15.1 %collective-permute-done.7.refs_2_ = bf16[1024,768]{1,0:T(8,128)(2,1)S(1)} collective-permute-done((bf16[1024,768]{1,0:T(8,128)(2,1)}, bf16[1024,768]{1,0:T(8,128)(2,1)S(1)}, u32[]{:S(2)}, u32[]{:S(2)}) %collective-permute-start.7) | collective-permute-done | bytes 1572896 | tf_op jit(solution)/shard_map/ppermute | solution.py:183
  175.9 2.1 collective-permute-done.8.refs_5_
  183.0 26.6 %collective-permute-done.13.refs_3_ = bf16[1024,768]{1,0:T(8,128)(2,1)S(1)} collective-permute-done((bf16[1024,768]{1,0:T(8,128)(2,1)S(1)}, bf16[1024,768]{1,0:T(8,128)(2,1)S(1)}, u32[]{:S(2)}, u32[]{:S(2)}) %collective-permute-start.13) | collective-permute-done | bytes 1572896 | tf_op jit(solution)/shard_map/ppermute | solution.py:183
  209.6 2.2 collective-permute-done.14.refs_4_
  211.8 15.4 %shard_map.80 = (f32[1024,1536]{1,0:T(8,128)}, bf16[1024,1536]{1,0:T(8,128)(2,1)}) custom-call(s32[2]{0:T(128)} %pad_add_fusion.5.source, s32[2,8]{1,0:T(2,128)} %add_convert_fusion.2.here, s32[2,8]{1,0:T(2,128)} %pad_add_fusion.2.at, bf16[1024,8192]{1,0:T(8,128)(2,1)} %shard_map.77.refs_0_.refs_1_.refs_2_.sigma, ...), custom_call_target="tpu_custom_call", output_to_operand_aliasing={{0}: (9, {}), {1}: (10, {})} | custom-call | flops 1572864 | bytes 786432 | tf_op jit(solution)/shard_map/pallas_call | solution.py:101
  227.2 16.0 %collective-permute-done.11.left = bf16[1024,768]{1,0:T(8,128)(2,1)} collective-permute-done((bf16[1024,768]{1,0:T(8,128)(2,1)S(1)}, bf16[1024,768]{1,0:T(8,128)(2,1)}, u32[]{:S(2)}, u32[]{:S(2)}) %collective-permute-start.11) | collective-permute-done | bytes 1572896 | tf_op jit(solution)/shard_map/ppermute | solution.py:183
  244.8 11.4 %shard_map.81 = (bf16[1024,1536]{1,0:T(8,128)(2,1)}, f32[1,1536]{1,0:T(1,128)}) custom-call(s32[1]{0:T(128)} %get-tuple-element.74.source, s32[8]{0:T(128)} %get-tuple-element.68.here, s32[8]{0:T(128)} %get-tuple-element.60.at, bf16[1024,8192]{1,0:T(8,128)(2,1)} %shard_map.77.refs_0_.refs_1_.refs_2_.sigma, bf16[1024,768]{1,0:T(8,128)(2,1)} %collective-permute-done.11.left, ...), custom_call_target="tpu_custom_call" | custom-call | flops 1572864 | bytes 1572864 | tf_op jit(solution)/shard_map/pallas_call | solution.py:142
  256.5 3.6 %collective-permute-done.15 = f32[1,1536]{1,0:T(1,128)S(1)} collective-permute-done((f32[1,1536]{1,0:T(1,128)}, f32[1,1536]{1,0:T(1,128)S(1)}, u32[]{:S(2)}, u32[]{:S(2)}) %collective-permute-start.15) | collective-permute-done | bytes 6176 | tf_op jit(solution)/shard_map/ppermute | solution.py:166
  262.3 2.1 collective-permute-done.16
  264.4 2.7 collective-permute-start.17
  267.0 1.9 collective-permute-done.17
  (71 shorter events, 20.8 us)
Async XLA Ops:
  0.6 42.7 %copy-start.11 = (s32[8]{0:T(128)S(1)}, s32[8]{0:T(128)}, u32[]{:S(2)}) copy-start(s32[8]{0:T(128)} %constant.118.clone) | copy-start | bytes 100
  0.6 48.3 %copy-start.7 = (s32[8]{0:T(128)S(1)}, s32[8]{0:T(128)}, u32[]{:S(2)}) copy-start(s32[8]{0:T(128)} %constant.117.clone) | copy-start | bytes 100
  0.7 59.8 %collective-permute-start.2 = (bf16[1024,4096]{1,0:T(8,128)(2,1)}, bf16[1024,4096]{1,0:T(8,128)(2,1)}, u32[]{:S(2)}, u32[]{:S(2)}) collective-permute-start(bf16[1024,4096]{1,0:T(8,128)(2,1)} %own.1), channel_id=1, source_target_pairs={{0,1},{1,0},{2,3},{3,2},{4,5},{5,4},{6,7},{7,6},{8,9},{9,8},{10,11... | collective-permute-start | bytes 25165832 | tf_op jit(solution)/shard_map/ppermute | solution.py:203
  3.3 97.0 %copy-start = (bf16[1024,768]{1,0:T(8,128)(2,1)}, bf16[1024,768]{1,0:T(8,128)(2,1)S(1)}, u32[]{:S(2)}) copy-start(bf16[1024,768]{1,0:T(8,128)(2,1)S(1)} %get-tuple-element.52.refs_3_) | copy-start | bytes 4718596
  3.3 97.0 %copy-start.1 = (bf16[1024,768]{1,0:T(8,128)(2,1)}, bf16[1024,768]{1,0:T(8,128)(2,1)S(1)}, u32[]{:S(2)}) copy-start(bf16[1024,768]{1,0:T(8,128)(2,1)S(1)} %get-tuple-element.53.refs_4_) | copy-start | bytes 4718596
  3.3 37.9 %collective-permute-start.3 = (bf16[1024,768]{1,0:T(8,128)(2,1)S(1)}, bf16[1024,768]{1,0:T(8,128)(2,1)}, u32[]{:S(2)}, u32[]{:S(2)}) collective-permute-start(bf16[1024,768]{1,0:T(8,128)(2,1)S(1)} %get-tuple-element.52.refs_3_), channel_id=1, source_target_pairs={{0,4},{4,8},{8,12},{12,14},{14,10},{10,6},{6,2},{2,0},{1,5},{5,9},... | collective-permute-start | bytes 4718600 | tf_op jit(solution)/shard_map/ppermute | solution.py:183
  5.9 37.3 %collective-permute-start.5 = (bf16[1024,768]{1,0:T(8,128)(2,1)S(1)}, bf16[1024,768]{1,0:T(8,128)(2,1)}, u32[]{:S(2)}, u32[]{:S(2)}) collective-permute-start(bf16[1024,768]{1,0:T(8,128)(2,1)S(1)} %get-tuple-element.53.refs_4_), channel_id=1, source_target_pairs={{4,0},{8,4},{12,8},{14,12},{10,14},{6,10},{2,6},{0,2},{5,1},{9,5},... | collective-permute-start | bytes 4718600 | tf_op jit(solution)/shard_map/ppermute | solution.py:184
  5.9 94.4 %collective-permute-start = (bf16[1024,768]{1,0:T(8,128)(2,1)S(1)}, bf16[1024,768]{1,0:T(8,128)(2,1)}, u32[]{:S(2)}, u32[]{:S(2)}) collective-permute-start(bf16[1024,768]{1,0:T(8,128)(2,1)S(1)} %get-tuple-element.53.refs_4_), channel_id=1, source_target_pairs={{0,4},{4,8},{8,12},{12,14},{14,10},{10,6},{6,2},{2,0},{1,5},{5,9},... | collective-permute-start | bytes 4718600 | tf_op jit(solution)/shard_map/ppermute | solution.py:183
  8.0 92.4 %collective-permute-start.1 = (bf16[1024,768]{1,0:T(8,128)(2,1)S(1)}, bf16[1024,768]{1,0:T(8,128)(2,1)}, u32[]{:S(2)}, u32[]{:S(2)}) collective-permute-start(bf16[1024,768]{1,0:T(8,128)(2,1)S(1)} %get-tuple-element.52.refs_3_), channel_id=1, source_target_pairs={{4,0},{8,4},{12,8},{14,12},{10,14},{6,10},{2,6},{0,2},{5,1},{9,5},... | collective-permute-start | bytes 4718600 | tf_op jit(solution)/shard_map/ppermute | solution.py:184
  8.1 52.4 %copy-start.9 = (s32[64]{0:T(128)}, s32[64]{0:T(128)S(1)}, u32[]{:S(2)}) copy-start(s32[64]{0:T(128)S(1)} %get-tuple-element.51.side) | copy-start | bytes 772
  41.2 78.4 %collective-permute-start.4 = (bf16[1024,768]{1,0:T(8,128)(2,1)}, bf16[1024,768]{1,0:T(8,128)(2,1)}, u32[]{:S(2)}, u32[]{:S(2)}) collective-permute-start(bf16[1024,768]{1,0:T(8,128)(2,1)} %collective-permute-done.3.refs_5_), channel_id=1, source_target_pairs={{0,4},{4,8},{8,12},{12,14},{14,10},{10,6},{6,2},{2,0},{1,5},{5,9},... | collective-permute-start | bytes 4718600 | tf_op jit(solution)/shard_map/ppermute | solution.py:183
  43.3 76.3 %collective-permute-start.6 = (bf16[1024,768]{1,0:T(8,128)(2,1)}, bf16[1024,768]{1,0:T(8,128)(2,1)}, u32[]{:S(2)}, u32[]{:S(2)}) collective-permute-start(bf16[1024,768]{1,0:T(8,128)(2,1)} %collective-permute-done.5.refs_8_), channel_id=1, source_target_pairs={{4,0},{8,4},{12,8},{14,12},{10,14},{6,10},{2,6},{0,2},{5,1},{9,5},... | collective-permute-start | bytes 4718600 | tf_op jit(solution)/shard_map/ppermute | solution.py:184
  100.3 44.0 %collective-permute-start.10 = (bf16[1024,768]{1,0:T(8,128)(2,1)}, bf16[1024,768]{1,0:T(8,128)(2,1)S(1)}, u32[]{:S(2)}, u32[]{:S(2)}) collective-permute-start(bf16[1024,768]{1,0:T(8,128)(2,1)} %collective-permute-done.1.refs_7_), channel_id=1, source_target_pairs={{4,0},{8,4},{12,8},{14,12},{10,14},{6,10},{2,6},{0,2},{5,1},{9,5},... | collective-permute-start | bytes 4718600 | tf_op jit(solution)/shard_map/ppermute | solution.py:184
  102.3 39.9 %collective-permute-start.9 = (bf16[1024,768]{1,0:T(8,128)(2,1)}, bf16[1024,768]{1,0:T(8,128)(2,1)S(1)}, u32[]{:S(2)}, u32[]{:S(2)}) collective-permute-start(bf16[1024,768]{1,0:T(8,128)(2,1)} %collective-permute-done.refs_6_), channel_id=1, source_target_pairs={{0,4},{4,8},{8,12},{12,14},{14,10},{10,6},{6,2},{2,0},{1,5},{5,9},... | collective-permute-start | bytes 4718600 | tf_op jit(solution)/shard_map/ppermute | solution.py:183
  119.6 56.3 %collective-permute-start.7 = (bf16[1024,768]{1,0:T(8,128)(2,1)}, bf16[1024,768]{1,0:T(8,128)(2,1)S(1)}, u32[]{:S(2)}, u32[]{:S(2)}) collective-permute-start(bf16[1024,768]{1,0:T(8,128)(2,1)} %collective-permute-done.4.refs_2_), channel_id=1, source_target_pairs={{0,4},{4,8},{8,12},{12,14},{14,10},{10,6},{6,2},{2,0},{1,5},{5,9},... | collective-permute-start | bytes 4718600 | tf_op jit(solution)/shard_map/ppermute | solution.py:183
  121.6 56.4 %collective-permute-start.8 = (bf16[1024,768]{1,0:T(8,128)(2,1)}, bf16[1024,768]{1,0:T(8,128)(2,1)S(1)}, u32[]{:S(2)}, u32[]{:S(2)}) collective-permute-start(bf16[1024,768]{1,0:T(8,128)(2,1)} %collective-permute-done.6.refs_5_), channel_id=1, source_target_pairs={{4,0},{8,4},{12,8},{14,12},{10,14},{6,10},{2,6},{0,2},{5,1},{9,5},... | collective-permute-start | bytes 4718600 | tf_op jit(solution)/shard_map/ppermute | solution.py:184
  142.2 67.4 %collective-permute-start.13 = (bf16[1024,768]{1,0:T(8,128)(2,1)S(1)}, bf16[1024,768]{1,0:T(8,128)(2,1)S(1)}, u32[]{:S(2)}, u32[]{:S(2)}) collective-permute-start(bf16[1024,768]{1,0:T(8,128)(2,1)S(1)} %collective-permute-done.9.refs_3_), channel_id=1, source_target_pairs={{0,4},{4,8},{8,12},{12,14},{14,10},{10,6},{6,2},{2,0},{1,5},{5,9},... | collective-permute-start | bytes 4718600 | tf_op jit(solution)/shard_map/ppermute | solution.py:183
  144.3 67.5 %collective-permute-start.14 = (bf16[1024,768]{1,0:T(8,128)(2,1)S(1)}, bf16[1024,768]{1,0:T(8,128)(2,1)}, u32[]{:S(2)}, u32[]{:S(2)}) collective-permute-start(bf16[1024,768]{1,0:T(8,128)(2,1)S(1)} %collective-permute-done.10.refs_4_), channel_id=1, source_target_pairs={{4,0},{8,4},{12,8},{14,12},{10,14},{6,10},{2,6},{0,2},{5,1},{9,5},... | collective-permute-start | bytes 4718600 | tf_op jit(solution)/shard_map/ppermute | solution.py:184
  175.9 35.9 %copy-start.4 = (bf16[1024,768]{1,0:T(8,128)(2,1)}, bf16[1024,768]{1,0:T(8,128)(2,1)S(1)}, u32[]{:S(2)}) copy-start(bf16[1024,768]{1,0:T(8,128)(2,1)S(1)} %collective-permute-done.7.refs_2_) | copy-start | bytes 4718596
  178.0 65.3 %collective-permute-start.11 = (bf16[1024,768]{1,0:T(8,128)(2,1)S(1)}, bf16[1024,768]{1,0:T(8,128)(2,1)}, u32[]{:S(2)}, u32[]{:S(2)}) collective-permute-start(bf16[1024,768]{1,0:T(8,128)(2,1)S(1)} %collective-permute-done.7.refs_2_), channel_id=1, source_target_pairs={{0,4},{4,8},{8,12},{12,14},{14,10},{10,6},{6,2},{2,0},{1,5},{5,9},... | collective-permute-start | bytes 4718600 | tf_op jit(solution)/shard_map/ppermute | solution.py:183
  179.6 65.2 %collective-permute-start.12 = (bf16[1024,768]{1,0:T(8,128)(2,1)S(1)}, bf16[1024,768]{1,0:T(8,128)(2,1)}, u32[]{:S(2)}, u32[]{:S(2)}) collective-permute-start(bf16[1024,768]{1,0:T(8,128)(2,1)S(1)} %collective-permute-done.8.refs_5_), channel_id=1, source_target_pairs={{4,0},{8,4},{12,8},{14,12},{10,14},{6,10},{2,6},{0,2},{5,1},{9,5},... | collective-permute-start | bytes 4718600 | tf_op jit(solution)/shard_map/ppermute | solution.py:184
  256.2 3.8 %collective-permute-start.15 = (f32[1,1536]{1,0:T(1,128)}, f32[1,1536]{1,0:T(1,128)S(1)}, u32[]{:S(2)}, u32[]{:S(2)}) collective-permute-start(f32[1,1536]{1,0:T(1,128)} %get-tuple-element.47), channel_id=1, source_target_pairs={{0,2},{2,0},{4,6},{6,4},{8,10},{10,8},{12,14},{14,12},{1,3},{3,1},... | collective-permute-start | bytes 18440 | tf_op jit(solution)/shard_map/ppermute | solution.py:166
  260.7 3.6 %collective-permute-start.16 = (f32[1,1536]{1,0:T(1,128)S(1)}, f32[1,1536]{1,0:T(1,128)S(1)}, u32[]{:S(2)}, u32[]{:S(2)}) collective-permute-start(f32[1,1536]{1,0:T(1,128)S(1)} %add.145), channel_id=1, source_target_pairs={{0,4},{2,6},{4,0},{6,2},{8,12},{10,14},{12,8},{14,10},{1,5},{3,7},... | collective-permute-start | bytes 18440 | tf_op jit(solution)/shard_map/ppermute | solution.py:166
  264.4 4.6 %collective-permute-start.17 = (f32[1,1536]{1,0:T(1,128)S(1)}, f32[1,1536]{1,0:T(1,128)S(1)}, u32[]{:S(2)}, u32[]{:S(2)}) collective-permute-start(f32[1,1536]{1,0:T(1,128)S(1)} %add.146), channel_id=1, source_target_pairs={{0,8},{2,10},{4,12},{6,14},{8,0},{10,2},{12,4},{14,6},{1,9},{3,11}... | collective-permute-start | bytes 18440 | tf_op jit(solution)/shard_map/ppermute | solution.py:166
  (6 other events, 70.7 us)

commit v4 on v3

--- a/solution.py
+++ b/solution.py
@@ -9,7 +9,7 @@
 
 TILE = 128
 F32 = jnp.float32
-VMEM_LIMIT = 56 * 1024 * 1024
+VMEM_LIMIT = 28 * 1024 * 1024
 
 
 def reorder_kernel(side, at, own, other, out):

time: 271 us -> 268 us (0.989)
  waiting for transfers between devices: 122 us -> 135 us
  Pallas kernels: 99.1 us -> 90 us
  other arithmetic: 11.8 us -> 5.39 us
    ppermute x7, waiting for transfers between devices: 108 us -> 122 us  [body(): ahead = lambda x: lax.ppermute(x, 'row', fwd)]
    pallas_call x3, Pallas kernels: 47.9 us -> 41.3 us  [accumulate(): pl.pallas_call(functools.partial(accumulate_kernel, count, first, blocks)...]
  transfers between devices with their start and end apart: 18 -> 18, of which waited for: 11 -> 11; matrix products, arithmetic and copies ran while one was open for 6% -> 4% of each run, Pallas kernels for 33% -> 30%
where the time goes in v4:
time: 268 us; the launch traced here: 266 us
  waiting for transfers between devices  135 us (50%)
  Pallas kernels  90 us (34%)
  starting transfers between devices  20.1 us (8%)
  between operations  10.1 us (4%)
  other arithmetic  5.39 us (2%)
  local copies, waits for them, and re-layouts  5.35 us (2%)
    ppermute x7, waiting for transfers between devices, body(): ahead = lambda x: lax.ppermute(x, 'row', fwd)  122 us
    pallas_call x3, Pallas kernels, accumulate(): pl.pallas_call(functools.partial(accumulate_kernel, count, first, blocks)...  41.3 us
    pallas_call x1, Pallas kernels, reorder(): pl.pallas_call(reorder_kernel, grid_spec=pltpu.PrefetchScalarGridSpec(num...  39.8 us
    ppermute x7, starting transfers between devices, body(): ahead = lambda x: lax.ppermute(x, 'row', fwd)  12.5 us
    pallas_call x1, Pallas kernels, finish(): pl.pallas_call(functools.partial(finish_kernel, blocks), grid_spec=pltpu....  8.94 us
    ppermute x3, waiting for transfers between devices, row_sum(): lax.ppermute(value, 'row', [(i, i ^ step) for i in range(n)])  7.34 us
    ppermute x7, waiting for transfers between devices, body(): back = lambda x: lax.ppermute(x, 'row', bwd)  5.76 us
  transfers between devices with their start and end apart: 18, of which 11 were waited for; matrix products, arithmetic and copies ran while one was open for 4% of the time, Pallas kernels for 30%

profile of v4, /device:TPU:0, one launch (start us, length us, event | category | flops | bytes accessed | tf_op | source)
XLA Modules:
  0.0 266.2 jit_solution(6325025564908669106)
XLA Ops:
  1.2 2.1 fusion.3
  3.3 2.6 collective-permute-start.3
  5.9 2.0 collective-permute-start
  8.1 33.1 %collective-permute-done.3.refs_5_ = bf16[1024,768]{1,0:T(8,128)(2,1)} collective-permute-done((bf16[1024,768]{1,0:T(8,128)(2,1)S(1)}, bf16[1024,768]{1,0:T(8,128)(2,1)}, u32[]{:S(2)}, u32[]{:S(2)}) %collective-permute-start.3) | collective-permute-done | bytes 1572896 | tf_op jit(solution)/shard_map/ppermute | solution.py:183
  41.2 2.0 collective-permute-start.4
  57.7 39.8 %shard_map.77.refs_0_.refs_1_.refs_2_.sigma = bf16[1024,8192]{1,0:T(8,128)(2,1)} custom-call(s32[64]{0:T(128)} %copy-done.2, s32[2,64]{1,0:T(2,128)} %reshape.146.at, bf16[1024,4096]{1,0:T(8,128)(2,1)} %own.1, bf16[1024,4096]{1,0:T(8,128)(2,1)} %collective-permute-done.2.other), custom_call_target="tpu_custom_call" | custom-call | bytes 4194304 | tf_op jit(solution)/shard_map/pallas_call | solution.py:29
  97.5 2.0 collective-permute-start.10
  99.6 16.3 %shard_map.78 = (f32[1024,1536]{1,0:T(8,128)S(1)}, bf16[1024,1536]{1,0:T(8,128)(2,1)S(1)}) custom-call(s32[3]{0:T(128)S(1)} %pad_add_fusion.3.source, s32[3,8]{1,0:T(4,128)S(1)} %add_convert_fusion.here, s32[3,8]{1,0:T(4,128)S(1)} %pad_add_fusion.at, bf16[1024,8192]{1,0:T(8,128)(2,1)} %shard_map.77.refs_0_.refs_1_.refs_2_.sigma, ...), custom_call_target="tpu_custom_call" | custom-call | flops 2359296 | bytes 786432 | tf_op jit(solution)/shard_map/pallas_call | solution.py:101
  115.9 2.0 collective-permute-start.7
  119.5 22.7 %collective-permute-done.9.refs_3_ = bf16[1024,768]{1,0:T(8,128)(2,1)S(1)} collective-permute-done((bf16[1024,768]{1,0:T(8,128)(2,1)}, bf16[1024,768]{1,0:T(8,128)(2,1)S(1)}, u32[]{:S(2)}, u32[]{:S(2)}) %collective-permute-start.9) | collective-permute-done | bytes 1572896 | tf_op jit(solution)/shard_map/ppermute | solution.py:183
  142.2 2.0 collective-permute-start.13
  144.3 12.5 %shard_map.79 = (f32[1024,1536]{1,0:T(8,128)S(1)}, bf16[1024,1536]{1,0:T(8,128)(2,1)S(1)}) custom-call(s32[2]{0:T(128)S(1)} %pad_add_fusion.4.source, s32[2,8]{1,0:T(2,128)S(1)} %add_convert_fusion.1.here, s32[2,8]{1,0:T(2,128)S(1)} %pad_add_fusion.1.at, ...), custom_call_target="tpu_custom_call", output_to_operand_aliasing={{0}: (9, {}), {1}: (10, {})} | custom-call | flops 1572864 | bytes 786432 | tf_op jit(solution)/shard_map/pallas_call | solution.py:101
  156.8 19.1 %collective-permute-done.7.refs_2_ = bf16[1024,768]{1,0:T(8,128)(2,1)S(1)} collective-permute-done((bf16[1024,768]{1,0:T(8,128)(2,1)}, bf16[1024,768]{1,0:T(8,128)(2,1)S(1)}, u32[]{:S(2)}, u32[]{:S(2)}) %collective-permute-start.7) | collective-permute-done | bytes 1572896 | tf_op jit(solution)/shard_map/ppermute | solution.py:183
  175.9 2.1 collective-permute-done.8.refs_5_
  181.3 28.3 %collective-permute-done.13.refs_3_ = bf16[1024,768]{1,0:T(8,128)(2,1)S(1)} collective-permute-done((bf16[1024,768]{1,0:T(8,128)(2,1)S(1)}, bf16[1024,768]{1,0:T(8,128)(2,1)S(1)}, u32[]{:S(2)}, u32[]{:S(2)}) %collective-permute-start.13) | collective-permute-done | bytes 1572896 | tf_op jit(solution)/shard_map/ppermute | solution.py:183
  209.6 2.1 collective-permute-done.14.refs_4_
  211.7 12.4 %shard_map.80 = (f32[1024,1536]{1,0:T(8,128)S(1)}, bf16[1024,1536]{1,0:T(8,128)(2,1)S(1)}) custom-call(s32[2]{0:T(128)S(1)} %pad_add_fusion.5.source, s32[2,8]{1,0:T(2,128)S(1)} %add_convert_fusion.2.here, s32[2,8]{1,0:T(2,128)S(1)} %pad_add_fusion.2.at, ...), custom_call_target="tpu_custom_call", output_to_operand_aliasing={{0}: (9, {}), {1}: (10, {})} | custom-call | flops 1572864 | bytes 786432 | tf_op jit(solution)/shard_map/pallas_call | solution.py:101
  224.1 19.0 %collective-permute-done.11.left = bf16[1024,768]{1,0:T(8,128)(2,1)S(1)} collective-permute-done((bf16[1024,768]{1,0:T(8,128)(2,1)S(1)}, bf16[1024,768]{1,0:T(8,128)(2,1)S(1)}, u32[]{:S(2)}, u32[]{:S(2)}) %collective-permute-start.11) | collective-permute-done | bytes 1572896 | tf_op jit(solution)/shard_map/ppermute | solution.py:183
  244.7 8.9 %shard_map.81 = (bf16[1024,1536]{1,0:T(8,128)(2,1)}, f32[1,1536]{1,0:T(1,128)S(1)}) custom-call(s32[1]{0:T(128)} %get-tuple-element.74.source, s32[8]{0:T(128)S(1)} %get-tuple-element.68.here, s32[8]{0:T(128)S(1)} %get-tuple-element.60.at, bf16[1024,8192]{1,0:T(8,128)(2,1)} %shard_map.77.refs_0_.refs_1_.refs_2_.sigma, ...), custom_call_target="tpu_custom_call" | custom-call | flops 1572864 | bytes 1572864 | tf_op jit(solution)/shard_map/pallas_call | solution.py:142
  253.9 3.3 %collective-permute-done.15 = f32[1,1536]{1,0:T(1,128)S(1)} collective-permute-done((f32[1,1536]{1,0:T(1,128)S(1)}, f32[1,1536]{1,0:T(1,128)S(1)}, u32[]{:S(2)}, u32[]{:S(2)}) %collective-permute-start.15) | collective-permute-done | bytes 6176 | tf_op jit(solution)/shard_map/ppermute | solution.py:166
  257.2 1.6 collective-permute-start.16
  258.9 2.1 collective-permute-done.16
  261.0 2.7 collective-permute-start.17
  263.6 1.9 collective-permute-done.17
  (57 shorter events, 13.3 us)
Async XLA Ops:
  0.6 42.6 %copy-start.4 = (s32[8]{0:T(128)S(1)}, s32[8]{0:T(128)}, u32[]{:S(2)}) copy-start(s32[8]{0:T(128)} %constant.118.clone) | copy-start | bytes 100
  0.6 47.9 %copy-start = (s32[8]{0:T(128)S(1)}, s32[8]{0:T(128)}, u32[]{:S(2)}) copy-start(s32[8]{0:T(128)} %constant.117.clone) | copy-start | bytes 100
  0.7 7.3 %copy-start.3 = (s32[64]{0:T(128)S(1)}, s32[64]{0:T(128)}, u32[]{:S(2)}) copy-start(s32[64]{0:T(128)} %param.8) | copy-start | bytes 772
  0.7 57.0 %collective-permute-start.2 = (bf16[1024,4096]{1,0:T(8,128)(2,1)}, bf16[1024,4096]{1,0:T(8,128)(2,1)}, u32[]{:S(2)}, u32[]{:S(2)}) collective-permute-start(bf16[1024,4096]{1,0:T(8,128)(2,1)} %own.1), channel_id=1, source_target_pairs={{0,1},{1,0},{2,3},{3,2},{4,5},{5,4},{6,7},{7,6},{8,9},{9,8},{10,11... | collective-permute-start | bytes 25165832 | tf_op jit(solution)/shard_map/ppermute | solution.py:203
  3.3 37.9 %collective-permute-start.3 = (bf16[1024,768]{1,0:T(8,128)(2,1)S(1)}, bf16[1024,768]{1,0:T(8,128)(2,1)}, u32[]{:S(2)}, u32[]{:S(2)}) collective-permute-start(bf16[1024,768]{1,0:T(8,128)(2,1)S(1)} %get-tuple-element.52.refs_3_), channel_id=1, source_target_pairs={{0,4},{4,8},{8,12},{12,14},{14,10},{10,6},{6,2},{2,0},{1,5},{5,9},... | collective-permute-start | bytes 4718600 | tf_op jit(solution)/shard_map/ppermute | solution.py:183
  5.9 37.3 %collective-permute-start.5 = (bf16[1024,768]{1,0:T(8,128)(2,1)S(1)}, bf16[1024,768]{1,0:T(8,128)(2,1)}, u32[]{:S(2)}, u32[]{:S(2)}) collective-permute-start(bf16[1024,768]{1,0:T(8,128)(2,1)S(1)} %get-tuple-element.53.refs_4_), channel_id=1, source_target_pairs={{4,0},{8,4},{12,8},{14,12},{10,14},{6,10},{2,6},{0,2},{5,1},{9,5},... | collective-permute-start | bytes 4718600 | tf_op jit(solution)/shard_map/ppermute | solution.py:184
  5.9 91.5 %collective-permute-start = (bf16[1024,768]{1,0:T(8,128)(2,1)S(1)}, bf16[1024,768]{1,0:T(8,128)(2,1)}, u32[]{:S(2)}, u32[]{:S(2)}) collective-permute-start(bf16[1024,768]{1,0:T(8,128)(2,1)S(1)} %get-tuple-element.53.refs_4_), channel_id=1, source_target_pairs={{0,4},{4,8},{8,12},{12,14},{14,10},{10,6},{6,2},{2,0},{1,5},{5,9},... | collective-permute-start | bytes 4718600 | tf_op jit(solution)/shard_map/ppermute | solution.py:183
  7.9 89.5 %collective-permute-start.1 = (bf16[1024,768]{1,0:T(8,128)(2,1)S(1)}, bf16[1024,768]{1,0:T(8,128)(2,1)}, u32[]{:S(2)}, u32[]{:S(2)}) collective-permute-start(bf16[1024,768]{1,0:T(8,128)(2,1)S(1)} %get-tuple-element.52.refs_3_), channel_id=1, source_target_pairs={{4,0},{8,4},{12,8},{14,12},{10,14},{6,10},{2,6},{0,2},{5,1},{9,5},... | collective-permute-start | bytes 4718600 | tf_op jit(solution)/shard_map/ppermute | solution.py:184
  8.1 49.6 %copy-start.2 = (s32[64]{0:T(128)}, s32[64]{0:T(128)S(1)}, u32[]{:S(2)}) copy-start(s32[64]{0:T(128)S(1)} %get-tuple-element.51.side) | copy-start | bytes 772
  41.2 74.7 %collective-permute-start.4 = (bf16[1024,768]{1,0:T(8,128)(2,1)}, bf16[1024,768]{1,0:T(8,128)(2,1)}, u32[]{:S(2)}, u32[]{:S(2)}) collective-permute-start(bf16[1024,768]{1,0:T(8,128)(2,1)} %collective-permute-done.3.refs_5_), channel_id=1, source_target_pairs={{0,4},{4,8},{8,12},{12,14},{14,10},{10,6},{6,2},{2,0},{1,5},{5,9},... | collective-permute-start | bytes 4718600 | tf_op jit(solution)/shard_map/ppermute | solution.py:183
  43.2 72.7 %collective-permute-start.6 = (bf16[1024,768]{1,0:T(8,128)(2,1)}, bf16[1024,768]{1,0:T(8,128)(2,1)}, u32[]{:S(2)}, u32[]{:S(2)}) collective-permute-start(bf16[1024,768]{1,0:T(8,128)(2,1)} %collective-permute-done.5.refs_8_), channel_id=1, source_target_pairs={{4,0},{8,4},{12,8},{14,12},{10,14},{6,10},{2,6},{0,2},{5,1},{9,5},... | collective-permute-start | bytes 4718600 | tf_op jit(solution)/shard_map/ppermute | solution.py:184
  97.5 46.8 %collective-permute-start.10 = (bf16[1024,768]{1,0:T(8,128)(2,1)}, bf16[1024,768]{1,0:T(8,128)(2,1)S(1)}, u32[]{:S(2)}, u32[]{:S(2)}) collective-permute-start(bf16[1024,768]{1,0:T(8,128)(2,1)} %collective-permute-done.1.refs_7_), channel_id=1, source_target_pairs={{4,0},{8,4},{12,8},{14,12},{10,14},{6,10},{2,6},{0,2},{5,1},{9,5},... | collective-permute-start | bytes 4718600 | tf_op jit(solution)/shard_map/ppermute | solution.py:184
  99.4 42.8 %collective-permute-start.9 = (bf16[1024,768]{1,0:T(8,128)(2,1)}, bf16[1024,768]{1,0:T(8,128)(2,1)S(1)}, u32[]{:S(2)}, u32[]{:S(2)}) collective-permute-start(bf16[1024,768]{1,0:T(8,128)(2,1)} %collective-permute-done.refs_6_), channel_id=1, source_target_pairs={{0,4},{4,8},{8,12},{12,14},{14,10},{10,6},{6,2},{2,0},{1,5},{5,9},... | collective-permute-start | bytes 4718600 | tf_op jit(solution)/shard_map/ppermute | solution.py:183
  115.9 60.0 %collective-permute-start.7 = (bf16[1024,768]{1,0:T(8,128)(2,1)}, bf16[1024,768]{1,0:T(8,128)(2,1)S(1)}, u32[]{:S(2)}, u32[]{:S(2)}) collective-permute-start(bf16[1024,768]{1,0:T(8,128)(2,1)} %collective-permute-done.4.refs_2_), channel_id=1, source_target_pairs={{0,4},{4,8},{8,12},{12,14},{14,10},{10,6},{6,2},{2,0},{1,5},{5,9},... | collective-permute-start | bytes 4718600 | tf_op jit(solution)/shard_map/ppermute | solution.py:183
  117.9 60.0 %collective-permute-start.8 = (bf16[1024,768]{1,0:T(8,128)(2,1)}, bf16[1024,768]{1,0:T(8,128)(2,1)S(1)}, u32[]{:S(2)}, u32[]{:S(2)}) collective-permute-start(bf16[1024,768]{1,0:T(8,128)(2,1)} %collective-permute-done.6.refs_5_), channel_id=1, source_target_pairs={{4,0},{8,4},{12,8},{14,12},{10,14},{6,10},{2,6},{0,2},{5,1},{9,5},... | collective-permute-start | bytes 4718600 | tf_op jit(solution)/shard_map/ppermute | solution.py:184
  142.2 67.4 %collective-permute-start.13 = (bf16[1024,768]{1,0:T(8,128)(2,1)S(1)}, bf16[1024,768]{1,0:T(8,128)(2,1)S(1)}, u32[]{:S(2)}, u32[]{:S(2)}) collective-permute-start(bf16[1024,768]{1,0:T(8,128)(2,1)S(1)} %collective-permute-done.9.refs_3_), channel_id=1, source_target_pairs={{0,4},{4,8},{8,12},{12,14},{14,10},{10,6},{6,2},{2,0},{1,5},{5,9},... | collective-permute-start | bytes 4718600 | tf_op jit(solution)/shard_map/ppermute | solution.py:183
  144.3 67.4 %collective-permute-start.14 = (bf16[1024,768]{1,0:T(8,128)(2,1)S(1)}, bf16[1024,768]{1,0:T(8,128)(2,1)S(1)}, u32[]{:S(2)}, u32[]{:S(2)}) collective-permute-start(bf16[1024,768]{1,0:T(8,128)(2,1)S(1)} %collective-permute-done.10.refs_4_), channel_id=1, source_target_pairs={{4,0},{8,4},{12,8},{14,12},{10,14},{6,10},{2,6},{0,2},{5,1},{9,5},... | collective-permute-start | bytes 4718600 | tf_op jit(solution)/shard_map/ppermute | solution.py:184
  178.0 65.1 %collective-permute-start.11 = (bf16[1024,768]{1,0:T(8,128)(2,1)S(1)}, bf16[1024,768]{1,0:T(8,128)(2,1)S(1)}, u32[]{:S(2)}, u32[]{:S(2)}) collective-permute-start(bf16[1024,768]{1,0:T(8,128)(2,1)S(1)} %collective-permute-done.7.refs_2_), channel_id=1, source_target_pairs={{0,4},{4,8},{8,12},{12,14},{14,10},{10,6},{6,2},{2,0},{1,5},{5,9},... | collective-permute-start | bytes 4718600 | tf_op jit(solution)/shard_map/ppermute | solution.py:183
  179.5 65.1 %collective-permute-start.12 = (bf16[1024,768]{1,0:T(8,128)(2,1)S(1)}, bf16[1024,768]{1,0:T(8,128)(2,1)S(1)}, u32[]{:S(2)}, u32[]{:S(2)}) collective-permute-start(bf16[1024,768]{1,0:T(8,128)(2,1)S(1)} %collective-permute-done.8.refs_5_), channel_id=1, source_target_pairs={{4,0},{8,4},{12,8},{14,12},{10,14},{6,10},{2,6},{0,2},{5,1},{9,5},... | collective-permute-start | bytes 4718600 | tf_op jit(solution)/shard_map/ppermute | solution.py:184
  244.7 20.9 %copy-start.1 = (f32[1536]{0:T(1024)S(1)}, f32[1536]{0:T(1024)}, u32[]{:S(2)}) copy-start(f32[1536]{0:T(1024)} %param.9) | copy-start | bytes 18436
  253.6 3.6 %collective-permute-start.15 = (f32[1,1536]{1,0:T(1,128)S(1)}, f32[1,1536]{1,0:T(1,128)S(1)}, u32[]{:S(2)}, u32[]{:S(2)}) collective-permute-start(f32[1,1536]{1,0:T(1,128)S(1)} %get-tuple-element.47), channel_id=1, source_target_pairs={{0,2},{2,0},{4,6},{6,4},{8,10},{10,8},{12,14},{14,12},{1,3},{3,1},... | collective-permute-start | bytes 18440 | tf_op jit(solution)/shard_map/ppermute | solution.py:166
  257.2 3.7 %collective-permute-start.16 = (f32[1,1536]{1,0:T(1,128)S(1)}, f32[1,1536]{1,0:T(1,128)S(1)}, u32[]{:S(2)}, u32[]{:S(2)}) collective-permute-start(f32[1,1536]{1,0:T(1,128)S(1)} %add.145), channel_id=1, source_target_pairs={{0,4},{2,6},{4,0},{6,2},{8,12},{10,14},{12,8},{14,10},{1,5},{3,7},... | collective-permute-start | bytes 18440 | tf_op jit(solution)/shard_map/ppermute | solution.py:166
  261.0 4.6 %collective-permute-start.17 = (f32[1,1536]{1,0:T(1,128)S(1)}, f32[1,1536]{1,0:T(1,128)S(1)}, u32[]{:S(2)}, u32[]{:S(2)}) collective-permute-start(f32[1,1536]{1,0:T(1,128)S(1)} %add.146), channel_id=1, source_target_pairs={{0,8},{2,10},{4,12},{6,14},{8,0},{10,2},{12,4},{14,6},{1,9},{3,11}... | collective-permute-start | bytes 18440 | tf_op jit(solution)/shard_map/ppermute | solution.py:166

commit v5 on v4

--- a/solution.py
+++ b/solution.py
@@ -116,7 +116,8 @@
     )(jnp.stack(sources), here, at, *([sigma] * count), *flat, *extra)
 
 
-def finish_kernel(blocks, source, here, at, sigma, left, right, acc, mine, out, part):
+def finish_kernel(blocks, here, at, sigma, left, right, acc, mine, *refs):
+    out, part = refs[-2:]
     j = pl.program_id(0)
     for side, late in enumerate((left, right)):
 
@@ -133,29 +134,34 @@
             part[...] = jnp.sum(total, axis=0, keepdims=True)
 
 
-def finish(sigma, source, left, right, state, wanted, unit):
+def finish(coeff, source, left, right, state, wanted, unit, begin, out):
     acc, mine = state
     rows, cols = acc.shape
-    blocks = left.shape[1] // unit
+    width = left.shape[1]
+    blocks = width // unit
     here, at = found(wanted, source, rows // TILE)
-    cut = pl.BlockSpec((rows, unit), lambda j, *_: (0, j))
+    first, second = begin // unit, (cols // 2 + begin) // unit - blocks
+    cut = pl.BlockSpec((rows, unit), lambda j, *_: (0, j + jnp.where(j < blocks, first, second)))
+    extra = [] if out is None else [out]
     return pl.pallas_call(
         functools.partial(finish_kernel, blocks),
         grid_spec=pltpu.PrefetchScalarGridSpec(
-            num_scalar_prefetch=3,
+            num_scalar_prefetch=2,
             grid=(2 * blocks,),
-            in_specs=[pl.BlockSpec((rows, rows), lambda j, s, *_: (0, s[0]))]
+            in_specs=[pl.BlockSpec((rows, rows), lambda j, *_: (0, 0))]
             + sides(rows, unit, blocks)
-            + [cut, cut],
+            + [cut, cut]
+            + [pl.BlockSpec(memory_space=pl.ANY)] * len(extra),
             out_specs=[cut, pl.BlockSpec((1, unit), lambda j, *_: (0, j))],
         ),
         out_shape=[
             jax.ShapeDtypeStruct((rows, cols), jnp.bfloat16),
-            jax.ShapeDtypeStruct((1, cols), F32),
+            jax.ShapeDtypeStruct((1, 2 * width), F32),
         ],
+        input_output_aliases={} if out is None else {7: 0},
         compiler_params=pltpu.CompilerParams(vmem_limit_bytes=VMEM_LIMIT),
-        cost_estimate=pl.CostEstimate(flops=rows * cols, bytes_accessed=rows * cols, transcendentals=0),
-    )(source[None], here, at, sigma, left, right, acc, mine)
+        cost_estimate=pl.CostEstimate(flops=rows * width, bytes_accessed=rows * width, transcendentals=0),
+    )(here, at, coeff, left, right, acc, mine, *extra)
 
 
 def row_sum(value, n):
@@ -211,11 +217,17 @@
         fresh = [(sources[0], (al, ar)), (sources[1], (bl, br))]
     state = accumulate(sigma, [s for s, _ in ready], [p for _, p in ready], wanted, state, unit)
     al, br, state = lax.optimization_barrier((al, br, state))
-    al, br = ahead(al), back(br)
+    splits = [(0, half - unit), (half - unit, unit)] if unit < half else [(0, half)]
+    late = [(ahead(al[:, lo : lo + w]), back(br[:, lo : lo + w])) for lo, w in splits]
     state = accumulate(sigma, [s for s, _ in fresh], [p for _, p in fresh], wanted, state, unit)
-    al, br, state = lax.optimization_barrier((al, br, state))
     source = table[(place + n // 2) % n]
-    out, part = finish(sigma, source, al, br, state, wanted, unit)
+    coeff = lax.dynamic_slice_in_dim(sigma, source * rows, rows, axis=1)
+    out, parts = None, []
+    for (lo, w), (left, right) in zip(splits, late):
+
+        out, part = finish(coeff, source, left, right, state, wanted, unit, lo, out)
+        parts.append((part[:, :w], part[:, w:]))
+    part = jnp.concatenate([p for p, _ in parts] + [p for _, p in parts], axis=1)
     return out, dinv_diag + row_sum(part, n).reshape(cols)
 
 

time: 268 us -> 263 us (0.981)
  waiting for transfers between devices: 135 us -> 107 us
  local copies, waits for them, and re-layouts: 5.35 us -> 22.6 us
  starting transfers between devices: 20.1 us -> 23.6 us
    ppermute x7 -> x8, waiting for transfers between devices: 122 us -> 96.1 us  [body(): ahead = lambda x: lax.ppermute(x, 'row', fwd)]
    unnamed x10 -> x34, local copies, waits for them, and re-layouts: 0.03 us -> 11.4 us
    slice x0 -> x6, local copies, waits for them, and re-layouts: none -> 3.91 us  [the longest x2 1.98 us: body(): al[:, lo:lo + w]]
    ppermute x7 -> x8, starting transfers between devices: 12.5 us -> 16 us  [body(): ahead = lambda x: lax.ppermute(x, 'row', fwd)]
    ppermute x7 -> x8, waiting for transfers between devices: 5.76 us -> 3.96 us  [body(): back = lambda x: lax.ppermute(x, 'row', bwd)]
    pallas_call x1 -> x2, Pallas kernels: 8.94 us -> 10.3 us  [finish(): pl.pallas_call(functools.partial(finish_kernel, blocks), grid_spec=pltpu....]
  transfers between devices with their start and end apart: 18 -> 20, of which waited for: 11 -> 11; matrix products, arithmetic and copies ran while one was open for 4% -> 6% of each run, Pallas kernels for 30% -> 34%
where the time goes in v5:
time: 263 us; the launch traced here: 262 us
  waiting for transfers between devices  107 us (41%)
  Pallas kernels  91.7 us (35%)
  starting transfers between devices  23.6 us (9%)
  local copies, waits for them, and re-layouts  22.6 us (9%)
  between operations  10.7 us (4%)
  other arithmetic  5.38 us (2%)
    ppermute x8, waiting for transfers between devices, body(): ahead = lambda x: lax.ppermute(x, 'row', fwd)  96.1 us
    pallas_call x3, Pallas kernels, accumulate(): pl.pallas_call(functools.partial(accumulate_kernel, count, first, blocks)...  41.5 us
    pallas_call x1, Pallas kernels, reorder(): pl.pallas_call(reorder_kernel, grid_spec=pltpu.PrefetchScalarGridSpec(num...  40 us
    ppermute x8, starting transfers between devices, body(): ahead = lambda x: lax.ppermute(x, 'row', fwd)  16 us
    unnamed x34, local copies, waits for them, and re-layouts  11.4 us
    pallas_call x2, Pallas kernels, finish(): pl.pallas_call(functools.partial(finish_kernel, blocks), grid_spec=pltpu....  10.3 us
    ppermute x3, waiting for transfers between devices, row_sum(): lax.ppermute(value, 'row', [(i, i ^ step) for i in range(n)])  7.34 us
  transfers between devices with their start and end apart: 20, of which 11 were waited for; matrix products, arithmetic and copies ran while one was open for 6% of the time, Pallas kernels for 34%

profile of v5, /device:TPU:0, one launch (start us, length us, event | category | flops | bytes accessed | tf_op | source)
XLA Modules:
  0.0 261.5 jit_solution(2804035032880046479)
XLA Ops:
  1.2 2.1 fusion.3
  3.3 2.6 %collective-permute-start.3 = (bf16[1024,768]{1,0:T(8,128)(2,1)S(1)}, bf16[1024,768]{1,0:T(8,128)(2,1)}, u32[]{:S(2)}, u32[]{:S(2)}) collective-permute-start(bf16[1024,768]{1,0:T(8,128)(2,1)S(1)} %get-tuple-element.48.refs_3_), channel_id=1, source_target_pairs={{0,4},{4,8},{8,12},{12,14},{14,10},{10,6},{6,2},{2,0},{1,5},{5,9},... | collective-permute-start | bytes 4718600 | tf_op jit(solution)/shard_map/ppermute | solution.py:189
  5.9 2.0 collective-permute-start
  8.1 33.1 %collective-permute-done.3.refs_5_ = bf16[1024,768]{1,0:T(8,128)(2,1)} collective-permute-done((bf16[1024,768]{1,0:T(8,128)(2,1)S(1)}, bf16[1024,768]{1,0:T(8,128)(2,1)}, u32[]{:S(2)}, u32[]{:S(2)}) %collective-permute-start.3) | collective-permute-done | bytes 1572896 | tf_op jit(solution)/shard_map/ppermute | solution.py:189
  41.2 2.0 collective-permute-start.4
  45.5 40.0 %shard_map.77.refs_0_.refs_1_.refs_2_ = bf16[1024,8192]{1,0:T(8,128)(2,1)} custom-call(s32[64]{0:T(128)} %copy-done.14, s32[2,64]{1,0:T(2,128)} %reshape.148.at, bf16[1024,4096]{1,0:T(8,128)(2,1)} %own.1, bf16[1024,4096]{1,0:T(8,128)(2,1)} %collective-permute-done.2.other), custom_call_target="tpu_custom_call" | custom-call | bytes 4194304 | tf_op jit(solution)/shard_map/pallas_call | solution.py:29
  85.5 2.1 collective-permute-start.9
  102.5 16.3 %shard_map.78 = (f32[1024,1536]{1,0:T(8,128)S(1)}, bf16[1024,1536]{1,0:T(8,128)(2,1)S(1)}) custom-call(s32[3]{0:T(128)S(1)} %pad_add_fusion.3.source, s32[3,8]{1,0:T(4,128)S(1)} %add_convert_fusion.here, s32[3,8]{1,0:T(4,128)S(1)} %pad_add_fusion.at, bf16[1024,8192]{1,0:T(8,128)(2,1)} %shard_map.77.refs_0_.refs_1_.refs_2_, ...), custom_call_target="tpu_custom_call" | custom-call | flops 2359296 | bytes 786432 | tf_op jit(solution)/shard_map/pallas_call | solution.py:101
  118.8 2.1 collective-permute-start.7
  120.9 21.4 %collective-permute-done.9.refs_3_ = bf16[1024,768]{1,0:T(8,128)(2,1)} collective-permute-done((bf16[1024,768]{1,0:T(8,128)(2,1)}, bf16[1024,768]{1,0:T(8,128)(2,1)}, u32[]{:S(2)}, u32[]{:S(2)}) %collective-permute-start.9) | collective-permute-done | bytes 1572896 | tf_op jit(solution)/shard_map/ppermute | solution.py:189
  142.3 2.0 collective-permute-start.13
  145.8 12.7 %shard_map.79 = (f32[1024,1536]{1,0:T(8,128)S(1)}, bf16[1024,1536]{1,0:T(8,128)(2,1)S(1)}) custom-call(s32[2]{0:T(128)S(1)} %pad_add_fusion.4.source, s32[2,8]{1,0:T(2,128)S(1)} %add_convert_fusion.1.here, s32[2,8]{1,0:T(2,128)S(1)} %pad_add_fusion.1.at, ...), custom_call_target="tpu_custom_call", output_to_operand_aliasing={{0}: (9, {}), {1}: (10, {})} | custom-call | flops 1572864 | bytes 786432 | tf_op jit(solution)/shard_map/pallas_call | solution.py:101
  158.6 2.6 %copy-done = f32[1024,1536]{1,0:T(8,128)} copy-done((f32[1024,1536]{1,0:T(8,128)}, f32[1024,1536]{1,0:T(8,128)S(1)}, u32[]{:S(2)}) %copy-start) | copy-done | bytes 6291480
  161.2 14.7 %collective-permute-done.7.refs_2_ = bf16[1024,768]{1,0:T(8,128)(2,1)S(1)} collective-permute-done((bf16[1024,768]{1,0:T(8,128)(2,1)}, bf16[1024,768]{1,0:T(8,128)(2,1)S(1)}, u32[]{:S(2)}, u32[]{:S(2)}) %collective-permute-start.7) | collective-permute-done | bytes 1572896 | tf_op jit(solution)/shard_map/ppermute | solution.py:189
  175.9 2.1 collective-permute-done.8.refs_5_
  185.5 24.1 %collective-permute-done.13.refs_3_ = bf16[1024,768]{1,0:T(8,128)(2,1)S(1)} collective-permute-done((bf16[1024,768]{1,0:T(8,128)(2,1)}, bf16[1024,768]{1,0:T(8,128)(2,1)S(1)}, u32[]{:S(2)}, u32[]{:S(2)}) %collective-permute-start.13) | collective-permute-done | bytes 1572896 | tf_op jit(solution)/shard_map/ppermute | solution.py:189
  217.3 2.8 %copy-done.1 = f32[1024,1536]{1,0:T(8,128)S(1)} copy-done((f32[1024,1536]{1,0:T(8,128)S(1)}, f32[1024,1536]{1,0:T(8,128)}, u32[]{:S(2)}) %copy-start.1) | copy-done | bytes 6291480
  221.5 12.4 %shard_map.80 = (f32[1024,1536]{1,0:T(8,128)S(1)}, bf16[1024,1536]{1,0:T(8,128)(2,1)S(1)}) custom-call(s32[2]{0:T(128)S(1)} %pad_add_fusion.5.source, s32[2,8]{1,0:T(2,128)S(1)} %add_convert_fusion.2.here, s32[2,8]{1,0:T(2,128)S(1)} %pad_add_fusion.2.at, ...), custom_call_target="tpu_custom_call", output_to_operand_aliasing={{0}: (9, {}), {1}: (10, {})} | custom-call | flops 1572864 | bytes 786432 | tf_op jit(solution)/shard_map/pallas_call | solution.py:101
  234.2 6.2 %shard_map.81 = (bf16[1024,1536]{1,0:T(8,128)(2,1)}, f32[1,1024]{1,0:T(1,128)S(1)}) custom-call(s32[8]{0:T(128)S(1)} %get-tuple-element.68.here, s32[8]{0:T(128)S(1)} %get-tuple-element.60.at, bf16[1024,1024]{1,0:T(8,128)(2,1)S(1)} %constant_dynamic-slice_fusion.sigma, bf16[1024,512]{1,0:T(8,128)(2,1)} %collective-permute-done.15.left, ...), custom_call_target="tpu_custom_call" | custom-call | flops 524288 | bytes 524288 | tf_op jit(solution)/shard_map/pallas_call | solution.py:146
  240.4 2.8 %collective-permute-done.11.left = bf16[1024,256]{1,0:T(8,128)(2,1)} collective-permute-done((bf16[1024,256]{1,0:T(8,128)(2,1)}, bf16[1024,256]{1,0:T(8,128)(2,1)}, u32[]{:S(2)}, u32[]{:S(2)}) %collective-permute-start.11) | collective-permute-done | bytes 524320 | tf_op jit(solution)/shard_map/ppermute | solution.py:189
  244.8 4.1 %shard_map.82 = (bf16[1024,1536]{1,0:T(8,128)(2,1)}, f32[1,512]{1,0:T(1,128)S(1)}) custom-call(s32[8]{0:T(128)S(1)} %get-tuple-element.68.here, s32[8]{0:T(128)S(1)} %get-tuple-element.60.at, bf16[1024,1024]{1,0:T(8,128)(2,1)S(1)} %constant_dynamic-slice_fusion.sigma, ...), custom_call_target="tpu_custom_call", output_to_operand_aliasing={{0}: (7, {})} | custom-call | flops 262144 | bytes 262144 | tf_op jit(solution)/shard_map/pallas_call | solution.py:146
  249.2 3.3 %collective-permute-done.17 = f32[1,1536]{1,0:T(1,128)S(1)} collective-permute-done((f32[1,1536]{1,0:T(1,128)S(1)}, f32[1,1536]{1,0:T(1,128)S(1)}, u32[]{:S(2)}, u32[]{:S(2)}) %collective-permute-start.17) | collective-permute-done | bytes 6176 | tf_op jit(solution)/shard_map/ppermute | solution.py:172
  254.2 2.1 collective-permute-done.18
  256.3 2.7 %collective-permute-start.19 = (f32[1,1536]{1,0:T(1,128)S(1)}, f32[1,1536]{1,0:T(1,128)S(1)}, u32[]{:S(2)}, u32[]{:S(2)}) collective-permute-start(f32[1,1536]{1,0:T(1,128)S(1)} %add.150), channel_id=1, source_target_pairs={{0,8},{2,10},{4,12},{6,14},{8,0},{10,2},{12,4},{14,6},{1,9},{3,11}... | collective-permute-start | bytes 18440 | tf_op jit(solution)/shard_map/ppermute | solution.py:172
  (94 shorter events, 32.5 us)
Async XLA Ops:
  0.6 44.9 %collective-permute-start.2 = (bf16[1024,4096]{1,0:T(8,128)(2,1)}, bf16[1024,4096]{1,0:T(8,128)(2,1)}, u32[]{:S(2)}, u32[]{:S(2)}) collective-permute-start(bf16[1024,4096]{1,0:T(8,128)(2,1)} %own.1), channel_id=1, source_target_pairs={{0,1},{1,0},{2,3},{3,2},{4,5},{5,4},{6,7},{7,6},{8,9},{9,8},{10,11... | collective-permute-start | bytes 25165832 | tf_op jit(solution)/shard_map/ppermute | solution.py:209
  3.2 82.2 %copy-start.6 = (bf16[1024,768]{1,0:T(8,128)(2,1)}, bf16[1024,768]{1,0:T(8,128)(2,1)S(1)}, u32[]{:S(2)}) copy-start(bf16[1024,768]{1,0:T(8,128)(2,1)S(1)} %get-tuple-element.48.refs_3_) | copy-start | bytes 4718596
  3.3 82.2 %copy-start.8 = (bf16[1024,768]{1,0:T(8,128)(2,1)}, bf16[1024,768]{1,0:T(8,128)(2,1)S(1)}, u32[]{:S(2)}) copy-start(bf16[1024,768]{1,0:T(8,128)(2,1)S(1)} %get-tuple-element.49.refs_4_) | copy-start | bytes 4718596
  3.3 37.9 %collective-permute-start.3 = (bf16[1024,768]{1,0:T(8,128)(2,1)S(1)}, bf16[1024,768]{1,0:T(8,128)(2,1)}, u32[]{:S(2)}, u32[]{:S(2)}) collective-permute-start(bf16[1024,768]{1,0:T(8,128)(2,1)S(1)} %get-tuple-element.48.refs_3_), channel_id=1, source_target_pairs={{0,4},{4,8},{8,12},{12,14},{14,10},{10,6},{6,2},{2,0},{1,5},{5,9},... | collective-permute-start | bytes 4718600 | tf_op jit(solution)/shard_map/ppermute | solution.py:189
  5.9 37.3 %collective-permute-start.5 = (bf16[1024,768]{1,0:T(8,128)(2,1)S(1)}, bf16[1024,768]{1,0:T(8,128)(2,1)}, u32[]{:S(2)}, u32[]{:S(2)}) collective-permute-start(bf16[1024,768]{1,0:T(8,128)(2,1)S(1)} %get-tuple-element.49.refs_4_), channel_id=1, source_target_pairs={{4,0},{8,4},{12,8},{14,12},{10,14},{6,10},{2,6},{0,2},{5,1},{9,5},... | collective-permute-start | bytes 4718600 | tf_op jit(solution)/shard_map/ppermute | solution.py:190
  5.9 79.6 %collective-permute-start = (bf16[1024,768]{1,0:T(8,128)(2,1)S(1)}, bf16[1024,768]{1,0:T(8,128)(2,1)}, u32[]{:S(2)}, u32[]{:S(2)}) collective-permute-start(bf16[1024,768]{1,0:T(8,128)(2,1)S(1)} %get-tuple-element.49.refs_4_), channel_id=1, source_target_pairs={{0,4},{4,8},{8,12},{12,14},{14,10},{10,6},{6,2},{2,0},{1,5},{5,9},... | collective-permute-start | bytes 4718600 | tf_op jit(solution)/shard_map/ppermute | solution.py:189
  7.9 77.6 %collective-permute-start.1 = (bf16[1024,768]{1,0:T(8,128)(2,1)S(1)}, bf16[1024,768]{1,0:T(8,128)(2,1)}, u32[]{:S(2)}, u32[]{:S(2)}) collective-permute-start(bf16[1024,768]{1,0:T(8,128)(2,1)S(1)} %get-tuple-element.48.refs_3_), channel_id=1, source_target_pairs={{4,0},{8,4},{12,8},{14,12},{10,14},{6,10},{2,6},{0,2},{5,1},{9,5},... | collective-permute-start | bytes 4718600 | tf_op jit(solution)/shard_map/ppermute | solution.py:190
  41.2 77.6 %collective-permute-start.4 = (bf16[1024,768]{1,0:T(8,128)(2,1)}, bf16[1024,768]{1,0:T(8,128)(2,1)}, u32[]{:S(2)}, u32[]{:S(2)}) collective-permute-start(bf16[1024,768]{1,0:T(8,128)(2,1)} %collective-permute-done.3.refs_5_), channel_id=1, source_target_pairs={{0,4},{4,8},{8,12},{12,14},{14,10},{10,6},{6,2},{2,0},{1,5},{5,9},... | collective-permute-start | bytes 4718600 | tf_op jit(solution)/shard_map/ppermute | solution.py:189
  43.2 75.6 %collective-permute-start.6 = (bf16[1024,768]{1,0:T(8,128)(2,1)}, bf16[1024,768]{1,0:T(8,128)(2,1)}, u32[]{:S(2)}, u32[]{:S(2)}) collective-permute-start(bf16[1024,768]{1,0:T(8,128)(2,1)} %collective-permute-done.5.refs_8_), channel_id=1, source_target_pairs={{4,0},{8,4},{12,8},{14,12},{10,14},{6,10},{2,6},{0,2},{5,1},{9,5},... | collective-permute-start | bytes 4718600 | tf_op jit(solution)/shard_map/ppermute | solution.py:190
  45.5 42.1 %copy-start.16 = (s32[8]{0:T(128)S(1)}, s32[8]{0:T(128)}, u32[]{:S(2)}) copy-start(s32[8]{0:T(128)} %constant.123.clone) | copy-start | bytes 100
  45.5 47.2 %copy-start.12 = (s32[8]{0:T(128)S(1)}, s32[8]{0:T(128)}, u32[]{:S(2)}) copy-start(s32[8]{0:T(128)} %constant.122.clone) | copy-start | bytes 100
  85.5 56.8 %collective-permute-start.9 = (bf16[1024,768]{1,0:T(8,128)(2,1)}, bf16[1024,768]{1,0:T(8,128)(2,1)}, u32[]{:S(2)}, u32[]{:S(2)}) collective-permute-start(bf16[1024,768]{1,0:T(8,128)(2,1)} %collective-permute-done.refs_6_), channel_id=1, source_target_pairs={{0,4},{4,8},{8,12},{12,14},{14,10},{10,6},{6,2},{2,0},{1,5},{5,9},... | collective-permute-start | bytes 4718600 | tf_op jit(solution)/shard_map/ppermute | solution.py:189
  98.2 46.2 %collective-permute-start.10 = (bf16[1024,768]{1,0:T(8,128)(2,1)}, bf16[1024,768]{1,0:T(8,128)(2,1)}, u32[]{:S(2)}, u32[]{:S(2)}) collective-permute-start(bf16[1024,768]{1,0:T(8,128)(2,1)} %collective-permute-done.1.refs_7_), channel_id=1, source_target_pairs={{4,0},{8,4},{12,8},{14,12},{10,14},{6,10},{2,6},{0,2},{5,1},{9,5},... | collective-permute-start | bytes 4718600 | tf_op jit(solution)/shard_map/ppermute | solution.py:190
  118.8 57.1 %collective-permute-start.7 = (bf16[1024,768]{1,0:T(8,128)(2,1)}, bf16[1024,768]{1,0:T(8,128)(2,1)S(1)}, u32[]{:S(2)}, u32[]{:S(2)}) collective-permute-start(bf16[1024,768]{1,0:T(8,128)(2,1)} %collective-permute-done.4.refs_2_), channel_id=1, source_target_pairs={{0,4},{4,8},{8,12},{12,14},{14,10},{10,6},{6,2},{2,0},{1,5},{5,9},... | collective-permute-start | bytes 4718600 | tf_op jit(solution)/shard_map/ppermute | solution.py:189
  120.9 57.1 %collective-permute-start.8 = (bf16[1024,768]{1,0:T(8,128)(2,1)}, bf16[1024,768]{1,0:T(8,128)(2,1)S(1)}, u32[]{:S(2)}, u32[]{:S(2)}) collective-permute-start(bf16[1024,768]{1,0:T(8,128)(2,1)} %collective-permute-done.6.refs_5_), channel_id=1, source_target_pairs={{4,0},{8,4},{12,8},{14,12},{10,14},{6,10},{2,6},{0,2},{5,1},{9,5},... | collective-permute-start | bytes 4718600 | tf_op jit(solution)/shard_map/ppermute | solution.py:190
  142.3 67.3 %collective-permute-start.13 = (bf16[1024,768]{1,0:T(8,128)(2,1)}, bf16[1024,768]{1,0:T(8,128)(2,1)S(1)}, u32[]{:S(2)}, u32[]{:S(2)}) collective-permute-start(bf16[1024,768]{1,0:T(8,128)(2,1)} %collective-permute-done.9.refs_3_), channel_id=1, source_target_pairs={{0,4},{4,8},{8,12},{12,14},{14,10},{10,6},{6,2},{2,0},{1,5},{5,9},... | collective-permute-start | bytes 4718600 | tf_op jit(solution)/shard_map/ppermute | solution.py:189
  144.4 72.4 %collective-permute-start.14 = (bf16[1024,768]{1,0:T(8,128)(2,1)}, bf16[1024,768]{1,0:T(8,128)(2,1)}, u32[]{:S(2)}, u32[]{:S(2)}) collective-permute-start(bf16[1024,768]{1,0:T(8,128)(2,1)} %collective-permute-done.10.refs_4_), channel_id=1, source_target_pairs={{4,0},{8,4},{12,8},{14,12},{10,14},{6,10},{2,6},{0,2},{5,1},{9,5},... | collective-permute-start | bytes 4718600 | tf_op jit(solution)/shard_map/ppermute | solution.py:190
  179.1 54.9 %collective-permute-start.15 = (bf16[1024,512]{1,0:T(8,128)(2,1)}, bf16[1024,512]{1,0:T(8,128)(2,1)}, u32[]{:S(2)}, u32[]{:S(2)}) collective-permute-start(bf16[1024,512]{1,0:T(8,128)(2,1)} %slice.34), channel_id=1, source_target_pairs={{0,4},{4,8},{8,12},{12,14},{14,10},{10,6},{6,2},{2,0},{1,5},{5,9},... | collective-permute-start | bytes 3145736 | tf_op jit(solution)/shard_map/ppermute | solution.py:189
  181.8 52.5 %collective-permute-start.16 = (bf16[1024,512]{1,0:T(8,128)(2,1)}, bf16[1024,512]{1,0:T(8,128)(2,1)}, u32[]{:S(2)}, u32[]{:S(2)}) collective-permute-start(bf16[1024,512]{1,0:T(8,128)(2,1)} %slice.35), channel_id=1, source_target_pairs={{4,0},{8,4},{12,8},{14,12},{10,14},{6,10},{2,6},{0,2},{5,1},{9,5},... | collective-permute-start | bytes 3145736 | tf_op jit(solution)/shard_map/ppermute | solution.py:190
  183.9 59.3 %collective-permute-start.11 = (bf16[1024,256]{1,0:T(8,128)(2,1)}, bf16[1024,256]{1,0:T(8,128)(2,1)}, u32[]{:S(2)}, u32[]{:S(2)}) collective-permute-start(bf16[1024,256]{1,0:T(8,128)(2,1)} %slice.32), channel_id=1, source_target_pairs={{0,4},{4,8},{8,12},{12,14},{14,10},{10,6},{6,2},{2,0},{1,5},{5,9},... | collective-permute-start | bytes 1572872 | tf_op jit(solution)/shard_map/ppermute | solution.py:189
  210.8 34.0 %collective-permute-start.12 = (bf16[1024,256]{1,0:T(8,128)(2,1)}, bf16[1024,256]{1,0:T(8,128)(2,1)}, u32[]{:S(2)}, u32[]{:S(2)}) collective-permute-start(bf16[1024,256]{1,0:T(8,128)(2,1)} %slice.33), channel_id=1, source_target_pairs={{4,0},{8,4},{12,8},{14,12},{10,14},{6,10},{2,6},{0,2},{5,1},{9,5},... | collective-permute-start | bytes 1572872 | tf_op jit(solution)/shard_map/ppermute | solution.py:190
  248.9 3.7 %collective-permute-start.17 = (f32[1,1536]{1,0:T(1,128)S(1)}, f32[1,1536]{1,0:T(1,128)S(1)}, u32[]{:S(2)}, u32[]{:S(2)}) collective-permute-start(f32[1,1536]{1,0:T(1,128)S(1)} %pad_maximum_fusion), channel_id=1, source_target_pairs={{0,2},{2,0},{4,6},{6,4},{8,10},{10,8},{12,14},{14,12},{1,3},{3,1},... | collective-permute-start | bytes 18440 | tf_op jit(solution)/shard_map/ppermute | solution.py:172
  252.6 3.7 %collective-permute-start.18 = (f32[1,1536]{1,0:T(1,128)S(1)}, f32[1,1536]{1,0:T(1,128)S(1)}, u32[]{:S(2)}, u32[]{:S(2)}) collective-permute-start(f32[1,1536]{1,0:T(1,128)S(1)} %fusion.7), channel_id=1, source_target_pairs={{0,4},{2,6},{4,0},{6,2},{8,12},{10,14},{12,8},{14,10},{1,5},{3,7},... | collective-permute-start | bytes 18440 | tf_op jit(solution)/shard_map/ppermute | solution.py:172
  256.3 4.6 %collective-permute-start.19 = (f32[1,1536]{1,0:T(1,128)S(1)}, f32[1,1536]{1,0:T(1,128)S(1)}, u32[]{:S(2)}, u32[]{:S(2)}) collective-permute-start(f32[1,1536]{1,0:T(1,128)S(1)} %add.150), channel_id=1, source_target_pairs={{0,8},{2,10},{4,12},{6,14},{8,0},{10,2},{12,4},{14,6},{1,9},{3,11}... | collective-permute-start | bytes 18440 | tf_op jit(solution)/shard_map/ppermute | solution.py:172
  (13 other events, 87.7 us)

commit v6 on v5

--- a/solution.py
+++ b/solution.py
@@ -70,8 +70,9 @@
                 rows = slice(t * TILE, (t + 1) * TILE)
                 value = None if first else mine_in[rows, :]
                 for p in range(count):
-                    got = pieces[2 * p + side][tile_rows(at[p, t]), :]
-                    value = got if value is None else jnp.where(here[p, t] != 0, got, value)
+                    q = 2 * p + side
+                    got = pieces[q][tile_rows(at[q, t]), :]
+                    value = got if value is None else jnp.where(here[q, t] != 0, got, value)
                 mine[rows, :] = value
 
 
@@ -83,6 +84,7 @@
 
 def accumulate(sigma, sources, pieces, wanted, state, unit):
     count = len(sources)
+    sources = [x for pair in sources for x in pair]
     first = state is None
     rows, half = pieces[0][0].shape
     blocks = half // unit
@@ -92,7 +94,7 @@
     at = jnp.stack([m[1] for m in marks])
     cut = pl.BlockSpec((rows, unit), lambda j, *_: (0, j))
     sigma_specs = [
-        pl.BlockSpec((rows, rows), functools.partial(lambda p, j, s, *_: (0, s[p]), p))
+        pl.BlockSpec((rows, rows), functools.partial(lambda p, j, s, *_: (0, s[2 * p + j // blocks]), p))
         for p in range(count)
     ]
     flat = [x for pair in pieces for x in pair]
@@ -197,7 +199,7 @@
     own = (panel[:, :half], panel[:, half:])
     (al, ar), (bl, br) = own, own
     state = None
-    ready = [(me, own)]
+    ready = [((me, me), own)]
     sigma = None
     for hop in range(1, n // 2):
         if hop > 2:
@@ -214,18 +216,28 @@
         sources = [table[(place - hop) % n], table[(place + hop) % n]]
         if hop > 1:
             ready += fresh
-        fresh = [(sources[0], (al, ar)), (sources[1], (bl, br))]
+        fresh = [((sources[0],) * 2, (al, ar)), ((sources[1],) * 2, (bl, br))]
     state = accumulate(sigma, [s for s, _ in ready], [p for _, p in ready], wanted, state, unit)
     al, br, state = lax.optimization_barrier((al, br, state))
-    splits = [(0, half - unit), (half - unit, unit)] if unit < half else [(0, half)]
-    late = [(ahead(al[:, lo : lo + w]), back(br[:, lo : lo + w])) for lo, w in splits]
-    state = accumulate(sigma, [s for s, _ in fresh], [p for _, p in fresh], wanted, state, unit)
+    if unit < half:
+        wide, thin = half - unit, unit // 2 if unit % (2 * TILE) == 0 else unit
+        splits = [(0, wide, unit)] + [(lo, thin, thin) for lo in range(wide, half, thin)]
+    else:
+        splits = [(0, half, unit)]
+    def send(lo, width):
+        return ahead(al[:, lo : lo + width]), back(br[:, lo : lo + width])
+
+    late = [send(*splits[0][:2])]
+    (from_a, (left, far_right)), (from_b, (far_left, right)) = fresh
+    state = accumulate(sigma, [(from_a[0], from_b[0])], [(left, right)], wanted, state, unit)
+    al, br, state = lax.optimization_barrier((al, br, state))
+    late += [send(lo, w) for lo, w, _ in splits[1:]]
+    state = accumulate(sigma, [(from_b[0], from_a[0])], [(far_left, far_right)], wanted, state, unit)
     source = table[(place + n // 2) % n]
     coeff = lax.dynamic_slice_in_dim(sigma, source * rows, rows, axis=1)
     out, parts = None, []
-    for (lo, w), (left, right) in zip(splits, late):
-
-        out, part = finish(coeff, source, left, right, state, wanted, unit, lo, out)
+    for (lo, w, step), (left, right) in zip(splits, late):
+        out, part = finish(coeff, source, left, right, state, wanted, step, lo, out)
         parts.append((part[:, :w], part[:, w:]))
     part = jnp.concatenate([p for p, _ in parts] + [p for _, p in parts], axis=1)
     return out, dinv_diag + row_sum(part, n).reshape(cols)

time: 263 us -> 262 us (level)
  waiting for transfers between devices: 107 us -> 96.6 us
  Pallas kernels: 91.7 us -> 98.6 us
    ppermute x8 -> x9, waiting for transfers between devices: 96.1 us -> 53.4 us  [body(): ahead = lambda x: lax.ppermute(x, 'row', fwd)]
    ppermute x8 -> x9, waiting for transfers between devices: 3.96 us -> 35.8 us  [body(): back = lambda x: lax.ppermute(x, 'row', bwd)]
    pallas_call x3 -> x4, Pallas kernels: 41.5 us -> 46.5 us  [accumulate(): pl.pallas_call(functools.partial(accumulate_kernel, count, first, blocks)...]
    another operation x0 -> x3, local copies, waits for them, and re-layouts: none -> 2.79 us  [the longest x1 2.73 us: accumulate(): jnp.stack(sources)]
    pallas_call x2 -> x3, Pallas kernels: 10.3 us -> 12.2 us  [finish(): pl.pallas_call(functools.partial(finish_kernel, blocks), grid_spec=pltpu....]
    ppermute x8 -> x9, starting transfers between devices: 16 us -> 16.2 us  [body(): ahead = lambda x: lax.ppermute(x, 'row', fwd)]
    unnamed x34 -> x35, local copies, waits for them, and re-layouts: 11.4 us -> 11.2 us
  transfers between devices with their start and end apart: 20 -> 22, of which waited for: 11 -> 11; matrix products, arithmetic and copies ran while one was open for 6% -> 6% of each run, Pallas kernels for 34% -> 37%
where the time goes in v6:
time: 262 us; the launch traced here: 260 us
  Pallas kernels  98.6 us (38%)
  waiting for transfers between devices  96.6 us (37%)
  starting transfers between devices  25.8 us (10%)
  local copies, waits for them, and re-layouts  23.5 us (9%)
  between operations  10.7 us (4%)
  other arithmetic  5.25 us (2%)
    ppermute x9, waiting for transfers between devices, body(): ahead = lambda x: lax.ppermute(x, 'row', fwd)  53.4 us
    pallas_call x4, Pallas kernels, accumulate(): pl.pallas_call(functools.partial(accumulate_kernel, count, first, blocks)...  46.5 us
    pallas_call x1, Pallas kernels, reorder(): pl.pallas_call(reorder_kernel, grid_spec=pltpu.PrefetchScalarGridSpec(num...  39.9 us
    ppermute x9, waiting for transfers between devices, body(): back = lambda x: lax.ppermute(x, 'row', bwd)  35.8 us
    ppermute x9, starting transfers between devices, body(): ahead = lambda x: lax.ppermute(x, 'row', fwd)  16.2 us
    pallas_call x3, Pallas kernels, finish(): pl.pallas_call(functools.partial(finish_kernel, blocks), grid_spec=pltpu....  12.2 us
    unnamed x35, local copies, waits for them, and re-layouts  11.2 us
    ppermute x3, waiting for transfers between devices, row_sum(): lax.ppermute(value, 'row', [(i, i ^ step) for i in range(n)])  7.33 us
  transfers between devices with their start and end apart: 22, of which 11 were waited for; matrix products, arithmetic and copies ran while one was open for 6% of the time, Pallas kernels for 37%

profile of v6, /device:TPU:0, one launch (start us, length us, event | category | flops | bytes accessed | tf_op | source)
XLA Modules:
  0.0 260.3 jit_solution(12628560840983752413)
XLA Ops:
  1.2 2.1 fusion.5
  3.3 2.6 %collective-permute-start.3 = (bf16[1024,768]{1,0:T(8,128)(2,1)S(1)}, bf16[1024,768]{1,0:T(8,128)(2,1)}, u32[]{:S(2)}, u32[]{:S(2)}) collective-permute-start(bf16[1024,768]{1,0:T(8,128)(2,1)S(1)} %get-tuple-element.64.refs_3_), channel_id=1, source_target_pairs={{0,4},{4,8},{8,12},{12,14},{14,10},{10,6},{6,2},{2,0},{1,5},{5,9},... | collective-permute-start | bytes 4718600 | tf_op jit(solution)/shard_map/ppermute | solution.py:191
  8.0 33.1 %collective-permute-done.3.refs_5_ = bf16[1024,768]{1,0:T(8,128)(2,1)} collective-permute-done((bf16[1024,768]{1,0:T(8,128)(2,1)S(1)}, bf16[1024,768]{1,0:T(8,128)(2,1)}, u32[]{:S(2)}, u32[]{:S(2)}) %collective-permute-start.3) | collective-permute-done | bytes 1572896 | tf_op jit(solution)/shard_map/ppermute | solution.py:191
  45.5 39.9 %shard_map.77.refs_0_.refs_1_.refs_2_ = bf16[1024,8192]{1,0:T(8,128)(2,1)} custom-call(s32[64]{0:T(128)} %copy-done.12, s32[2,64]{1,0:T(2,128)} %reshape.150.at, bf16[1024,4096]{1,0:T(8,128)(2,1)} %own.1, bf16[1024,4096]{1,0:T(8,128)(2,1)} %collective-permute-done.2.other), custom_call_target="tpu_custom_call" | custom-call | bytes 4194304 | tf_op jit(solution)/shard_map/pallas_call | solution.py:29
  98.2 2.7 %stack.124.source = s32[6]{0:T(128)S(1)} concatenate(s32[1]{0:T(128)} %bitcast.5, s32[1]{0:T(128)} %bitcast.5, s32[1]{0:T(128)} %get-tuple-element.93, s32[1]{0:T(128)} %get-tuple-element.93, s32[1]{0:T(128)} %get-tuple-element.92, s32[1]{0:T(128)} %get-tuple-element.92), dimensions={0} | concatenate | bytes 48 | tf_op jit(solution)/shard_map/stack | solution.py:118
  103.8 16.4 %shard_map.78 = (f32[1024,1536]{1,0:T(8,128)S(1)}, bf16[1024,1536]{1,0:T(8,128)(2,1)S(1)}) custom-call(s32[6]{0:T(128)S(1)} %stack.124.source, s32[6,8]{1,0:T(8,128)S(1)} %stack.129.here, s32[6,8]{1,0:T(8,128)S(1)} %stack.133.at, bf16[1024,8192]{1,0:T(8,128)(2,1)} %shard_map.77.refs_0_.refs_1_.refs_2_, bf16[1024,8192]{1,0:T(8,128)(2,1)} %shard_map.77.refs_0_.refs_1_.refs_2_, ...), custom_call_target="tpu_custom_call" | custom-call | flops 2359296 | bytes 786432 | tf_op jit(solution)/shard_map/pallas_call | solution.py:103
  120.2 2.1 collective-permute-start.7
  122.3 22.1 %collective-permute-done.10.refs_4_ = bf16[1024,768]{1,0:T(8,128)(2,1)} collective-permute-done((bf16[1024,768]{1,0:T(8,128)(2,1)}, bf16[1024,768]{1,0:T(8,128)(2,1)}, u32[]{:S(2)}, u32[]{:S(2)}) %collective-permute-start.10) | collective-permute-done | bytes 1572896 | tf_op jit(solution)/shard_map/ppermute | solution.py:192
  147.9 12.8 %shard_map.79 = (f32[1024,1536]{1,0:T(8,128)S(1)}, bf16[1024,1536]{1,0:T(8,128)(2,1)S(1)}) custom-call(s32[4]{0:T(128)S(1)} %pad_add_fusion.5.source, s32[4,8]{1,0:T(4,128)S(1)} %add_convert_fusion.here, s32[4,8]{1,0:T(4,128)S(1)} %pad_add_fusion.at, ...), custom_call_target="tpu_custom_call", output_to_operand_aliasing={{0}: (9, {}), {1}: (10, {})} | custom-call | flops 1572864 | bytes 786432 | tf_op jit(solution)/shard_map/pallas_call | solution.py:103
  160.7 2.7 %copy-done = f32[1024,1536]{1,0:T(8,128)} copy-done((f32[1024,1536]{1,0:T(8,128)}, f32[1024,1536]{1,0:T(8,128)S(1)}, u32[]{:S(2)}) %copy-start) | copy-done | bytes 6291480
  163.4 12.5 %collective-permute-done.7.refs_1_ = bf16[1024,768]{1,0:T(8,128)(2,1)S(1)} collective-permute-done((bf16[1024,768]{1,0:T(8,128)(2,1)}, bf16[1024,768]{1,0:T(8,128)(2,1)S(1)}, u32[]{:S(2)}, u32[]{:S(2)}) %collective-permute-start.7) | collective-permute-done | bytes 1572896 | tf_op jit(solution)/shard_map/ppermute | solution.py:191
  175.9 2.1 collective-permute-done.8.refs_2_
  185.6 2.8 %copy-done.1 = f32[1024,1536]{1,0:T(8,128)S(1)} copy-done((f32[1024,1536]{1,0:T(8,128)S(1)}, f32[1024,1536]{1,0:T(8,128)}, u32[]{:S(2)}) %copy-start.1) | copy-done | bytes 6291480
  191.2 8.5 %shard_map.80 = (f32[1024,1536]{1,0:T(8,128)S(1)}, bf16[1024,1536]{1,0:T(8,128)(2,1)S(1)}) custom-call(s32[2]{0:T(128)S(1)} %pad_add_fusion.6.source, s32[2,8]{1,0:T(2,128)S(1)} %get-tuple-element.73.here, s32[2,8]{1,0:T(2,128)S(1)} %get-tuple-element.96.at, ...), custom_call_target="tpu_custom_call", output_to_operand_aliasing={{0}: (6, {}), {1}: (7, {})} | custom-call | flops 786432 | bytes 786432 | tf_op jit(solution)/shard_map/pallas_call | solution.py:103
  201.4 10.4 %collective-permute-done.13.refs_1_ = bf16[1024,768]{1,0:T(8,128)(2,1)} collective-permute-done((bf16[1024,768]{1,0:T(8,128)(2,1)}, bf16[1024,768]{1,0:T(8,128)(2,1)}, u32[]{:S(2)}, u32[]{:S(2)}) %collective-permute-start.13) | collective-permute-done | bytes 1572896 | tf_op jit(solution)/shard_map/ppermute | solution.py:192
  213.6 2.1 collective-permute-start.11
  215.6 8.8 %shard_map.81 = (f32[1024,1536]{1,0:T(8,128)S(1)}, bf16[1024,1536]{1,0:T(8,128)(2,1)S(1)}) custom-call(s32[2]{0:T(128)S(1)} %pad_add_fusion.7.source, s32[2,8]{1,0:T(2,128)S(1)} %get-tuple-element.72.here, s32[2,8]{1,0:T(2,128)S(1)} %get-tuple-element.97.at, ...), custom_call_target="tpu_custom_call", output_to_operand_aliasing={{0}: (6, {}), {1}: (7, {})} | custom-call | flops 786432 | bytes 786432 | tf_op jit(solution)/shard_map/pallas_call | solution.py:103
  224.4 7.8 %collective-permute-done.17.left = bf16[1024,512]{1,0:T(8,128)(2,1)} collective-permute-done((bf16[1024,512]{1,0:T(8,128)(2,1)}, bf16[1024,512]{1,0:T(8,128)(2,1)}, u32[]{:S(2)}, u32[]{:S(2)}) %collective-permute-start.17) | collective-permute-done | bytes 1048608 | tf_op jit(solution)/shard_map/ppermute | solution.py:191
  234.2 6.2 %shard_map.82 = (bf16[1024,1536]{1,0:T(8,128)(2,1)}, f32[1,1024]{1,0:T(1,128)S(1)}) custom-call(s32[8]{0:T(128)S(1)} %get-tuple-element.88.here, s32[8]{0:T(128)S(1)} %get-tuple-element.80.at, bf16[1024,1024]{1,0:T(8,128)(2,1)S(1)} %constant_dynamic-slice_fusion.sigma, bf16[1024,512]{1,0:T(8,128)(2,1)} %collective-permute-done.17.left, ...), custom_call_target="tpu_custom_call" | custom-call | flops 524288 | bytes 524288 | tf_op jit(solution)/shard_map/pallas_call | solution.py:148
  240.4 3.0 %shard_map.83 = (bf16[1024,1536]{1,0:T(8,128)(2,1)}, f32[1,256]{1,0:T(1,128)S(1)}) custom-call(s32[8]{0:T(128)S(1)} %get-tuple-element.88.here, s32[8]{0:T(128)S(1)} %get-tuple-element.80.at, bf16[1024,1024]{1,0:T(8,128)(2,1)S(1)} %constant_dynamic-slice_fusion.sigma, ...), custom_call_target="tpu_custom_call", output_to_operand_aliasing={{0}: (7, {})} | custom-call | flops 131072 | bytes 131072 | tf_op jit(solution)/shard_map/pallas_call | solution.py:148
  244.7 3.0 %shard_map.84 = (bf16[1024,1536]{1,0:T(8,128)(2,1)}, f32[1,256]{1,0:T(1,128)S(1)}) custom-call(s32[8]{0:T(128)S(1)} %get-tuple-element.88.here, s32[8]{0:T(128)S(1)} %get-tuple-element.80.at, bf16[1024,1024]{1,0:T(8,128)(2,1)S(1)} %constant_dynamic-slice_fusion.sigma, ...), custom_call_target="tpu_custom_call", output_to_operand_aliasing={{0}: (7, {})} | custom-call | flops 131072 | bytes 131072 | tf_op jit(solution)/shard_map/pallas_call | solution.py:148
  248.0 3.3 %collective-permute-done.19 = f32[1,1536]{1,0:T(1,128)S(1)} collective-permute-done((f32[1,1536]{1,0:T(1,128)S(1)}, f32[1,1536]{1,0:T(1,128)S(1)}, u32[]{:S(2)}, u32[]{:S(2)}) %collective-permute-start.19) | collective-permute-done | bytes 6176 | tf_op jit(solution)/shard_map/ppermute | solution.py:174
  253.0 2.1 collective-permute-done.20
  255.1 2.7 %collective-permute-start.21 = (f32[1,1536]{1,0:T(1,128)S(1)}, f32[1,1536]{1,0:T(1,128)S(1)}, u32[]{:S(2)}, u32[]{:S(2)}) collective-permute-start(f32[1,1536]{1,0:T(1,128)S(1)} %add.150), channel_id=1, source_target_pairs={{0,8},{2,10},{4,12},{6,14},{8,0},{10,2},{12,4},{14,6},{1,9},{3,11}... | collective-permute-start | bytes 18440 | tf_op jit(solution)/shard_map/ppermute | solution.py:174
  (100 shorter events, 38.1 us)
Async XLA Ops:
  0.6 44.9 %collective-permute-start.2 = (bf16[1024,4096]{1,0:T(8,128)(2,1)}, bf16[1024,4096]{1,0:T(8,128)(2,1)}, u32[]{:S(2)}, u32[]{:S(2)}) collective-permute-start(bf16[1024,4096]{1,0:T(8,128)(2,1)} %own.1), channel_id=1, source_target_pairs={{0,1},{1,0},{2,3},{3,2},{4,5},{5,4},{6,7},{7,6},{8,9},{9,8},{10,11... | collective-permute-start | bytes 25165832 | tf_op jit(solution)/shard_map/ppermute | solution.py:211
  3.2 82.2 %copy-start.2 = (bf16[1024,768]{1,0:T(8,128)(2,1)}, bf16[1024,768]{1,0:T(8,128)(2,1)S(1)}, u32[]{:S(2)}) copy-start(bf16[1024,768]{1,0:T(8,128)(2,1)S(1)} %get-tuple-element.64.refs_3_) | copy-start | bytes 4718596
  3.3 82.2 %copy-start.4 = (bf16[1024,768]{1,0:T(8,128)(2,1)}, bf16[1024,768]{1,0:T(8,128)(2,1)S(1)}, u32[]{:S(2)}) copy-start(bf16[1024,768]{1,0:T(8,128)(2,1)S(1)} %get-tuple-element.65.refs_4_) | copy-start | bytes 4718596
  3.3 37.9 %collective-permute-start.3 = (bf16[1024,768]{1,0:T(8,128)(2,1)S(1)}, bf16[1024,768]{1,0:T(8,128)(2,1)}, u32[]{:S(2)}, u32[]{:S(2)}) collective-permute-start(bf16[1024,768]{1,0:T(8,128)(2,1)S(1)} %get-tuple-element.64.refs_3_), channel_id=1, source_target_pairs={{0,4},{4,8},{8,12},{12,14},{14,10},{10,6},{6,2},{2,0},{1,5},{5,9},... | collective-permute-start | bytes 4718600 | tf_op jit(solution)/shard_map/ppermute | solution.py:191
  5.9 37.3 %collective-permute-start.5 = (bf16[1024,768]{1,0:T(8,128)(2,1)S(1)}, bf16[1024,768]{1,0:T(8,128)(2,1)}, u32[]{:S(2)}, u32[]{:S(2)}) collective-permute-start(bf16[1024,768]{1,0:T(8,128)(2,1)S(1)} %get-tuple-element.65.refs_4_), channel_id=1, source_target_pairs={{4,0},{8,4},{12,8},{14,12},{10,14},{6,10},{2,6},{0,2},{5,1},{9,5},... | collective-permute-start | bytes 4718600 | tf_op jit(solution)/shard_map/ppermute | solution.py:192
  5.9 79.5 %collective-permute-start = (bf16[1024,768]{1,0:T(8,128)(2,1)S(1)}, bf16[1024,768]{1,0:T(8,128)(2,1)}, u32[]{:S(2)}, u32[]{:S(2)}) collective-permute-start(bf16[1024,768]{1,0:T(8,128)(2,1)S(1)} %get-tuple-element.65.refs_4_), channel_id=1, source_target_pairs={{0,4},{4,8},{8,12},{12,14},{14,10},{10,6},{6,2},{2,0},{1,5},{5,9},... | collective-permute-start | bytes 4718600 | tf_op jit(solution)/shard_map/ppermute | solution.py:191
  7.9 77.5 %collective-permute-start.1 = (bf16[1024,768]{1,0:T(8,128)(2,1)S(1)}, bf16[1024,768]{1,0:T(8,128)(2,1)}, u32[]{:S(2)}, u32[]{:S(2)}) collective-permute-start(bf16[1024,768]{1,0:T(8,128)(2,1)S(1)} %get-tuple-element.64.refs_3_), channel_id=1, source_target_pairs={{4,0},{8,4},{12,8},{14,12},{10,14},{6,10},{2,6},{0,2},{5,1},{9,5},... | collective-permute-start | bytes 4718600 | tf_op jit(solution)/shard_map/ppermute | solution.py:192
  41.2 79.0 %collective-permute-start.4 = (bf16[1024,768]{1,0:T(8,128)(2,1)}, bf16[1024,768]{1,0:T(8,128)(2,1)}, u32[]{:S(2)}, u32[]{:S(2)}) collective-permute-start(bf16[1024,768]{1,0:T(8,128)(2,1)} %collective-permute-done.3.refs_5_), channel_id=1, source_target_pairs={{0,4},{4,8},{8,12},{12,14},{14,10},{10,6},{6,2},{2,0},{1,5},{5,9},... | collective-permute-start | bytes 4718600 | tf_op jit(solution)/shard_map/ppermute | solution.py:191
  43.2 77.0 %collective-permute-start.6 = (bf16[1024,768]{1,0:T(8,128)(2,1)}, bf16[1024,768]{1,0:T(8,128)(2,1)}, u32[]{:S(2)}, u32[]{:S(2)}) collective-permute-start(bf16[1024,768]{1,0:T(8,128)(2,1)} %collective-permute-done.5.refs_8_), channel_id=1, source_target_pairs={{4,0},{8,4},{12,8},{14,12},{10,14},{6,10},{2,6},{0,2},{5,1},{9,5},... | collective-permute-start | bytes 4718600 | tf_op jit(solution)/shard_map/ppermute | solution.py:192
  85.5 58.9 %collective-permute-start.10 = (bf16[1024,768]{1,0:T(8,128)(2,1)}, bf16[1024,768]{1,0:T(8,128)(2,1)}, u32[]{:S(2)}, u32[]{:S(2)}) collective-permute-start(bf16[1024,768]{1,0:T(8,128)(2,1)} %collective-permute-done.1.refs_7_), channel_id=1, source_target_pairs={{4,0},{8,4},{12,8},{14,12},{10,14},{6,10},{2,6},{0,2},{5,1},{9,5},... | collective-permute-start | bytes 4718600 | tf_op jit(solution)/shard_map/ppermute | solution.py:192
  97.9 46.5 %collective-permute-start.9 = (bf16[1024,768]{1,0:T(8,128)(2,1)}, bf16[1024,768]{1,0:T(8,128)(2,1)}, u32[]{:S(2)}, u32[]{:S(2)}) collective-permute-start(bf16[1024,768]{1,0:T(8,128)(2,1)} %collective-permute-done.refs_6_), channel_id=1, source_target_pairs={{0,4},{4,8},{8,12},{12,14},{14,10},{10,6},{6,2},{2,0},{1,5},{5,9},... | collective-permute-start | bytes 4718600 | tf_op jit(solution)/shard_map/ppermute | solution.py:191
  120.2 55.7 %collective-permute-start.7 = (bf16[1024,768]{1,0:T(8,128)(2,1)}, bf16[1024,768]{1,0:T(8,128)(2,1)S(1)}, u32[]{:S(2)}, u32[]{:S(2)}) collective-permute-start(bf16[1024,768]{1,0:T(8,128)(2,1)} %collective-permute-done.4.refs_2_), channel_id=1, source_target_pairs={{0,4},{4,8},{8,12},{12,14},{14,10},{10,6},{6,2},{2,0},{1,5},{5,9},... | collective-permute-start | bytes 4718600 | tf_op jit(solution)/shard_map/ppermute | solution.py:191
  122.3 55.7 %collective-permute-start.8 = (bf16[1024,768]{1,0:T(8,128)(2,1)}, bf16[1024,768]{1,0:T(8,128)(2,1)S(1)}, u32[]{:S(2)}, u32[]{:S(2)}) collective-permute-start(bf16[1024,768]{1,0:T(8,128)(2,1)} %collective-permute-done.6.refs_5_), channel_id=1, source_target_pairs={{4,0},{8,4},{12,8},{14,12},{10,14},{6,10},{2,6},{0,2},{5,1},{9,5},... | collective-permute-start | bytes 4718600 | tf_op jit(solution)/shard_map/ppermute | solution.py:192
  144.4 67.4 %collective-permute-start.13 = (bf16[1024,768]{1,0:T(8,128)(2,1)}, bf16[1024,768]{1,0:T(8,128)(2,1)}, u32[]{:S(2)}, u32[]{:S(2)}) collective-permute-start(bf16[1024,768]{1,0:T(8,128)(2,1)} %collective-permute-done.10.refs_4_), channel_id=1, source_target_pairs={{4,0},{8,4},{12,8},{14,12},{10,14},{6,10},{2,6},{0,2},{5,1},{9,5},... | collective-permute-start | bytes 4718600 | tf_op jit(solution)/shard_map/ppermute | solution.py:192
  144.4 69.2 %collective-permute-start.14 = (bf16[1024,768]{1,0:T(8,128)(2,1)}, bf16[1024,768]{1,0:T(8,128)(2,1)}, u32[]{:S(2)}, u32[]{:S(2)}) collective-permute-start(bf16[1024,768]{1,0:T(8,128)(2,1)} %collective-permute-done.9.refs_3_), channel_id=1, source_target_pairs={{0,4},{4,8},{8,12},{12,14},{14,10},{10,6},{6,2},{2,0},{1,5},{5,9},... | collective-permute-start | bytes 4718600 | tf_op jit(solution)/shard_map/ppermute | solution.py:191
  179.1 53.1 %collective-permute-start.17 = (bf16[1024,512]{1,0:T(8,128)(2,1)}, bf16[1024,512]{1,0:T(8,128)(2,1)}, u32[]{:S(2)}, u32[]{:S(2)}) collective-permute-start(bf16[1024,512]{1,0:T(8,128)(2,1)} %slice.48), channel_id=1, source_target_pairs={{0,4},{4,8},{8,12},{12,14},{14,10},{10,6},{6,2},{2,0},{1,5},{5,9},... | collective-permute-start | bytes 3145736 | tf_op jit(solution)/shard_map/ppermute | solution.py:191
  181.8 52.4 %collective-permute-start.18 = (bf16[1024,512]{1,0:T(8,128)(2,1)}, bf16[1024,512]{1,0:T(8,128)(2,1)}, u32[]{:S(2)}, u32[]{:S(2)}) collective-permute-start(bf16[1024,512]{1,0:T(8,128)(2,1)} %slice.49), channel_id=1, source_target_pairs={{4,0},{8,4},{12,8},{14,12},{10,14},{6,10},{2,6},{0,2},{5,1},{9,5},... | collective-permute-start | bytes 3145736 | tf_op jit(solution)/shard_map/ppermute | solution.py:192
  199.8 40.7 %collective-permute-start.15 = (bf16[1024,128]{1,0:T(8,128)(2,1)S(1)}, bf16[1024,128]{1,0:T(8,128)(2,1)S(1)}, u32[]{:S(2)}, u32[]{:S(2)}) collective-permute-start(bf16[1024,128]{1,0:T(8,128)(2,1)S(1)} %get-tuple-element.68), channel_id=1, source_target_pairs={{0,4},{4,8},{8,12},{12,14},{14,10},{10,6},{6,2},{2,0},{1,5},{5,9},... | collective-permute-start | bytes 786440 | tf_op jit(solution)/shard_map/ppermute | solution.py:191
  211.8 28.7 %collective-permute-start.16 = (bf16[1024,128]{1,0:T(8,128)(2,1)S(1)}, bf16[1024,128]{1,0:T(8,128)(2,1)S(1)}, u32[]{:S(2)}, u32[]{:S(2)}) collective-permute-start(bf16[1024,128]{1,0:T(8,128)(2,1)S(1)} %get-tuple-element.66), channel_id=1, source_target_pairs={{4,0},{8,4},{12,8},{14,12},{10,14},{6,10},{2,6},{0,2},{5,1},{9,5},... | collective-permute-start | bytes 786440 | tf_op jit(solution)/shard_map/ppermute | solution.py:192
  213.6 29.9 %collective-permute-start.11 = (bf16[1024,128]{1,0:T(8,128)(2,1)S(1)}, bf16[1024,128]{1,0:T(8,128)(2,1)S(1)}, u32[]{:S(2)}, u32[]{:S(2)}) collective-permute-start(bf16[1024,128]{1,0:T(8,128)(2,1)S(1)} %get-tuple-element.69), channel_id=1, source_target_pairs={{0,4},{4,8},{8,12},{12,14},{14,10},{10,6},{6,2},{2,0},{1,5},{5,9},... | collective-permute-start | bytes 786440 | tf_op jit(solution)/shard_map/ppermute | solution.py:191
  232.2 12.5 %collective-permute-start.12 = (bf16[1024,128]{1,0:T(8,128)(2,1)S(1)}, bf16[1024,128]{1,0:T(8,128)(2,1)S(1)}, u32[]{:S(2)}, u32[]{:S(2)}) collective-permute-start(bf16[1024,128]{1,0:T(8,128)(2,1)S(1)} %get-tuple-element.67), channel_id=1, source_target_pairs={{4,0},{8,4},{12,8},{14,12},{10,14},{6,10},{2,6},{0,2},{5,1},{9,5},... | collective-permute-start | bytes 786440 | tf_op jit(solution)/shard_map/ppermute | solution.py:192
  247.7 3.7 %collective-permute-start.19 = (f32[1,1536]{1,0:T(1,128)S(1)}, f32[1,1536]{1,0:T(1,128)S(1)}, u32[]{:S(2)}, u32[]{:S(2)}) collective-permute-start(f32[1,1536]{1,0:T(1,128)S(1)} %constant_dynamic-update-slice_fusion), channel_id=1, source_target_pairs={{0,2},{2,0},{4,6},{6,4},{8,10},{10,8},{12,14},{14,12},{1,3},{3,1},... | collective-permute-start | bytes 18440 | tf_op jit(solution)/shard_map/ppermute | solution.py:174
  251.4 3.7 %collective-permute-start.20 = (f32[1,1536]{1,0:T(1,128)S(1)}, f32[1,1536]{1,0:T(1,128)S(1)}, u32[]{:S(2)}, u32[]{:S(2)}) collective-permute-start(f32[1,1536]{1,0:T(1,128)S(1)} %add.149), channel_id=1, source_target_pairs={{0,4},{2,6},{4,0},{6,2},{8,12},{10,14},{12,8},{14,10},{1,5},{3,7},... | collective-permute-start | bytes 18440 | tf_op jit(solution)/shard_map/ppermute | solution.py:174
  255.1 4.6 %collective-permute-start.21 = (f32[1,1536]{1,0:T(1,128)S(1)}, f32[1,1536]{1,0:T(1,128)S(1)}, u32[]{:S(2)}, u32[]{:S(2)}) collective-permute-start(f32[1,1536]{1,0:T(1,128)S(1)} %add.150), channel_id=1, source_target_pairs={{0,8},{2,10},{4,12},{6,14},{8,0},{10,2},{12,4},{14,6},{1,9},{3,11}... | collective-permute-start | bytes 18440 | tf_op jit(solution)/shard_map/ppermute | solution.py:174
  (13 other events, 134.6 us)

commit v7 on v6

--- a/solution.py
+++ b/solution.py
@@ -118,14 +118,27 @@
     )(jnp.stack(sources), here, at, *([sigma] * count), *flat, *extra)
 
 
-def finish_kernel(blocks, here, at, sigma, left, right, acc, mine, *refs):
-    out, part = refs[-2:]
+def finish_kernel(blocks, here, at, coeff, left, right, acc, mine, *refs):
+    *_, out, part, both = refs
     j = pl.program_id(0)
+    unit = acc.shape[1]
+
+    if blocks == 1:
+
+        @pl.when(j == 0)
+        def _():
+            thin = jnp.concatenate([left[...], right[...]], axis=1)
+            both[...] = jnp.dot(coeff[...], thin, preferred_element_type=F32)
+
     for side, late in enumerate((left, right)):
 
         @pl.when(j // blocks == side)
         def _():
-            prod = acc[...] + jnp.dot(sigma[...], late[...], preferred_element_type=F32)
+            if blocks == 1:
+                term = both[:, side * unit : (side + 1) * unit]
+            else:
+                term = jnp.dot(coeff[...], late[...], preferred_element_type=F32)
+            prod = acc[...] + term
             out[...] = (-prod).astype(out.dtype)
             total = None
             for t in range(acc.shape[0] // TILE):
@@ -155,6 +168,7 @@
             + [cut, cut]
             + [pl.BlockSpec(memory_space=pl.ANY)] * len(extra),
             out_specs=[cut, pl.BlockSpec((1, unit), lambda j, *_: (0, j))],
+            scratch_shapes=[pltpu.VMEM((rows, 2 * unit) if blocks == 1 else (8, TILE), F32)],
         ),
         out_shape=[
             jax.ShapeDtypeStruct((rows, cols), jnp.bfloat16),

time: 262 us -> 261 us (level)
  transfers between devices with their start and end apart: 22 -> 22, of which waited for: 11 -> 12; matrix products, arithmetic and copies ran while one was open for 6% -> 6% of each run, Pallas kernels for 37% -> 37%
where the time goes in v7:
time: 261 us; the launch traced here: 260 us
  Pallas kernels  97.4 us (37%)
  waiting for transfers between devices  97.2 us (37%)
  starting transfers between devices  25.8 us (10%)
  local copies, waits for them, and re-layouts  23.5 us (9%)
  between operations  10.7 us (4%)
  other arithmetic  5.25 us (2%)
    ppermute x9, waiting for transfers between devices, body(): ahead = lambda x: lax.ppermute(x, 'row', fwd)  53.7 us
    pallas_call x4, Pallas kernels, accumulate(): pl.pallas_call(functools.partial(accumulate_kernel, count, first, blocks)...  46.5 us
    pallas_call x1, Pallas kernels, reorder(): pl.pallas_call(reorder_kernel, grid_spec=pltpu.PrefetchScalarGridSpec(num...  39.9 us
    ppermute x9, waiting for transfers between devices, body(): back = lambda x: lax.ppermute(x, 'row', bwd)  36.2 us
    ppermute x9, starting transfers between devices, body(): ahead = lambda x: lax.ppermute(x, 'row', fwd)  16.2 us
    unnamed x35, local copies, waits for them, and re-layouts  11.2 us
    pallas_call x3, Pallas kernels, finish(): pl.pallas_call(functools.partial(finish_kernel, blocks), grid_spec=pltpu....  11 us
    ppermute x3, waiting for transfers between devices, row_sum(): lax.ppermute(value, 'row', [(i, i ^ step) for i in range(n)])  7.34 us
  transfers between devices with their start and end apart: 22, of which 12 were waited for; matrix products, arithmetic and copies ran while one was open for 6% of the time, Pallas kernels for 37%

profile of v7, /device:TPU:0, one launch (start us, length us, event | category | flops | bytes accessed | tf_op | source)
XLA Modules:
  0.0 259.7 jit_solution(4420534409276131299)
XLA Ops:
  1.2 2.1 fusion.5
  3.3 2.6 %collective-permute-start.3 = (bf16[1024,768]{1,0:T(8,128)(2,1)S(1)}, bf16[1024,768]{1,0:T(8,128)(2,1)}, u32[]{:S(2)}, u32[]{:S(2)}) collective-permute-start(bf16[1024,768]{1,0:T(8,128)(2,1)S(1)} %get-tuple-element.64.refs_3_), channel_id=1, source_target_pairs={{0,4},{4,8},{8,12},{12,14},{14,10},{10,6},{6,2},{2,0},{1,5},{5,9},... | collective-permute-start | bytes 4718600 | tf_op jit(solution)/shard_map/ppermute | solution.py:205
  8.0 33.1 %collective-permute-done.3.refs_5_ = bf16[1024,768]{1,0:T(8,128)(2,1)} collective-permute-done((bf16[1024,768]{1,0:T(8,128)(2,1)S(1)}, bf16[1024,768]{1,0:T(8,128)(2,1)}, u32[]{:S(2)}, u32[]{:S(2)}) %collective-permute-start.3) | collective-permute-done | bytes 1572896 | tf_op jit(solution)/shard_map/ppermute | solution.py:205
  45.5 39.9 %shard_map.77.refs_0_.refs_1_.refs_2_ = bf16[1024,8192]{1,0:T(8,128)(2,1)} custom-call(s32[64]{0:T(128)} %copy-done.12, s32[2,64]{1,0:T(2,128)} %reshape.150.at, bf16[1024,4096]{1,0:T(8,128)(2,1)} %own.1, bf16[1024,4096]{1,0:T(8,128)(2,1)} %collective-permute-done.2.other), custom_call_target="tpu_custom_call" | custom-call | bytes 4194304 | tf_op jit(solution)/shard_map/pallas_call | solution.py:29
  98.2 2.7 %stack.124.source = s32[6]{0:T(128)S(1)} concatenate(s32[1]{0:T(128)} %bitcast.5, s32[1]{0:T(128)} %bitcast.5, s32[1]{0:T(128)} %get-tuple-element.93, s32[1]{0:T(128)} %get-tuple-element.93, s32[1]{0:T(128)} %get-tuple-element.92, s32[1]{0:T(128)} %get-tuple-element.92), dimensions={0} | concatenate | bytes 48 | tf_op jit(solution)/shard_map/stack | solution.py:118
  103.8 16.4 %shard_map.78 = (f32[1024,1536]{1,0:T(8,128)S(1)}, bf16[1024,1536]{1,0:T(8,128)(2,1)S(1)}) custom-call(s32[6]{0:T(128)S(1)} %stack.124.source, s32[6,8]{1,0:T(8,128)S(1)} %stack.129.here, s32[6,8]{1,0:T(8,128)S(1)} %stack.133.at, bf16[1024,8192]{1,0:T(8,128)(2,1)} %shard_map.77.refs_0_.refs_1_.refs_2_, bf16[1024,8192]{1,0:T(8,128)(2,1)} %shard_map.77.refs_0_.refs_1_.refs_2_, ...), custom_call_target="tpu_custom_call" | custom-call | flops 2359296 | bytes 786432 | tf_op jit(solution)/shard_map/pallas_call | solution.py:103
  120.2 2.1 collective-permute-start.7
  122.3 22.1 %collective-permute-done.10.refs_4_ = bf16[1024,768]{1,0:T(8,128)(2,1)} collective-permute-done((bf16[1024,768]{1,0:T(8,128)(2,1)}, bf16[1024,768]{1,0:T(8,128)(2,1)}, u32[]{:S(2)}, u32[]{:S(2)}) %collective-permute-start.10) | collective-permute-done | bytes 1572896 | tf_op jit(solution)/shard_map/ppermute | solution.py:206
  147.9 12.8 %shard_map.79 = (f32[1024,1536]{1,0:T(8,128)S(1)}, bf16[1024,1536]{1,0:T(8,128)(2,1)S(1)}) custom-call(s32[4]{0:T(128)S(1)} %pad_add_fusion.5.source, s32[4,8]{1,0:T(4,128)S(1)} %add_convert_fusion.here, s32[4,8]{1,0:T(4,128)S(1)} %pad_add_fusion.at, ...), custom_call_target="tpu_custom_call", output_to_operand_aliasing={{0}: (9, {}), {1}: (10, {})} | custom-call | flops 1572864 | bytes 786432 | tf_op jit(solution)/shard_map/pallas_call | solution.py:103
  160.7 2.7 %copy-done = f32[1024,1536]{1,0:T(8,128)} copy-done((f32[1024,1536]{1,0:T(8,128)}, f32[1024,1536]{1,0:T(8,128)S(1)}, u32[]{:S(2)}) %copy-start) | copy-done | bytes 6291480
  163.4 12.5 %collective-permute-done.7.refs_1_ = bf16[1024,768]{1,0:T(8,128)(2,1)S(1)} collective-permute-done((bf16[1024,768]{1,0:T(8,128)(2,1)}, bf16[1024,768]{1,0:T(8,128)(2,1)S(1)}, u32[]{:S(2)}, u32[]{:S(2)}) %collective-permute-start.7) | collective-permute-done | bytes 1572896 | tf_op jit(solution)/shard_map/ppermute | solution.py:205
  175.9 2.1 collective-permute-done.8.refs_2_
  185.6 2.8 %copy-done.1 = f32[1024,1536]{1,0:T(8,128)S(1)} copy-done((f32[1024,1536]{1,0:T(8,128)S(1)}, f32[1024,1536]{1,0:T(8,128)}, u32[]{:S(2)}) %copy-start.1) | copy-done | bytes 6291480
  191.2 8.5 %shard_map.80 = (f32[1024,1536]{1,0:T(8,128)S(1)}, bf16[1024,1536]{1,0:T(8,128)(2,1)S(1)}) custom-call(s32[2]{0:T(128)S(1)} %pad_add_fusion.6.source, s32[2,8]{1,0:T(2,128)S(1)} %get-tuple-element.73.here, s32[2,8]{1,0:T(2,128)S(1)} %get-tuple-element.96.at, ...), custom_call_target="tpu_custom_call", output_to_operand_aliasing={{0}: (6, {}), {1}: (7, {})} | custom-call | flops 786432 | bytes 786432 | tf_op jit(solution)/shard_map/pallas_call | solution.py:103
  201.4 10.4 %collective-permute-done.13.refs_1_ = bf16[1024,768]{1,0:T(8,128)(2,1)} collective-permute-done((bf16[1024,768]{1,0:T(8,128)(2,1)}, bf16[1024,768]{1,0:T(8,128)(2,1)}, u32[]{:S(2)}, u32[]{:S(2)}) %collective-permute-start.13) | collective-permute-done | bytes 1572896 | tf_op jit(solution)/shard_map/ppermute | solution.py:206
  213.6 2.1 collective-permute-start.11
  215.6 8.8 %shard_map.81 = (f32[1024,1536]{1,0:T(8,128)S(1)}, bf16[1024,1536]{1,0:T(8,128)(2,1)S(1)}) custom-call(s32[2]{0:T(128)S(1)} %pad_add_fusion.7.source, s32[2,8]{1,0:T(2,128)S(1)} %get-tuple-element.72.here, s32[2,8]{1,0:T(2,128)S(1)} %get-tuple-element.97.at, ...), custom_call_target="tpu_custom_call", output_to_operand_aliasing={{0}: (6, {}), {1}: (7, {})} | custom-call | flops 786432 | bytes 786432 | tf_op jit(solution)/shard_map/pallas_call | solution.py:103
  224.4 7.8 %collective-permute-done.17.left = bf16[1024,512]{1,0:T(8,128)(2,1)} collective-permute-done((bf16[1024,512]{1,0:T(8,128)(2,1)}, bf16[1024,512]{1,0:T(8,128)(2,1)}, u32[]{:S(2)}, u32[]{:S(2)}) %collective-permute-start.17) | collective-permute-done | bytes 1048608 | tf_op jit(solution)/shard_map/ppermute | solution.py:205
  234.2 6.2 %shard_map.82 = (bf16[1024,1536]{1,0:T(8,128)(2,1)}, f32[1,1024]{1,0:T(1,128)S(1)}) custom-call(s32[8]{0:T(128)S(1)} %get-tuple-element.88.here, s32[8]{0:T(128)S(1)} %get-tuple-element.80.at, bf16[1024,1024]{1,0:T(8,128)(2,1)S(1)} %constant_dynamic-slice_fusion.coeff, bf16[1024,512]{1,0:T(8,128)(2,1)} %collective-permute-done.17.left, ...), custom_call_target="tpu_custom_call" | custom-call | flops 524288 | bytes 524288 | tf_op jit(solution)/shard_map/pallas_call | solution.py:161
  240.4 2.4 shard_map.83
  244.7 2.4 shard_map.84
  247.4 3.3 %collective-permute-done.19 = f32[1,1536]{1,0:T(1,128)S(1)} collective-permute-done((f32[1,1536]{1,0:T(1,128)S(1)}, f32[1,1536]{1,0:T(1,128)S(1)}, u32[]{:S(2)}, u32[]{:S(2)}) %collective-permute-start.19) | collective-permute-done | bytes 6176 | tf_op jit(solution)/shard_map/ppermute | solution.py:188
  252.4 2.1 collective-permute-done.20
  254.5 2.7 %collective-permute-start.21 = (f32[1,1536]{1,0:T(1,128)S(1)}, f32[1,1536]{1,0:T(1,128)S(1)}, u32[]{:S(2)}, u32[]{:S(2)}) collective-permute-start(f32[1,1536]{1,0:T(1,128)S(1)} %add.150), channel_id=1, source_target_pairs={{0,8},{2,10},{4,12},{6,14},{8,0},{10,2},{12,4},{14,6},{1,9},{3,11}... | collective-permute-start | bytes 18440 | tf_op jit(solution)/shard_map/ppermute | solution.py:188
  (100 shorter events, 38.7 us)
Async XLA Ops:
  0.6 44.9 %collective-permute-start.2 = (bf16[1024,4096]{1,0:T(8,128)(2,1)}, bf16[1024,4096]{1,0:T(8,128)(2,1)}, u32[]{:S(2)}, u32[]{:S(2)}) collective-permute-start(bf16[1024,4096]{1,0:T(8,128)(2,1)} %own.1), channel_id=1, source_target_pairs={{0,1},{1,0},{2,3},{3,2},{4,5},{5,4},{6,7},{7,6},{8,9},{9,8},{10,11... | collective-permute-start | bytes 25165832 | tf_op jit(solution)/shard_map/ppermute | solution.py:225
  3.2 82.2 %copy-start.2 = (bf16[1024,768]{1,0:T(8,128)(2,1)}, bf16[1024,768]{1,0:T(8,128)(2,1)S(1)}, u32[]{:S(2)}) copy-start(bf16[1024,768]{1,0:T(8,128)(2,1)S(1)} %get-tuple-element.64.refs_3_) | copy-start | bytes 4718596
  3.3 82.2 %copy-start.4 = (bf16[1024,768]{1,0:T(8,128)(2,1)}, bf16[1024,768]{1,0:T(8,128)(2,1)S(1)}, u32[]{:S(2)}) copy-start(bf16[1024,768]{1,0:T(8,128)(2,1)S(1)} %get-tuple-element.65.refs_4_) | copy-start | bytes 4718596
  3.3 37.9 %collective-permute-start.3 = (bf16[1024,768]{1,0:T(8,128)(2,1)S(1)}, bf16[1024,768]{1,0:T(8,128)(2,1)}, u32[]{:S(2)}, u32[]{:S(2)}) collective-permute-start(bf16[1024,768]{1,0:T(8,128)(2,1)S(1)} %get-tuple-element.64.refs_3_), channel_id=1, source_target_pairs={{0,4},{4,8},{8,12},{12,14},{14,10},{10,6},{6,2},{2,0},{1,5},{5,9},... | collective-permute-start | bytes 4718600 | tf_op jit(solution)/shard_map/ppermute | solution.py:205
  5.9 37.3 %collective-permute-start.5 = (bf16[1024,768]{1,0:T(8,128)(2,1)S(1)}, bf16[1024,768]{1,0:T(8,128)(2,1)}, u32[]{:S(2)}, u32[]{:S(2)}) collective-permute-start(bf16[1024,768]{1,0:T(8,128)(2,1)S(1)} %get-tuple-element.65.refs_4_), channel_id=1, source_target_pairs={{4,0},{8,4},{12,8},{14,12},{10,14},{6,10},{2,6},{0,2},{5,1},{9,5},... | collective-permute-start | bytes 4718600 | tf_op jit(solution)/shard_map/ppermute | solution.py:206
  5.9 79.5 %collective-permute-start = (bf16[1024,768]{1,0:T(8,128)(2,1)S(1)}, bf16[1024,768]{1,0:T(8,128)(2,1)}, u32[]{:S(2)}, u32[]{:S(2)}) collective-permute-start(bf16[1024,768]{1,0:T(8,128)(2,1)S(1)} %get-tuple-element.65.refs_4_), channel_id=1, source_target_pairs={{0,4},{4,8},{8,12},{12,14},{14,10},{10,6},{6,2},{2,0},{1,5},{5,9},... | collective-permute-start | bytes 4718600 | tf_op jit(solution)/shard_map/ppermute | solution.py:205
  7.9 77.5 %collective-permute-start.1 = (bf16[1024,768]{1,0:T(8,128)(2,1)S(1)}, bf16[1024,768]{1,0:T(8,128)(2,1)}, u32[]{:S(2)}, u32[]{:S(2)}) collective-permute-start(bf16[1024,768]{1,0:T(8,128)(2,1)S(1)} %get-tuple-element.64.refs_3_), channel_id=1, source_target_pairs={{4,0},{8,4},{12,8},{14,12},{10,14},{6,10},{2,6},{0,2},{5,1},{9,5},... | collective-permute-start | bytes 4718600 | tf_op jit(solution)/shard_map/ppermute | solution.py:206
  41.2 79.0 %collective-permute-start.4 = (bf16[1024,768]{1,0:T(8,128)(2,1)}, bf16[1024,768]{1,0:T(8,128)(2,1)}, u32[]{:S(2)}, u32[]{:S(2)}) collective-permute-start(bf16[1024,768]{1,0:T(8,128)(2,1)} %collective-permute-done.3.refs_5_), channel_id=1, source_target_pairs={{0,4},{4,8},{8,12},{12,14},{14,10},{10,6},{6,2},{2,0},{1,5},{5,9},... | collective-permute-start | bytes 4718600 | tf_op jit(solution)/shard_map/ppermute | solution.py:205
  43.2 77.0 %collective-permute-start.6 = (bf16[1024,768]{1,0:T(8,128)(2,1)}, bf16[1024,768]{1,0:T(8,128)(2,1)}, u32[]{:S(2)}, u32[]{:S(2)}) collective-permute-start(bf16[1024,768]{1,0:T(8,128)(2,1)} %collective-permute-done.5.refs_8_), channel_id=1, source_target_pairs={{4,0},{8,4},{12,8},{14,12},{10,14},{6,10},{2,6},{0,2},{5,1},{9,5},... | collective-permute-start | bytes 4718600 | tf_op jit(solution)/shard_map/ppermute | solution.py:206
  85.5 58.9 %collective-permute-start.10 = (bf16[1024,768]{1,0:T(8,128)(2,1)}, bf16[1024,768]{1,0:T(8,128)(2,1)}, u32[]{:S(2)}, u32[]{:S(2)}) collective-permute-start(bf16[1024,768]{1,0:T(8,128)(2,1)} %collective-permute-done.1.refs_7_), channel_id=1, source_target_pairs={{4,0},{8,4},{12,8},{14,12},{10,14},{6,10},{2,6},{0,2},{5,1},{9,5},... | collective-permute-start | bytes 4718600 | tf_op jit(solution)/shard_map/ppermute | solution.py:206
  97.9 46.5 %collective-permute-start.9 = (bf16[1024,768]{1,0:T(8,128)(2,1)}, bf16[1024,768]{1,0:T(8,128)(2,1)}, u32[]{:S(2)}, u32[]{:S(2)}) collective-permute-start(bf16[1024,768]{1,0:T(8,128)(2,1)} %collective-permute-done.refs_6_), channel_id=1, source_target_pairs={{0,4},{4,8},{8,12},{12,14},{14,10},{10,6},{6,2},{2,0},{1,5},{5,9},... | collective-permute-start | bytes 4718600 | tf_op jit(solution)/shard_map/ppermute | solution.py:205
  120.2 55.7 %collective-permute-start.7 = (bf16[1024,768]{1,0:T(8,128)(2,1)}, bf16[1024,768]{1,0:T(8,128)(2,1)S(1)}, u32[]{:S(2)}, u32[]{:S(2)}) collective-permute-start(bf16[1024,768]{1,0:T(8,128)(2,1)} %collective-permute-done.4.refs_2_), channel_id=1, source_target_pairs={{0,4},{4,8},{8,12},{12,14},{14,10},{10,6},{6,2},{2,0},{1,5},{5,9},... | collective-permute-start | bytes 4718600 | tf_op jit(solution)/shard_map/ppermute | solution.py:205
  122.3 55.7 %collective-permute-start.8 = (bf16[1024,768]{1,0:T(8,128)(2,1)}, bf16[1024,768]{1,0:T(8,128)(2,1)S(1)}, u32[]{:S(2)}, u32[]{:S(2)}) collective-permute-start(bf16[1024,768]{1,0:T(8,128)(2,1)} %collective-permute-done.6.refs_5_), channel_id=1, source_target_pairs={{4,0},{8,4},{12,8},{14,12},{10,14},{6,10},{2,6},{0,2},{5,1},{9,5},... | collective-permute-start | bytes 4718600 | tf_op jit(solution)/shard_map/ppermute | solution.py:206
  144.4 67.4 %collective-permute-start.13 = (bf16[1024,768]{1,0:T(8,128)(2,1)}, bf16[1024,768]{1,0:T(8,128)(2,1)}, u32[]{:S(2)}, u32[]{:S(2)}) collective-permute-start(bf16[1024,768]{1,0:T(8,128)(2,1)} %collective-permute-done.10.refs_4_), channel_id=1, source_target_pairs={{4,0},{8,4},{12,8},{14,12},{10,14},{6,10},{2,6},{0,2},{5,1},{9,5},... | collective-permute-start | bytes 4718600 | tf_op jit(solution)/shard_map/ppermute | solution.py:206
  144.4 69.2 %collective-permute-start.14 = (bf16[1024,768]{1,0:T(8,128)(2,1)}, bf16[1024,768]{1,0:T(8,128)(2,1)}, u32[]{:S(2)}, u32[]{:S(2)}) collective-permute-start(bf16[1024,768]{1,0:T(8,128)(2,1)} %collective-permute-done.9.refs_3_), channel_id=1, source_target_pairs={{0,4},{4,8},{8,12},{12,14},{14,10},{10,6},{6,2},{2,0},{1,5},{5,9},... | collective-permute-start | bytes 4718600 | tf_op jit(solution)/shard_map/ppermute | solution.py:205
  179.1 53.1 %collective-permute-start.17 = (bf16[1024,512]{1,0:T(8,128)(2,1)}, bf16[1024,512]{1,0:T(8,128)(2,1)}, u32[]{:S(2)}, u32[]{:S(2)}) collective-permute-start(bf16[1024,512]{1,0:T(8,128)(2,1)} %slice.48), channel_id=1, source_target_pairs={{0,4},{4,8},{8,12},{12,14},{14,10},{10,6},{6,2},{2,0},{1,5},{5,9},... | collective-permute-start | bytes 3145736 | tf_op jit(solution)/shard_map/ppermute | solution.py:205
  181.8 52.4 %collective-permute-start.18 = (bf16[1024,512]{1,0:T(8,128)(2,1)}, bf16[1024,512]{1,0:T(8,128)(2,1)}, u32[]{:S(2)}, u32[]{:S(2)}) collective-permute-start(bf16[1024,512]{1,0:T(8,128)(2,1)} %slice.49), channel_id=1, source_target_pairs={{4,0},{8,4},{12,8},{14,12},{10,14},{6,10},{2,6},{0,2},{5,1},{9,5},... | collective-permute-start | bytes 3145736 | tf_op jit(solution)/shard_map/ppermute | solution.py:206
  199.8 40.7 %collective-permute-start.15 = (bf16[1024,128]{1,0:T(8,128)(2,1)S(1)}, bf16[1024,128]{1,0:T(8,128)(2,1)S(1)}, u32[]{:S(2)}, u32[]{:S(2)}) collective-permute-start(bf16[1024,128]{1,0:T(8,128)(2,1)S(1)} %get-tuple-element.68), channel_id=1, source_target_pairs={{0,4},{4,8},{8,12},{12,14},{14,10},{10,6},{6,2},{2,0},{1,5},{5,9},... | collective-permute-start | bytes 786440 | tf_op jit(solution)/shard_map/ppermute | solution.py:205
  211.8 28.7 %collective-permute-start.16 = (bf16[1024,128]{1,0:T(8,128)(2,1)S(1)}, bf16[1024,128]{1,0:T(8,128)(2,1)S(1)}, u32[]{:S(2)}, u32[]{:S(2)}) collective-permute-start(bf16[1024,128]{1,0:T(8,128)(2,1)S(1)} %get-tuple-element.66), channel_id=1, source_target_pairs={{4,0},{8,4},{12,8},{14,12},{10,14},{6,10},{2,6},{0,2},{5,1},{9,5},... | collective-permute-start | bytes 786440 | tf_op jit(solution)/shard_map/ppermute | solution.py:206
  213.6 29.6 %collective-permute-start.11 = (bf16[1024,128]{1,0:T(8,128)(2,1)S(1)}, bf16[1024,128]{1,0:T(8,128)(2,1)S(1)}, u32[]{:S(2)}, u32[]{:S(2)}) collective-permute-start(bf16[1024,128]{1,0:T(8,128)(2,1)S(1)} %get-tuple-element.69), channel_id=1, source_target_pairs={{0,4},{4,8},{8,12},{12,14},{14,10},{10,6},{6,2},{2,0},{1,5},{5,9},... | collective-permute-start | bytes 786440 | tf_op jit(solution)/shard_map/ppermute | solution.py:205
  232.2 12.5 %collective-permute-start.12 = (bf16[1024,128]{1,0:T(8,128)(2,1)S(1)}, bf16[1024,128]{1,0:T(8,128)(2,1)S(1)}, u32[]{:S(2)}, u32[]{:S(2)}) collective-permute-start(bf16[1024,128]{1,0:T(8,128)(2,1)S(1)} %get-tuple-element.67), channel_id=1, source_target_pairs={{4,0},{8,4},{12,8},{14,12},{10,14},{6,10},{2,6},{0,2},{5,1},{9,5},... | collective-permute-start | bytes 786440 | tf_op jit(solution)/shard_map/ppermute | solution.py:206
  247.1 3.7 %collective-permute-start.19 = (f32[1,1536]{1,0:T(1,128)S(1)}, f32[1,1536]{1,0:T(1,128)S(1)}, u32[]{:S(2)}, u32[]{:S(2)}) collective-permute-start(f32[1,1536]{1,0:T(1,128)S(1)} %constant_dynamic-update-slice_fusion), channel_id=1, source_target_pairs={{0,2},{2,0},{4,6},{6,4},{8,10},{10,8},{12,14},{14,12},{1,3},{3,1},... | collective-permute-start | bytes 18440 | tf_op jit(solution)/shard_map/ppermute | solution.py:188
  250.8 3.7 %collective-permute-start.20 = (f32[1,1536]{1,0:T(1,128)S(1)}, f32[1,1536]{1,0:T(1,128)S(1)}, u32[]{:S(2)}, u32[]{:S(2)}) collective-permute-start(f32[1,1536]{1,0:T(1,128)S(1)} %add.149), channel_id=1, source_target_pairs={{0,4},{2,6},{4,0},{6,2},{8,12},{10,14},{12,8},{14,10},{1,5},{3,7},... | collective-permute-start | bytes 18440 | tf_op jit(solution)/shard_map/ppermute | solution.py:188
  254.5 4.6 %collective-permute-start.21 = (f32[1,1536]{1,0:T(1,128)S(1)}, f32[1,1536]{1,0:T(1,128)S(1)}, u32[]{:S(2)}, u32[]{:S(2)}) collective-permute-start(f32[1,1536]{1,0:T(1,128)S(1)} %add.150), channel_id=1, source_target_pairs={{0,8},{2,10},{4,12},{6,14},{8,0},{10,2},{12,4},{14,6},{1,9},{3,11}... | collective-permute-start | bytes 18440 | tf_op jit(solution)/shard_map/ppermute | solution.py:188
  (13 other events, 134.0 us)
